TPU v7x, 512 devices: a whole 4x8x8 slice. The times are simulated.
512 devices in a mesh: layer: 8 (over z), dom: 64 (over x, y, core).
Axes of the slice: x: 4, y: 8, z: 8, core: 2. Of those that a mesh axis runs over, the one named last changes fastest.
Arguments:
- features: bfloat16 [2, 16384, 256], P(None, 'dom'), may hold values from -6 to 6
- weight: bfloat16 [8, 256, 256], P('layer'), may hold values from -0.375 to 0.375
- bias: float32 [8, 256], P('layer'), may hold values from -3 to 3
- gain: float32 [8, 256], P('layer'), may hold values from 0.5 to 1.5
- tile_col: int32 [2, 128, 4], P(None, 'dom'), may hold values from 0 to 1
- tile_adj: int32 [2, 128, 4, 128, 128], P(None, 'dom'), may hold values 0 or 1
- send_rows: int32 [2, 64, 64, 8], P(None, 'dom'), may hold values from 0 to 255
- recv_dst: int32 [2, 64, 64, 8], P(None, 'dom'), may hold values from -1 to 255, as said below
Outputs:
- layer_states: bfloat16 [8, 2, 16384, 256], P('layer', None, 'dom')
Inputs may be any that keep to these rules, and one draw needn't show every extreme that they name: `recv_dst`: no partition has slots from itself (all -1). From every other sender either no slot or all 8 slots are live; every receiver has at least one sender whose 8 slots are all live.
All inputs are finite; a program needn't handle non-finite values. No bound on the sum of `tile_adj` on one device may be relied on, other than what follows from the above.
Results may differ from a plain program's by a relative error of at most 0.02.
Values may be sent and summed in bfloat16 or wider, within the bound.
No kernel may reach another device: no remote copies, remote signals or barrier semaphores. Data moves between devices by JAX's collectives and lax.ppermute only.
A program may use at most 64 MiB of HBM per device.

v0:
```python
import jax
import jax.numpy as jnp
from jax import lax
from jax.sharding import PartitionSpec as P


def from_behind(array, axis, by):
    count = lax.axis_size(axis)
    pairs = [(i, i + by) for i in range(count) if 0 <= i + by < count]
    return lax.ppermute(array, axis, pairs)


def boundary_rows(hidden, gather_sel):
    outgoing = jnp.einsum(
        "cpsi,cid->pcsd", gather_sel, hidden, preferred_element_type=jnp.float32
    ).astype(jnp.bfloat16)
    return lax.all_to_all(outgoing, "dom", split_axis=0, concat_axis=0, tiled=True)


def finish_layer(own_rows, local_sum, boundary_sum, degree, layer_weight, layer_bias, layer_gain):
    feature_width = own_rows.shape[-1]
    base = own_rows.astype(jnp.float32)
    neighbour_mean = ((base + local_sum + boundary_sum) / degree[..., None]).astype(jnp.bfloat16)
    projected = (
        jnp.dot(
            neighbour_mean.reshape(-1, feature_width),
            layer_weight,
            preferred_element_type=jnp.float32,
        ).reshape(base.shape)
        + layer_bias
    )
    summed = base + jnp.maximum(projected, 0.0)
    scaled = summed * lax.rsqrt(jnp.mean(summed * summed, axis=-1, keepdims=True) + 1e-05)
    return (scaled * layer_gain).astype(jnp.bfloat16)


def apply_layer(
    hidden,
    own_rows,
    dense_adj,
    degree,
    gather_sel,
    scatter_sel,
    layer_weight,
    layer_bias,
    layer_gain,
):
    local_sum = jnp.einsum("cij,cjd->cid", dense_adj, hidden, preferred_element_type=jnp.float32)
    arrived = boundary_rows(hidden, gather_sel)
    boundary_sum = jnp.einsum(
        "ciqs,qcsd->cid", scatter_sel, arrived, preferred_element_type=jnp.float32
    )
    return finish_layer(
        own_rows, local_sum, boundary_sum, degree, layer_weight, layer_bias, layer_gain
    )


def pass_down(section_output):
    return from_behind(section_output, "layer", 1)


def local(features, weight, bias, gain, tile_col, tile_adj, send_rows, recv_dst):
    section_index = lax.axis_index("layer")
    chain_length = lax.axis_size("layer")
    span_total = features.shape[0]
    row_count = features.shape[1]
    row_blocks = tile_col.shape[1]
    column_hit = (tile_col[..., None] == jnp.arange(row_blocks)[None, None, None, :]).astype(
        jnp.float32
    )
    dense_f32 = jnp.einsum("crkb,crkij->cribj", column_hit, tile_adj.astype(jnp.float32)).reshape(
        span_total, row_count, row_count
    )
    local_degree = jnp.sum(dense_f32, axis=2)
    dense_adj = dense_f32.astype(jnp.bfloat16)
    send_list = send_rows[:, 0]
    dest_rows = recv_dst[:, 0]
    row_ids = jnp.arange(row_count)
    gather_sel = (send_list[..., None] == row_ids[None, None, None, :]).astype(jnp.bfloat16)
    scatter_hit = (dest_rows[:, None, :, :] == row_ids[None, :, None, None]).astype(jnp.float32)
    degree_all = 1.0 + local_degree + jnp.sum(scatter_hit, axis=(2, 3))
    scatter_sel = scatter_hit.astype(jnp.bfloat16)
    layer_weight = weight[0]
    layer_bias = bias[0]
    layer_gain = gain[0]
    empty_states = jnp.zeros_like(features)

    def whole_step(step_now, state_pair):
        incoming, stored_states = state_pair
        section_input = jnp.where(section_index == 0, features, incoming)
        section_output = apply_layer(
            section_input,
            section_input,
            dense_adj,
            degree_all,
            gather_sel,
            scatter_sel,
            layer_weight,
            layer_bias,
            layer_gain,
        )
        stored_states = jnp.where(step_now == section_index, section_output, stored_states)
        return (pass_down(section_output), stored_states)

    finished = lax.fori_loop(0, chain_length, whole_step, (jnp.zeros_like(features), empty_states))
    return finished[1][None]


def solution(mesh):
    in_specs = (
        P(None, "dom", None),
        P("layer", None, None),
        P("layer", None),
        P("layer", None),
        P(None, "dom", None),
        P(None, "dom", None, None, None),
        P(None, "dom", None, None),
        P(None, "dom", None, None),
    )
    out_specs = P("layer", None, "dom", None)
    return jax.shard_map(local, mesh=mesh, in_specs=in_specs, out_specs=out_specs, check_vma=False)
```

profile of v0, /device:TPU:1, one launch (start us, length us, event | category | flops | bytes accessed | tf_op | source)
XLA Modules:
  0.0 305.4 jit_solution(400597779670945757)
XLA Ops:
  0.0 1.3 convert_element_type.54
  1.4 1.6 fusion.24
  3.6 0.8 copy-done
  4.5 0.8 copy-done.1
  5.3 0.6 copy-done.4
  6.1 0.6 copy-done.2
  6.7 297.8 %while.17 = (s32[]{:T(128)}, bf16[2,256,256]{1,2,0:T(8,128)(2,1)S(1)}, bf16[2,256,256]{1,2,0:T(8,128)(2,1)S(1)}, pred[]{:T(512)}, bf16[2,256,256]{1,2,0:T(8,128)...) while((s32[]{:T(128)}, ...), condition=%wide.region_4.5_spmd.clone, body=%wide.region_2.4_spmd.clone.sunk | while | flops 406848000 | bytes 8016107 | solution.py:105
  6.7 1.1 fusion.38
  7.9 11.6 %all-to-all-start = ((bf16[64,2,8,256]{3,2,1,0:T(8,128)(2,1)}), bf16[64,2,8,256]{3,2,1,0:T(8,128)(2,1)S(1)}, u32[]{:S(2)}, u32[]{:S(2)}) async-start(bf16[64,2,8,256]{3,2,1,0:T(8,128)(2,1)} %fusion.38), calls=%async_computation | async-start | bytes 1048576 | tf_op jit(solution)/shard_map/while/body/eval_jaxpr/all_to_all | solution.py:17
  19.5 17.3 %all-to-all-done = bf16[64,2,8,256]{3,2,1,0:T(8,128)(2,1)S(1)} async-done(((bf16[64,2,8,256]{3,2,1,0:T(8,128)(2,1)}), bf16[64,2,8,256]{3,2,1,0:T(8,128)(2,1)S(1)}, u32[]{:S(2)}, u32[]{:S(2)}) %all-to-all-start) | async-done | bytes 524320 | tf_op jit(solution)/shard_map/while/body/eval_jaxpr/all_to_all | solution.py:17
  36.8 0.5 convolution_bitcast_fusion.4
  37.3 0.5 multiply_reduce_fusion.2
  38.0 4.0 %collective-permute-start = (bf16[2,256,256]{1,2,0:T(8,128)(2,1)S(1)}, bf16[2,256,256]{1,2,0:T(8,128)(2,1)S(1)}, u32[]{:S(2)}, u32[]{:S(2)}) collective-permute-start(bf16[2,256,256]{1,2,0:T(8,128)(2,1)S(1)} %get-tuple-element.463), channel_id=1, source_target_pairs={{0,64},{64,128},{128,192},{192,256},{256,320},{320,384},{384,448},... | collective-permute-start | bytes 786440 | tf_op jit(solution)/shard_map/while/body/eval_jaxpr/ppermute | solution.py:10
  42.0 5.3 %collective-permute-done = bf16[2,256,256]{1,2,0:T(8,128)(2,1)S(1)} collective-permute-done((bf16[2,256,256]{1,2,0:T(8,128)(2,1)S(1)}, bf16[2,256,256]{1,2,0:T(8,128)(2,1)S(1)}, u32[]{:S(2)}, u32[]{:S(2)}) %collective-permute-start) | collective-permute-done | bytes 262176 | tf_op jit(solution)/shard_map/while/body/eval_jaxpr/ppermute | solution.py:10
  47.4 1.1 fusion.38
  48.5 6.8 %all-to-all-start = ((bf16[64,2,8,256]{3,2,1,0:T(8,128)(2,1)}), bf16[64,2,8,256]{3,2,1,0:T(8,128)(2,1)S(1)}, u32[]{:S(2)}, u32[]{:S(2)}) async-start(bf16[64,2,8,256]{3,2,1,0:T(8,128)(2,1)} %fusion.38), calls=%async_computation | async-start | bytes 1048576 | tf_op jit(solution)/shard_map/while/body/eval_jaxpr/all_to_all | solution.py:17
  55.3 17.3 %all-to-all-done = bf16[64,2,8,256]{3,2,1,0:T(8,128)(2,1)S(1)} async-done(((bf16[64,2,8,256]{3,2,1,0:T(8,128)(2,1)}), bf16[64,2,8,256]{3,2,1,0:T(8,128)(2,1)S(1)}, u32[]{:S(2)}, u32[]{:S(2)}) %all-to-all-start) | async-done | bytes 524320 | tf_op jit(solution)/shard_map/while/body/eval_jaxpr/all_to_all | solution.py:17
  72.6 0.5 convolution_bitcast_fusion.4
  73.2 0.5 multiply_reduce_fusion.2
  73.8 4.1 %collective-permute-start = (bf16[2,256,256]{1,2,0:T(8,128)(2,1)S(1)}, bf16[2,256,256]{1,2,0:T(8,128)(2,1)S(1)}, u32[]{:S(2)}, u32[]{:S(2)}) collective-permute-start(bf16[2,256,256]{1,2,0:T(8,128)(2,1)S(1)} %get-tuple-element.463), channel_id=1, source_target_pairs={{0,64},{64,128},{128,192},{192,256},{256,320},{320,384},{384,448},... | collective-permute-start | bytes 786440 | tf_op jit(solution)/shard_map/while/body/eval_jaxpr/ppermute | solution.py:10
  78.0 5.3 %collective-permute-done = bf16[2,256,256]{1,2,0:T(8,128)(2,1)S(1)} collective-permute-done((bf16[2,256,256]{1,2,0:T(8,128)(2,1)S(1)}, bf16[2,256,256]{1,2,0:T(8,128)(2,1)S(1)}, u32[]{:S(2)}, u32[]{:S(2)}) %collective-permute-start) | collective-permute-done | bytes 262176 | tf_op jit(solution)/shard_map/while/body/eval_jaxpr/ppermute | solution.py:10
  83.3 1.1 fusion.38
  84.4 6.8 %all-to-all-start = ((bf16[64,2,8,256]{3,2,1,0:T(8,128)(2,1)}), bf16[64,2,8,256]{3,2,1,0:T(8,128)(2,1)S(1)}, u32[]{:S(2)}, u32[]{:S(2)}) async-start(bf16[64,2,8,256]{3,2,1,0:T(8,128)(2,1)} %fusion.38), calls=%async_computation | async-start | bytes 1048576 | tf_op jit(solution)/shard_map/while/body/eval_jaxpr/all_to_all | solution.py:17
  91.2 17.3 %all-to-all-done = bf16[64,2,8,256]{3,2,1,0:T(8,128)(2,1)S(1)} async-done(((bf16[64,2,8,256]{3,2,1,0:T(8,128)(2,1)}), bf16[64,2,8,256]{3,2,1,0:T(8,128)(2,1)S(1)}, u32[]{:S(2)}, u32[]{:S(2)}) %all-to-all-start) | async-done | bytes 524320 | tf_op jit(solution)/shard_map/while/body/eval_jaxpr/all_to_all | solution.py:17
  108.5 0.5 convolution_bitcast_fusion.4
  109.1 0.5 multiply_reduce_fusion.2
  109.8 4.1 %collective-permute-start = (bf16[2,256,256]{1,2,0:T(8,128)(2,1)S(1)}, bf16[2,256,256]{1,2,0:T(8,128)(2,1)S(1)}, u32[]{:S(2)}, u32[]{:S(2)}) collective-permute-start(bf16[2,256,256]{1,2,0:T(8,128)(2,1)S(1)} %get-tuple-element.463), channel_id=1, source_target_pairs={{0,64},{64,128},{128,192},{192,256},{256,320},{320,384},{384,448},... | collective-permute-start | bytes 786440 | tf_op jit(solution)/shard_map/while/body/eval_jaxpr/ppermute | solution.py:10
  113.9 5.3 %collective-permute-done = bf16[2,256,256]{1,2,0:T(8,128)(2,1)S(1)} collective-permute-done((bf16[2,256,256]{1,2,0:T(8,128)(2,1)S(1)}, bf16[2,256,256]{1,2,0:T(8,128)(2,1)S(1)}, u32[]{:S(2)}, u32[]{:S(2)}) %collective-permute-start) | collective-permute-done | bytes 262176 | tf_op jit(solution)/shard_map/while/body/eval_jaxpr/ppermute | solution.py:10
  119.2 1.1 fusion.38
  120.4 6.8 %all-to-all-start = ((bf16[64,2,8,256]{3,2,1,0:T(8,128)(2,1)}), bf16[64,2,8,256]{3,2,1,0:T(8,128)(2,1)S(1)}, u32[]{:S(2)}, u32[]{:S(2)}) async-start(bf16[64,2,8,256]{3,2,1,0:T(8,128)(2,1)} %fusion.38), calls=%async_computation | async-start | bytes 1048576 | tf_op jit(solution)/shard_map/while/body/eval_jaxpr/all_to_all | solution.py:17
  127.1 17.3 %all-to-all-done = bf16[64,2,8,256]{3,2,1,0:T(8,128)(2,1)S(1)} async-done(((bf16[64,2,8,256]{3,2,1,0:T(8,128)(2,1)}), bf16[64,2,8,256]{3,2,1,0:T(8,128)(2,1)S(1)}, u32[]{:S(2)}, u32[]{:S(2)}) %all-to-all-start) | async-done | bytes 524320 | tf_op jit(solution)/shard_map/while/body/eval_jaxpr/all_to_all | solution.py:17
  144.5 0.5 convolution_bitcast_fusion.4
  145.0 0.5 multiply_reduce_fusion.2
  145.7 5.0 %collective-permute-start = (bf16[2,256,256]{1,2,0:T(8,128)(2,1)S(1)}, bf16[2,256,256]{1,2,0:T(8,128)(2,1)S(1)}, u32[]{:S(2)}, u32[]{:S(2)}) collective-permute-start(bf16[2,256,256]{1,2,0:T(8,128)(2,1)S(1)} %get-tuple-element.463), channel_id=1, source_target_pairs={{0,64},{64,128},{128,192},{192,256},{256,320},{320,384},{384,448},... | collective-permute-start | bytes 786440 | tf_op jit(solution)/shard_map/while/body/eval_jaxpr/ppermute | solution.py:10
  150.7 5.3 %collective-permute-done = bf16[2,256,256]{1,2,0:T(8,128)(2,1)S(1)} collective-permute-done((bf16[2,256,256]{1,2,0:T(8,128)(2,1)S(1)}, bf16[2,256,256]{1,2,0:T(8,128)(2,1)S(1)}, u32[]{:S(2)}, u32[]{:S(2)}) %collective-permute-start) | collective-permute-done | bytes 262176 | tf_op jit(solution)/shard_map/while/body/eval_jaxpr/ppermute | solution.py:10
  156.0 1.1 fusion.38
  157.1 6.8 %all-to-all-start = ((bf16[64,2,8,256]{3,2,1,0:T(8,128)(2,1)}), bf16[64,2,8,256]{3,2,1,0:T(8,128)(2,1)S(1)}, u32[]{:S(2)}, u32[]{:S(2)}) async-start(bf16[64,2,8,256]{3,2,1,0:T(8,128)(2,1)} %fusion.38), calls=%async_computation | async-start | bytes 1048576 | tf_op jit(solution)/shard_map/while/body/eval_jaxpr/all_to_all | solution.py:17
  163.9 17.3 %all-to-all-done = bf16[64,2,8,256]{3,2,1,0:T(8,128)(2,1)S(1)} async-done(((bf16[64,2,8,256]{3,2,1,0:T(8,128)(2,1)}), bf16[64,2,8,256]{3,2,1,0:T(8,128)(2,1)S(1)}, u32[]{:S(2)}, u32[]{:S(2)}) %all-to-all-start) | async-done | bytes 524320 | tf_op jit(solution)/shard_map/while/body/eval_jaxpr/all_to_all | solution.py:17
  181.3 0.5 convolution_bitcast_fusion.4
  181.8 0.5 multiply_reduce_fusion.2
  182.5 5.3 %collective-permute-start = (bf16[2,256,256]{1,2,0:T(8,128)(2,1)S(1)}, bf16[2,256,256]{1,2,0:T(8,128)(2,1)S(1)}, u32[]{:S(2)}, u32[]{:S(2)}) collective-permute-start(bf16[2,256,256]{1,2,0:T(8,128)(2,1)S(1)} %get-tuple-element.463), channel_id=1, source_target_pairs={{0,64},{64,128},{128,192},{192,256},{256,320},{320,384},{384,448},... | collective-permute-start | bytes 786440 | tf_op jit(solution)/shard_map/while/body/eval_jaxpr/ppermute | solution.py:10
  187.8 5.3 %collective-permute-done = bf16[2,256,256]{1,2,0:T(8,128)(2,1)S(1)} collective-permute-done((bf16[2,256,256]{1,2,0:T(8,128)(2,1)S(1)}, bf16[2,256,256]{1,2,0:T(8,128)(2,1)S(1)}, u32[]{:S(2)}, u32[]{:S(2)}) %collective-permute-start) | collective-permute-done | bytes 262176 | tf_op jit(solution)/shard_map/while/body/eval_jaxpr/ppermute | solution.py:10
  193.1 1.1 fusion.38
  194.3 6.8 %all-to-all-start = ((bf16[64,2,8,256]{3,2,1,0:T(8,128)(2,1)}), bf16[64,2,8,256]{3,2,1,0:T(8,128)(2,1)S(1)}, u32[]{:S(2)}, u32[]{:S(2)}) async-start(bf16[64,2,8,256]{3,2,1,0:T(8,128)(2,1)} %fusion.38), calls=%async_computation | async-start | bytes 1048576 | tf_op jit(solution)/shard_map/while/body/eval_jaxpr/all_to_all | solution.py:17
  201.1 17.3 %all-to-all-done = bf16[64,2,8,256]{3,2,1,0:T(8,128)(2,1)S(1)} async-done(((bf16[64,2,8,256]{3,2,1,0:T(8,128)(2,1)}), bf16[64,2,8,256]{3,2,1,0:T(8,128)(2,1)S(1)}, u32[]{:S(2)}, u32[]{:S(2)}) %all-to-all-start) | async-done | bytes 524320 | tf_op jit(solution)/shard_map/while/body/eval_jaxpr/all_to_all | solution.py:17
  218.4 0.5 convolution_bitcast_fusion.4
  218.9 0.5 multiply_reduce_fusion.2
  219.6 5.3 %collective-permute-start = (bf16[2,256,256]{1,2,0:T(8,128)(2,1)S(1)}, bf16[2,256,256]{1,2,0:T(8,128)(2,1)S(1)}, u32[]{:S(2)}, u32[]{:S(2)}) collective-permute-start(bf16[2,256,256]{1,2,0:T(8,128)(2,1)S(1)} %get-tuple-element.463), channel_id=1, source_target_pairs={{0,64},{64,128},{128,192},{192,256},{256,320},{320,384},{384,448},... | collective-permute-start | bytes 786440 | tf_op jit(solution)/shard_map/while/body/eval_jaxpr/ppermute | solution.py:10
  224.9 5.3 %collective-permute-done = bf16[2,256,256]{1,2,0:T(8,128)(2,1)S(1)} collective-permute-done((bf16[2,256,256]{1,2,0:T(8,128)(2,1)S(1)}, bf16[2,256,256]{1,2,0:T(8,128)(2,1)S(1)}, u32[]{:S(2)}, u32[]{:S(2)}) %collective-permute-start) | collective-permute-done | bytes 262176 | tf_op jit(solution)/shard_map/while/body/eval_jaxpr/ppermute | solution.py:10
  230.3 1.1 fusion.38
  231.4 6.8 %all-to-all-start = ((bf16[64,2,8,256]{3,2,1,0:T(8,128)(2,1)}), bf16[64,2,8,256]{3,2,1,0:T(8,128)(2,1)S(1)}, u32[]{:S(2)}, u32[]{:S(2)}) async-start(bf16[64,2,8,256]{3,2,1,0:T(8,128)(2,1)} %fusion.38), calls=%async_computation | async-start | bytes 1048576 | tf_op jit(solution)/shard_map/while/body/eval_jaxpr/all_to_all | solution.py:17
  238.2 17.3 %all-to-all-done = bf16[64,2,8,256]{3,2,1,0:T(8,128)(2,1)S(1)} async-done(((bf16[64,2,8,256]{3,2,1,0:T(8,128)(2,1)}), bf16[64,2,8,256]{3,2,1,0:T(8,128)(2,1)S(1)}, u32[]{:S(2)}, u32[]{:S(2)}) %all-to-all-start) | async-done | bytes 524320 | tf_op jit(solution)/shard_map/while/body/eval_jaxpr/all_to_all | solution.py:17
  255.5 0.5 convolution_bitcast_fusion.4
  256.0 0.5 multiply_reduce_fusion.2
  256.7 5.3 %collective-permute-start = (bf16[2,256,256]{1,2,0:T(8,128)(2,1)S(1)}, bf16[2,256,256]{1,2,0:T(8,128)(2,1)S(1)}, u32[]{:S(2)}, u32[]{:S(2)}) collective-permute-start(bf16[2,256,256]{1,2,0:T(8,128)(2,1)S(1)} %get-tuple-element.463), channel_id=1, source_target_pairs={{0,64},{64,128},{128,192},{192,256},{256,320},{320,384},{384,448},... | collective-permute-start | bytes 786440 | tf_op jit(solution)/shard_map/while/body/eval_jaxpr/ppermute | solution.py:10
  262.1 5.3 %collective-permute-done = bf16[2,256,256]{1,2,0:T(8,128)(2,1)S(1)} collective-permute-done((bf16[2,256,256]{1,2,0:T(8,128)(2,1)S(1)}, bf16[2,256,256]{1,2,0:T(8,128)(2,1)S(1)}, u32[]{:S(2)}, u32[]{:S(2)}) %collective-permute-start) | collective-permute-done | bytes 262176 | tf_op jit(solution)/shard_map/while/body/eval_jaxpr/ppermute | solution.py:10
  267.4 1.1 fusion.38
  268.5 6.8 %all-to-all-start = ((bf16[64,2,8,256]{3,2,1,0:T(8,128)(2,1)}), bf16[64,2,8,256]{3,2,1,0:T(8,128)(2,1)S(1)}, u32[]{:S(2)}, u32[]{:S(2)}) async-start(bf16[64,2,8,256]{3,2,1,0:T(8,128)(2,1)} %fusion.38), calls=%async_computation | async-start | bytes 1048576 | tf_op jit(solution)/shard_map/while/body/eval_jaxpr/all_to_all | solution.py:17
  275.3 17.3 %all-to-all-done = bf16[64,2,8,256]{3,2,1,0:T(8,128)(2,1)S(1)} async-done(((bf16[64,2,8,256]{3,2,1,0:T(8,128)(2,1)}), bf16[64,2,8,256]{3,2,1,0:T(8,128)(2,1)S(1)}, u32[]{:S(2)}, u32[]{:S(2)}) %all-to-all-start) | async-done | bytes 524320 | tf_op jit(solution)/shard_map/while/body/eval_jaxpr/all_to_all | solution.py:17
  292.6 0.5 convolution_bitcast_fusion.4
  293.2 0.5 multiply_reduce_fusion.2
  293.9 5.3 %collective-permute-start = (bf16[2,256,256]{1,2,0:T(8,128)(2,1)S(1)}, bf16[2,256,256]{1,2,0:T(8,128)(2,1)S(1)}, u32[]{:S(2)}, u32[]{:S(2)}) collective-permute-start(bf16[2,256,256]{1,2,0:T(8,128)(2,1)S(1)} %get-tuple-element.463), channel_id=1, source_target_pairs={{0,64},{64,128},{128,192},{192,256},{256,320},{320,384},{384,448},... | collective-permute-start | bytes 786440 | tf_op jit(solution)/shard_map/while/body/eval_jaxpr/ppermute | solution.py:10
  299.2 5.3 %collective-permute-done = bf16[2,256,256]{1,2,0:T(8,128)(2,1)S(1)} collective-permute-done((bf16[2,256,256]{1,2,0:T(8,128)(2,1)S(1)}, bf16[2,256,256]{1,2,0:T(8,128)(2,1)S(1)}, u32[]{:S(2)}, u32[]{:S(2)}) %collective-permute-start) | collective-permute-done | bytes 262176 | tf_op jit(solution)/shard_map/while/body/eval_jaxpr/ppermute | solution.py:10
  304.5 0.8 copy.33
  (36 shorter events, 2.0 us)
Async XLA Ops:
  0.0 1.4 copy-start.5
  1.4 1.7 copy-start.3
  3.4 1.0 copy-start
  4.3 0.9 copy-start.1
  5.2 0.7 copy-start.4
  6.0 0.7 copy-start.2
  6.0 0.7 copy-start.6
  7.9 29.0 %all-to-all-start = ((bf16[64,2,8,256]{3,2,1,0:T(8,128)(2,1)}), bf16[64,2,8,256]{3,2,1,0:T(8,128)(2,1)S(1)}, u32[]{:S(2)}, u32[]{:S(2)}) async-start(bf16[64,2,8,256]{3,2,1,0:T(8,128)(2,1)} %fusion.38), calls=%async_computation | async-start | bytes 1048576 | tf_op jit(solution)/shard_map/while/body/eval_jaxpr/all_to_all | solution.py:17
  38.0 9.3 %collective-permute-start = (bf16[2,256,256]{1,2,0:T(8,128)(2,1)S(1)}, bf16[2,256,256]{1,2,0:T(8,128)(2,1)S(1)}, u32[]{:S(2)}, u32[]{:S(2)}) collective-permute-start(bf16[2,256,256]{1,2,0:T(8,128)(2,1)S(1)} %get-tuple-element.463), channel_id=1, source_target_pairs={{0,64},{64,128},{128,192},{192,256},{256,320},{320,384},{384,448},... | collective-permute-start | bytes 786440 | tf_op jit(solution)/shard_map/while/body/eval_jaxpr/ppermute | solution.py:10
  48.5 24.1 %all-to-all-start = ((bf16[64,2,8,256]{3,2,1,0:T(8,128)(2,1)}), bf16[64,2,8,256]{3,2,1,0:T(8,128)(2,1)S(1)}, u32[]{:S(2)}, u32[]{:S(2)}) async-start(bf16[64,2,8,256]{3,2,1,0:T(8,128)(2,1)} %fusion.38), calls=%async_computation | async-start | bytes 1048576 | tf_op jit(solution)/shard_map/while/body/eval_jaxpr/all_to_all | solution.py:17
  73.8 9.5 %collective-permute-start = (bf16[2,256,256]{1,2,0:T(8,128)(2,1)S(1)}, bf16[2,256,256]{1,2,0:T(8,128)(2,1)S(1)}, u32[]{:S(2)}, u32[]{:S(2)}) collective-permute-start(bf16[2,256,256]{1,2,0:T(8,128)(2,1)S(1)} %get-tuple-element.463), channel_id=1, source_target_pairs={{0,64},{64,128},{128,192},{192,256},{256,320},{320,384},{384,448},... | collective-permute-start | bytes 786440 | tf_op jit(solution)/shard_map/while/body/eval_jaxpr/ppermute | solution.py:10
  84.4 24.1 %all-to-all-start = ((bf16[64,2,8,256]{3,2,1,0:T(8,128)(2,1)}), bf16[64,2,8,256]{3,2,1,0:T(8,128)(2,1)S(1)}, u32[]{:S(2)}, u32[]{:S(2)}) async-start(bf16[64,2,8,256]{3,2,1,0:T(8,128)(2,1)} %fusion.38), calls=%async_computation | async-start | bytes 1048576 | tf_op jit(solution)/shard_map/while/body/eval_jaxpr/all_to_all | solution.py:17
  109.8 9.5 %collective-permute-start = (bf16[2,256,256]{1,2,0:T(8,128)(2,1)S(1)}, bf16[2,256,256]{1,2,0:T(8,128)(2,1)S(1)}, u32[]{:S(2)}, u32[]{:S(2)}) collective-permute-start(bf16[2,256,256]{1,2,0:T(8,128)(2,1)S(1)} %get-tuple-element.463), channel_id=1, source_target_pairs={{0,64},{64,128},{128,192},{192,256},{256,320},{320,384},{384,448},... | collective-permute-start | bytes 786440 | tf_op jit(solution)/shard_map/while/body/eval_jaxpr/ppermute | solution.py:10
  120.4 24.1 %all-to-all-start = ((bf16[64,2,8,256]{3,2,1,0:T(8,128)(2,1)}), bf16[64,2,8,256]{3,2,1,0:T(8,128)(2,1)S(1)}, u32[]{:S(2)}, u32[]{:S(2)}) async-start(bf16[64,2,8,256]{3,2,1,0:T(8,128)(2,1)} %fusion.38), calls=%async_computation | async-start | bytes 1048576 | tf_op jit(solution)/shard_map/while/body/eval_jaxpr/all_to_all | solution.py:17
  145.7 10.3 %collective-permute-start = (bf16[2,256,256]{1,2,0:T(8,128)(2,1)S(1)}, bf16[2,256,256]{1,2,0:T(8,128)(2,1)S(1)}, u32[]{:S(2)}, u32[]{:S(2)}) collective-permute-start(bf16[2,256,256]{1,2,0:T(8,128)(2,1)S(1)} %get-tuple-element.463), channel_id=1, source_target_pairs={{0,64},{64,128},{128,192},{192,256},{256,320},{320,384},{384,448},... | collective-permute-start | bytes 786440 | tf_op jit(solution)/shard_map/while/body/eval_jaxpr/ppermute | solution.py:10
  157.1 24.1 %all-to-all-start = ((bf16[64,2,8,256]{3,2,1,0:T(8,128)(2,1)}), bf16[64,2,8,256]{3,2,1,0:T(8,128)(2,1)S(1)}, u32[]{:S(2)}, u32[]{:S(2)}) async-start(bf16[64,2,8,256]{3,2,1,0:T(8,128)(2,1)} %fusion.38), calls=%async_computation | async-start | bytes 1048576 | tf_op jit(solution)/shard_map/while/body/eval_jaxpr/all_to_all | solution.py:17
  182.5 10.7 %collective-permute-start = (bf16[2,256,256]{1,2,0:T(8,128)(2,1)S(1)}, bf16[2,256,256]{1,2,0:T(8,128)(2,1)S(1)}, u32[]{:S(2)}, u32[]{:S(2)}) collective-permute-start(bf16[2,256,256]{1,2,0:T(8,128)(2,1)S(1)} %get-tuple-element.463), channel_id=1, source_target_pairs={{0,64},{64,128},{128,192},{192,256},{256,320},{320,384},{384,448},... | collective-permute-start | bytes 786440 | tf_op jit(solution)/shard_map/while/body/eval_jaxpr/ppermute | solution.py:10
  194.3 24.1 %all-to-all-start = ((bf16[64,2,8,256]{3,2,1,0:T(8,128)(2,1)}), bf16[64,2,8,256]{3,2,1,0:T(8,128)(2,1)S(1)}, u32[]{:S(2)}, u32[]{:S(2)}) async-start(bf16[64,2,8,256]{3,2,1,0:T(8,128)(2,1)} %fusion.38), calls=%async_computation | async-start | bytes 1048576 | tf_op jit(solution)/shard_map/while/body/eval_jaxpr/all_to_all | solution.py:17
  219.6 10.7 %collective-permute-start = (bf16[2,256,256]{1,2,0:T(8,128)(2,1)S(1)}, bf16[2,256,256]{1,2,0:T(8,128)(2,1)S(1)}, u32[]{:S(2)}, u32[]{:S(2)}) collective-permute-start(bf16[2,256,256]{1,2,0:T(8,128)(2,1)S(1)} %get-tuple-element.463), channel_id=1, source_target_pairs={{0,64},{64,128},{128,192},{192,256},{256,320},{320,384},{384,448},... | collective-permute-start | bytes 786440 | tf_op jit(solution)/shard_map/while/body/eval_jaxpr/ppermute | solution.py:10
  231.4 24.1 %all-to-all-start = ((bf16[64,2,8,256]{3,2,1,0:T(8,128)(2,1)}), bf16[64,2,8,256]{3,2,1,0:T(8,128)(2,1)S(1)}, u32[]{:S(2)}, u32[]{:S(2)}) async-start(bf16[64,2,8,256]{3,2,1,0:T(8,128)(2,1)} %fusion.38), calls=%async_computation | async-start | bytes 1048576 | tf_op jit(solution)/shard_map/while/body/eval_jaxpr/all_to_all | solution.py:17
  256.7 10.7 %collective-permute-start = (bf16[2,256,256]{1,2,0:T(8,128)(2,1)S(1)}, bf16[2,256,256]{1,2,0:T(8,128)(2,1)S(1)}, u32[]{:S(2)}, u32[]{:S(2)}) collective-permute-start(bf16[2,256,256]{1,2,0:T(8,128)(2,1)S(1)} %get-tuple-element.463), channel_id=1, source_target_pairs={{0,64},{64,128},{128,192},{192,256},{256,320},{320,384},{384,448},... | collective-permute-start | bytes 786440 | tf_op jit(solution)/shard_map/while/body/eval_jaxpr/ppermute | solution.py:10
  268.5 24.1 %all-to-all-start = ((bf16[64,2,8,256]{3,2,1,0:T(8,128)(2,1)}), bf16[64,2,8,256]{3,2,1,0:T(8,128)(2,1)S(1)}, u32[]{:S(2)}, u32[]{:S(2)}) async-start(bf16[64,2,8,256]{3,2,1,0:T(8,128)(2,1)} %fusion.38), calls=%async_computation | async-start | bytes 1048576 | tf_op jit(solution)/shard_map/while/body/eval_jaxpr/all_to_all | solution.py:17
  293.9 10.7 %collective-permute-start = (bf16[2,256,256]{1,2,0:T(8,128)(2,1)S(1)}, bf16[2,256,256]{1,2,0:T(8,128)(2,1)S(1)}, u32[]{:S(2)}, u32[]{:S(2)}) collective-permute-start(bf16[2,256,256]{1,2,0:T(8,128)(2,1)S(1)} %get-tuple-element.463), channel_id=1, source_target_pairs={{0,64},{64,128},{128,192},{192,256},{256,320},{320,384},{384,448},... | collective-permute-start | bytes 786440 | tf_op jit(solution)/shard_map/while/body/eval_jaxpr/ppermute | solution.py:10
where the time goes:
time: 310 us; the launch traced here: 305 us
  waiting for transfers between devices  181 us (58%)
  starting transfers between devices  97.6 us (31%)
  matrix products  19.1 us (6%)
  local copies, waits for them, and re-layouts  4.22 us (1%)
    all_to_all x8, waiting for transfers between devices, boundary_rows(): lax.all_to_all(outgoing, 'dom', split_axis=0, concat_axis=0, tiled=True)  139 us
    all_to_all x8, starting transfers between devices, boundary_rows(): lax.all_to_all(outgoing, 'dom', split_axis=0, concat_axis=0, tiled=True)  59.1 us
    ppermute x8, waiting for transfers between devices, from_behind(): return lax.ppermute(array, axis, pairs)  42.7 us
    ppermute x8, starting transfers between devices, from_behind(): return lax.ppermute(array, axis, pairs)  38.6 us
    dot_general x8, matrix products, boundary_rows(): jnp.einsum('cpsi,cid->pcsd', gather_sel, hidden, preferred_element_type=j...  9.02 us
  transfers between devices with their start and end apart: 16, of which 16 were waited for; matrix products, arithmetic and copies ran while one was open for 0% of the time, Pallas kernels for 0%

commit v1 on v0

v1 whole, which is shorter than its diff:
```python
import functools

import jax
import jax.numpy as jnp
from jax import lax
from jax.experimental import pallas as pl
from jax.experimental.pallas import tpu as pltpu
from jax.sharding import PartitionSpec as P

VMEM = pltpu.VMEM
PACK_ROWS = 16


def whole(count):
    return [pl.BlockSpec(memory_space=VMEM)] * count


def slot_column(table, slots):
    count = table.shape[0]
    rows = count * slots
    expand = (
        lax.broadcasted_iota(jnp.int32, (rows, count), 0) // slots
        == lax.broadcasted_iota(jnp.int32, (rows, count), 1)
    ).astype(jnp.bfloat16)
    spread = jnp.dot(expand, table.astype(jnp.float32).astype(jnp.bfloat16), preferred_element_type=jnp.float32)
    here = lax.broadcasted_iota(jnp.int32, (rows, slots), 0) % slots == lax.broadcasted_iota(
        jnp.int32, (rows, slots), 1
    )
    return jnp.sum(jnp.where(here, spread, 0.0), axis=1, keepdims=True)


def one_hot_rows(column, width):
    ids = lax.broadcasted_iota(jnp.int32, (column.shape[0], width), 1)
    return (column.astype(jnp.int32) == ids).astype(jnp.float32).astype(jnp.bfloat16)


def first_kernel(span_ref, features_ref, send_ref, hidden_ref, select_ref, outgoing_ref):
    hidden = features_ref[0]
    hidden_ref[...] = hidden
    select = one_hot_rows(slot_column(send_ref[0, 0], send_ref.shape[-1]), hidden.shape[0])
    select_ref[...] = select
    outgoing_ref[...] = jnp.dot(select, hidden, preferred_element_type=jnp.float32).astype(jnp.bfloat16)


def first_gather(span, features, send_rows):
    _, rows, width = features.shape
    peers, slots = send_rows.shape[2:]
    return pl.pallas_call(
        first_kernel,
        grid_spec=pltpu.PrefetchScalarGridSpec(
            num_scalar_prefetch=1,
            grid=(1,),
            in_specs=[
                pl.BlockSpec((1, rows, width), lambda i, s: (s[0], 0, 0)),
                pl.BlockSpec((1, 1, peers, slots), lambda i, s: (s[0], 0, 0, 0)),
            ],
            out_specs=[
                pl.BlockSpec((rows, width), lambda i, s: (0, 0)),
                pl.BlockSpec((peers * slots, rows), lambda i, s: (0, 0)),
                pl.BlockSpec((peers * slots, width), lambda i, s: (0, 0)),
            ],
        ),
        out_shape=[
            jax.ShapeDtypeStruct((rows, width), jnp.bfloat16),
            jax.ShapeDtypeStruct((peers * slots, rows), jnp.bfloat16),
            jax.ShapeDtypeStruct((peers * slots, width), jnp.bfloat16),
        ],
        name="first_gather",
    )(span, features, send_rows)


def tables_kernel(span_ref, col_ref, adj_ref, dest_ref, near_ref, scatter_ref, inverse_ref):
    _, blocks, tiles, side, _ = adj_ref.shape
    span = span_ref[0]
    rows = blocks * side
    scatter = one_hot_rows(slot_column(dest_ref[0, 0], dest_ref.shape[-1]), rows).astype(jnp.float32).T
    scatter_ref[...] = scatter.astype(jnp.bfloat16)
    degree = 1.0 + jnp.sum(scatter, axis=1, keepdims=True)
    for r in range(blocks):
        below = slice(r * side, (r + 1) * side)
        local_degree = jnp.zeros((side, 1), jnp.float32)
        for b in range(blocks):
            total = jnp.zeros((side, side), jnp.int32)
            for k in range(tiles):
                hit = col_ref[(span * blocks + r) * tiles + k] == b
                total += jnp.where(hit, adj_ref[0, r, k], 0)
            dense = total.astype(jnp.float32)
            local_degree += jnp.sum(dense, axis=1, keepdims=True)
            if b == r:
                dense += (
                    lax.broadcasted_iota(jnp.int32, (side, side), 0)
                    == lax.broadcasted_iota(jnp.int32, (side, side), 1)
                ).astype(jnp.float32)
            near_ref[below, b * side : (b + 1) * side] = dense.astype(jnp.bfloat16)
        inverse_ref[below, :] = jnp.broadcast_to(
            1.0 / (degree[below] + local_degree), (side, inverse_ref.shape[1])
        )


def build_tables(span, tile_col, tile_adj, recv_dst):
    _, blocks, tiles, side, _ = tile_adj.shape
    rows = blocks * side
    peers, slots = recv_dst.shape[2:]
    return pl.pallas_call(
        tables_kernel,
        grid_spec=pltpu.PrefetchScalarGridSpec(
            num_scalar_prefetch=2,
            grid=(1,),
            in_specs=[
                pl.BlockSpec((1, blocks, tiles, side, side), lambda i, s, c: (s[0], 0, 0, 0, 0)),
                pl.BlockSpec((1, 1, peers, slots), lambda i, s, c: (s[0], 0, 0, 0)),
            ],
            out_specs=[
                pl.BlockSpec((rows, rows), lambda i, s, c: (0, 0)),
                pl.BlockSpec((rows, peers * slots), lambda i, s, c: (0, 0)),
                pl.BlockSpec((rows, side), lambda i, s, c: (0, 0)),
            ],
        ),
        out_shape=[
            jax.ShapeDtypeStruct((rows, rows), jnp.bfloat16),
            jax.ShapeDtypeStruct((rows, peers * slots), jnp.bfloat16),
            jax.ShapeDtypeStruct((rows, side), jnp.float32),
        ],
        name="build_tables",
    )(span, tile_col.reshape(-1), tile_adj, recv_dst)


def layer_math(hidden_ref, arrived_ref, near_ref, scatter_ref, inverse_ref, pack_ref):
    rows, width = hidden_ref.shape
    hidden = hidden_ref[...]
    total = jnp.dot(near_ref[...], hidden, preferred_element_type=jnp.float32)
    total += jnp.dot(scatter_ref[...], arrived_ref[...], preferred_element_type=jnp.float32)
    inverse = jnp.concatenate([inverse_ref[...]] * (width // inverse_ref.shape[1]), axis=1)
    mean = (total * inverse).astype(jnp.bfloat16)
    vectors = pack_ref[width : width + PACK_ROWS, :].astype(jnp.float32)
    bias = vectors[0:1] + vectors[1:2]
    gain = vectors[2:3] + vectors[3:4]
    projected = jnp.dot(mean, pack_ref[0:width, :], preferred_element_type=jnp.float32) + bias
    summed = hidden.astype(jnp.float32) + jnp.maximum(projected, 0.0)
    scale = lax.rsqrt(jnp.mean(summed * summed, axis=1, keepdims=True) + 1e-05)
    return (summed * scale * gain).astype(jnp.bfloat16)


def layer_kernel(
    hidden_ref, arrived_ref, near_ref, scatter_ref, inverse_ref, pack_ref, select_ref, next_ref, outgoing_ref
):
    state = layer_math(hidden_ref, arrived_ref, near_ref, scatter_ref, inverse_ref, pack_ref)
    next_ref[...] = state
    outgoing_ref[...] = jnp.dot(select_ref[...], state, preferred_element_type=jnp.float32).astype(jnp.bfloat16)


def last_kernel(hidden_ref, arrived_ref, near_ref, scatter_ref, inverse_ref, pack_ref, next_ref):
    next_ref[...] = layer_math(hidden_ref, arrived_ref, near_ref, scatter_ref, inverse_ref, pack_ref)


def run_layer(hidden, arrived, tables, pack, select):
    state = jax.ShapeDtypeStruct(hidden.shape, jnp.bfloat16)
    if select is None:
        return pl.pallas_call(
            last_kernel,
            out_shape=state,
            in_specs=whole(6),
            out_specs=pl.BlockSpec(memory_space=VMEM),
            name="last_layer",
        )(hidden, arrived, *tables, pack), None
    return pl.pallas_call(
        layer_kernel,
        out_shape=[state, jax.ShapeDtypeStruct((select.shape[0], hidden.shape[1]), jnp.bfloat16)],
        in_specs=whole(7),
        out_specs=whole(2),
        name="layer",
    )(hidden, arrived, *tables, pack, select)


def pack_layer(weight, bias, gain):
    rows = []
    for vector in (bias, gain):
        high = lax.reduce_precision(vector, 8, 7)
        rows += [high, vector - high]
    small = jnp.concatenate(rows + [jnp.zeros((PACK_ROWS - 4, weight.shape[1]), jnp.float32)], axis=0)
    return jnp.concatenate([weight, small.astype(jnp.bfloat16)], axis=0)


def local(features, weight, bias, gain, tile_col, tile_adj, send_rows, recv_dst):
    layers = lax.axis_size("layer")
    plane = lax.axis_index("layer")
    first, last = 0, layers - 1
    peers, slots = send_rows.shape[2:]
    width = features.shape[-1]
    span = (2 * plane >= layers).astype(jnp.int32).reshape(1)
    hidden, select, outgoing = first_gather(span, features, send_rows)
    own_pack = pack_layer(weight[0], bias, gain)
    tables = build_tables(span, tile_col, tile_adj, recv_dst)

    previous = before = None
    came = own_pack
    kept = [None, None]
    for step in range(layers):
        arrived = lax.all_to_all(outgoing.reshape(peers, slots, width), "dom", 0, 0, tiled=True)
        if step < last:
            arriving = lax.ppermute(own_pack, "layer", [(step, last), (step + 1, first)])
        else:
            arriving = own_pack
        pack = jnp.where(plane == first, came, arriving)
        came = arriving
        if step >= 2:
            back = lax.ppermute(
                jnp.where(plane == first, hidden, previous), "layer", [(first, step - 1), (last, step - 2)]
            )
            kept[0] = jnp.where(plane == step - 1, back, kept[0])
            kept[1] = back if kept[1] is None else jnp.where(plane == step - 2, back, kept[1])
        previous, before = hidden, previous
        hidden, outgoing = run_layer(
            hidden, arrived.reshape(peers * slots, width), tables, pack, select if step < last else None
        )
        if step == 0:
            kept[0] = hidden
    back = lax.ppermute(
        jnp.where(plane == first, hidden, previous), "layer", [(first, last), (last, last - 1)]
    )
    kept[0] = jnp.where(plane == last, back, kept[0])
    kept[1] = jnp.where(plane == last, hidden, jnp.where(plane == last - 1, back, kept[1]))
    return jnp.stack(kept)[None]


def solution(mesh):
    in_specs = (
        P(None, "dom", None),
        P("layer", None, None),
        P("layer", None),
        P("layer", None),
        P(None, "dom", None),
        P(None, "dom", None, None, None),
        P(None, "dom", None, None),
        P(None, "dom", None, None),
    )
    out_specs = P("layer", None, "dom", None)
    return jax.shard_map(local, mesh=mesh, in_specs=in_specs, out_specs=out_specs, check_vma=False)
```

time: 310 us -> 230 us (0.74)
  waiting for transfers between devices: 181 us -> 19 us
  blocking collectives: 0 us -> 131 us
  starting transfers between devices: 97.6 us -> 43.4 us
  Pallas kernels: 0 us -> 26.8 us
  matrix products: 19.1 us -> 0 us
    all_to_all x8 -> x1, waiting for transfers between devices: 139 us -> 0.01 us  [local(): lax.all_to_all(outgoing.reshape(peers, slots, width), 'dom', 0, 0, tiled=...]
    all_to_all x0 -> x7, blocking collectives: none -> 131 us  [local(): lax.all_to_all(outgoing.reshape(peers, slots, width), 'dom', 0, 0, tiled=...]
    all_to_all x8 -> x1, starting transfers between devices: 59.1 us -> 11.2 us  [local(): lax.all_to_all(outgoing.reshape(peers, slots, width), 'dom', 0, 0, tiled=...]
    pallas_call x0 -> x10, Pallas kernels: none -> 26.8 us  [the longest x7 19.5 us: run_layer(): pl.pallas_call(layer_kernel, out_shape=[state, jax.ShapeDtypeStruct((sele...]
    ppermute x8 -> x14, waiting for transfers between devices: 42.7 us -> 19 us  [the longest x7 13.8 us: local(): lax.ppermute(own_pack, 'layer', [(step, last), (step + 1, first)])]
    dot_general x25 -> x0, matrix products: 19.1 us -> none  [the longest x8 9.02 us: boundary_rows(): jnp.einsum('cpsi,cid->pcsd', gather_sel, hidden, preferred_element_type=j...]
    ppermute x8 -> x14, starting transfers between devices: 38.6 us -> 32.2 us  [the longest x7 19.3 us: local(): lax.ppermute(own_pack, 'layer', [(step, last), (step + 1, first)])]
  transfers between devices with their start and end apart: 16 -> 15, of which waited for: 16 -> 7; matrix products, arithmetic and copies ran while one was open for 0% -> 1% of each run, Pallas kernels for 0% -> 2%
where the time goes in v1:
time: 230 us; the launch traced here: 228 us
  blocking collectives  131 us (57%)
  starting transfers between devices  43.4 us (19%)
  Pallas kernels  26.8 us (12%)
  waiting for transfers between devices  19 us (8%)
  local copies, waits for them, and re-layouts  3.93 us (2%)
  other arithmetic  3.57 us (2%)
    all_to_all x7, blocking collectives, local(): lax.all_to_all(outgoing.reshape(peers, slots, width), 'dom', 0, 0, tiled=...  131 us
    pallas_call x7, Pallas kernels, run_layer(): pl.pallas_call(layer_kernel, out_shape=[state, jax.ShapeDtypeStruct((sele...  19.5 us
    ppermute x7, starting transfers between devices, local(): lax.ppermute(own_pack, 'layer', [(step, last), (step + 1, first)])  19.3 us
    ppermute x7, waiting for transfers between devices, local(): lax.ppermute(own_pack, 'layer', [(step, last), (step + 1, first)])  13.8 us
    ppermute x7, starting transfers between devices, local(): lax.ppermute(jnp.where(plane == first, hidden, previous), 'layer', [(firs...  13 us
    all_to_all x1, starting transfers between devices, local(): lax.all_to_all(outgoing.reshape(peers, slots, width), 'dom', 0, 0, tiled=...  11.2 us
    ppermute x7, waiting for transfers between devices, local(): lax.ppermute(jnp.where(plane == first, hidden, previous), 'layer', [(firs...  5.12 us
  transfers between devices with their start and end apart: 15, of which 7 were waited for; matrix products, arithmetic and copies ran while one was open for 1% of the time, Pallas kernels for 2%

profile of v1, /device:TPU:1, one launch (start us, length us, event | category | flops | bytes accessed | tf_op | source)
XLA Modules:
  0.0 228.5 jit_solution(414965271610732460)
XLA Ops:
  0.0 0.7 fusion
  0.7 1.1 concatenate.6
  1.8 0.0 copy-start.9
  1.8 11.5 %collective-permute-start = (bf16[272,256]{1,0:T(8,128)(2,1)S(1)}, bf16[272,256]{1,0:T(8,128)(2,1)S(1)}, u32[]{:S(2)}, u32[]{:S(2)}) collective-permute-start(bf16[272,256]{1,0:T(8,128)(2,1)S(1)} %concatenate.6), channel_id=1, source_target_pairs={{0,448},{64,0},{1,449},{65,1},{2,450},{66,2},{3,451},{67,3},{4,452... | collective-permute-start | bytes 417800 | tf_op jit(solution)/shard_map/ppermute | solution.py:201
  13.3 1.3 collective-permute-start.1
  14.6 0.0 copy-done.9
  14.6 0.7 copy.9.send_ref
  15.3 2.0 first_gather.1
  17.4 11.2 %all-to-all-start = ((bf16[64,8,256]{2,1,0:T(8,128)(2,1)}), bf16[64,8,256]{2,1,0:T(8,128)(2,1)S(1)}, u32[]{:S(2)}, u32[]{:S(2)}) async-start(bf16[64,8,256]{2,1,0:T(8,128)(2,1)} %bitcast.32), calls=%async_computation | async-start | bytes 524288 | tf_op jit(solution)/shard_map/all_to_all | solution.py:199
  28.6 1.3 collective-permute-start.2
  29.9 1.3 collective-permute-start.3
  31.2 1.3 collective-permute-start.4
  32.5 0.0 collective-permute-done
  32.5 1.3 collective-permute-start.5
  33.8 0.0 collective-permute-done.1
  33.8 1.3 collective-permute-start.6
  35.1 0.0 copy-start.11
  35.1 0.7 copy.10.dest_ref
  35.9 0.7 reshape.60.col_ref
  36.5 2.9 %build_tables.1 = (bf16[256,256]{1,0:T(8,128)(2,1)}, bf16[256,512]{1,0:T(8,128)(2,1)}, f32[256,128]{1,0:T(8,128)}) custom-call(s32[1]{0:T(128)} %bitcast.span_ref, s32[16]{0:T(128)} %reshape.60.col_ref, s32[2,2,4,128,128]{4,3,2,1,0:T(8,128)} %adj_ref.1, s32[2,1,64,8]{3,2,1,0:T(8,128)} %copy.10.dest_ref), custom_call_target="tpu_custom_call" | custom-call | tf_op jit(solution)/shard_map/build_tables/pallas_call | solution.py:104
  39.4 0.0 collective-permute-done.2
  39.4 1.1 collective-permute-done.3
  40.5 6.8 %collective-permute-done.4 = bf16[272,256]{1,0:T(8,128)(2,1)S(1)} collective-permute-done((bf16[272,256]{1,0:T(8,128)(2,1)S(1)}, bf16[272,256]{1,0:T(8,128)(2,1)S(1)}, u32[]{:S(2)}, u32[]{:S(2)}) %collective-permute-start.4) | collective-permute-done | bytes 139296 | tf_op jit(solution)/shard_map/ppermute | solution.py:201
  47.3 5.9 %collective-permute-done.5 = bf16[272,256]{1,0:T(8,128)(2,1)S(1)} collective-permute-done((bf16[272,256]{1,0:T(8,128)(2,1)S(1)}, bf16[272,256]{1,0:T(8,128)(2,1)S(1)}, u32[]{:S(2)}, u32[]{:S(2)}) %collective-permute-start.5) | collective-permute-done | bytes 139296 | tf_op jit(solution)/shard_map/ppermute | solution.py:201
  53.2 0.0 collective-permute-done.6
  53.2 1.0 broadcast_select_fusion
  54.3 0.0 all-to-all-done
  54.3 0.7 copy-done.2
  55.0 2.8 %layer.7 = (bf16[256,256]{1,0:T(8,128)(2,1)}, bf16[512,256]{1,0:T(8,128)(2,1)}) custom-call(bf16[256,256]{1,0:T(8,128)(2,1)} %get-tuple-element.25.hidden_ref, bf16[512,256]{1,0:T(8,128)(2,1)} %bitcast.24, bf16[256,256]{1,0:T(8,128)(2,1)} %get-tuple-element.27.near_ref, bf16[256,512]{1,0:T(8,128)(2,1)} %get-tuple-element.28.scatter_ref, ...), custom_call_target="tpu_custom_call" | custom-call | tf_op jit(solution)/shard_map/layer/pallas_call | solution.py:166
  57.8 22.6 %all_to_all.40 = bf16[64,8,256]{2,1,0:T(8,128)(2,1)} all-to-all(bf16[64,8,256]{2,1,0:T(8,128)(2,1)} %bitcast.33), channel_id=1, replica_groups=mesh['layer'=8,'dom'=64] {'dom'}, dimensions={0} | all-to-all | bytes 524288 | tf_op jit(solution)/shard_map/all_to_all | solution.py:199
  80.4 2.8 %layer.8 = (bf16[256,256]{1,0:T(8,128)(2,1)}, bf16[512,256]{1,0:T(8,128)(2,1)}) custom-call(bf16[256,256]{1,0:T(8,128)(2,1)} %get-tuple-element.31.hidden_ref, bf16[512,256]{1,0:T(8,128)(2,1)} %bitcast.26, bf16[256,256]{1,0:T(8,128)(2,1)} %get-tuple-element.27.near_ref, bf16[256,512]{1,0:T(8,128)(2,1)} %get-tuple-element.28.scatter_ref, ...), custom_call_target="tpu_custom_call" | custom-call | tf_op jit(solution)/shard_map/layer/pallas_call | solution.py:166
  83.2 18.1 %all_to_all.41 = bf16[64,8,256]{2,1,0:T(8,128)(2,1)} all-to-all(bf16[64,8,256]{2,1,0:T(8,128)(2,1)} %bitcast.35), channel_id=1, replica_groups=mesh['layer'=8,'dom'=64] {'dom'}, dimensions={0} | all-to-all | bytes 524288 | tf_op jit(solution)/shard_map/all_to_all | solution.py:199
  101.3 2.8 %layer.9 = (bf16[256,256]{1,0:T(8,128)(2,1)}, bf16[512,256]{1,0:T(8,128)(2,1)}) custom-call(bf16[256,256]{1,0:T(8,128)(2,1)} %get-tuple-element.33.hidden_ref, bf16[512,256]{1,0:T(8,128)(2,1)} %bitcast.27, bf16[256,256]{1,0:T(8,128)(2,1)} %get-tuple-element.27.near_ref, bf16[256,512]{1,0:T(8,128)(2,1)} %get-tuple-element.28.scatter_ref, ...), custom_call_target="tpu_custom_call" | custom-call | tf_op jit(solution)/shard_map/layer/pallas_call | solution.py:166
  104.1 18.1 %all_to_all.42 = bf16[64,8,256]{2,1,0:T(8,128)(2,1)} all-to-all(bf16[64,8,256]{2,1,0:T(8,128)(2,1)} %bitcast.36), channel_id=1, replica_groups=mesh['layer'=8,'dom'=64] {'dom'}, dimensions={0} | all-to-all | bytes 524288 | tf_op jit(solution)/shard_map/all_to_all | solution.py:199
  122.2 2.8 %layer.10 = (bf16[256,256]{1,0:T(8,128)(2,1)}, bf16[512,256]{1,0:T(8,128)(2,1)}) custom-call(bf16[256,256]{1,0:T(8,128)(2,1)} %get-tuple-element.35.hidden_ref, bf16[512,256]{1,0:T(8,128)(2,1)} %bitcast.28, bf16[256,256]{1,0:T(8,128)(2,1)} %get-tuple-element.27.near_ref, bf16[256,512]{1,0:T(8,128)(2,1)} %get-tuple-element.28.scatter_ref, ...), custom_call_target="tpu_custom_call" | custom-call | tf_op jit(solution)/shard_map/layer/pallas_call | solution.py:166
  125.0 18.1 %all_to_all.43 = bf16[64,8,256]{2,1,0:T(8,128)(2,1)} all-to-all(bf16[64,8,256]{2,1,0:T(8,128)(2,1)} %bitcast.37), channel_id=1, replica_groups=mesh['layer'=8,'dom'=64] {'dom'}, dimensions={0} | all-to-all | bytes 524288 | tf_op jit(solution)/shard_map/all_to_all | solution.py:199
  143.1 2.8 %layer.11 = (bf16[256,256]{1,0:T(8,128)(2,1)}, bf16[512,256]{1,0:T(8,128)(2,1)}) custom-call(bf16[256,256]{1,0:T(8,128)(2,1)} %get-tuple-element.37.hidden_ref, bf16[512,256]{1,0:T(8,128)(2,1)} %bitcast.29, bf16[256,256]{1,0:T(8,128)(2,1)} %get-tuple-element.27.near_ref, bf16[256,512]{1,0:T(8,128)(2,1)} %get-tuple-element.28.scatter_ref, ...), custom_call_target="tpu_custom_call" | custom-call | tf_op jit(solution)/shard_map/layer/pallas_call | solution.py:166
  145.9 18.1 %all_to_all.44 = bf16[64,8,256]{2,1,0:T(8,128)(2,1)} all-to-all(bf16[64,8,256]{2,1,0:T(8,128)(2,1)} %bitcast.38), channel_id=1, replica_groups=mesh['layer'=8,'dom'=64] {'dom'}, dimensions={0} | all-to-all | bytes 524288 | tf_op jit(solution)/shard_map/all_to_all | solution.py:199
  164.1 2.8 %layer.12 = (bf16[256,256]{1,0:T(8,128)(2,1)}, bf16[512,256]{1,0:T(8,128)(2,1)}) custom-call(bf16[256,256]{1,0:T(8,128)(2,1)} %get-tuple-element.39.hidden_ref, bf16[512,256]{1,0:T(8,128)(2,1)} %bitcast.30, bf16[256,256]{1,0:T(8,128)(2,1)} %get-tuple-element.27.near_ref, bf16[256,512]{1,0:T(8,128)(2,1)} %get-tuple-element.28.scatter_ref, ...), custom_call_target="tpu_custom_call" | custom-call | tf_op jit(solution)/shard_map/layer/pallas_call | solution.py:166
  166.9 18.1 %all_to_all.45 = bf16[64,8,256]{2,1,0:T(8,128)(2,1)} all-to-all(bf16[64,8,256]{2,1,0:T(8,128)(2,1)} %bitcast.39), channel_id=1, replica_groups=mesh['layer'=8,'dom'=64] {'dom'}, dimensions={0} | all-to-all | bytes 524288 | tf_op jit(solution)/shard_map/all_to_all | solution.py:199
  185.0 2.8 %layer.13 = (bf16[256,256]{1,0:T(8,128)(2,1)}, bf16[512,256]{1,0:T(8,128)(2,1)}) custom-call(bf16[256,256]{1,0:T(8,128)(2,1)} %get-tuple-element.41.hidden_ref, bf16[512,256]{1,0:T(8,128)(2,1)} %bitcast.25, bf16[256,256]{1,0:T(8,128)(2,1)} %get-tuple-element.27.near_ref, bf16[256,512]{1,0:T(8,128)(2,1)} %get-tuple-element.28.scatter_ref, ...), custom_call_target="tpu_custom_call" | custom-call | tf_op jit(solution)/shard_map/layer/pallas_call | solution.py:166
  187.8 18.1 %all_to_all.46 = bf16[64,8,256]{2,1,0:T(8,128)(2,1)} all-to-all(bf16[64,8,256]{2,1,0:T(8,128)(2,1)} %bitcast.34), channel_id=1, replica_groups=mesh['layer'=8,'dom'=64] {'dom'}, dimensions={0} | all-to-all | bytes 524288 | tf_op jit(solution)/shard_map/all_to_all | solution.py:199
  205.9 0.0 copy-start.6
  205.9 0.0 copy-start.7
  205.9 0.0 copy-start.8
  205.9 2.4 %last_layer.1 = bf16[256,256]{1,0:T(8,128)(2,1)} custom-call(bf16[256,256]{1,0:T(8,128)(2,1)} %get-tuple-element.43.hidden_ref, bf16[512,256]{1,0:T(8,128)(2,1)} %bitcast.31, bf16[256,256]{1,0:T(8,128)(2,1)} %get-tuple-element.27.near_ref, bf16[256,512]{1,0:T(8,128)(2,1)} %get-tuple-element.28.scatter_ref, f32[256,128]{1,0:T(8,128)} %get-tuple-element.29.inverse_ref, ...), custom_call_target="tpu_custom_call" | custom-call | tf_op jit(solution)/shard_map/last_layer/pallas_call | solution.py:159
  208.4 0.0 copy-start.1
  208.4 1.0 broadcast_select_fusion.8
  209.5 1.3 collective-permute-start.10
  210.8 1.3 collective-permute-start.11
  212.1 1.3 collective-permute-start.12
  213.4 1.9 collective-permute-start.13
  215.3 4.6 %collective-permute-start.7 = (bf16[256,256]{1,0:T(8,128)(2,1)S(1)}, bf16[256,256]{1,0:T(8,128)(2,1)S(1)}, u32[]{:S(2)}, u32[]{:S(2)}) collective-permute-start(bf16[256,256]{1,0:T(8,128)(2,1)S(1)} %get-tuple-element.61), channel_id=1, source_target_pairs={{0,448},{448,384},{1,449},{449,385},{2,450},{450,386},{3,451},{451... | collective-permute-start | bytes 393224 | tf_op jit(solution)/shard_map/ppermute | solution.py:218
  219.9 0.0 collective-permute-done.10
  219.9 1.3 collective-permute-start.8
  221.2 0.7 collective-permute-done.11
  221.9 1.3 collective-permute-start.9
  223.2 1.5 collective-permute-done.12
  224.7 2.8 %collective-permute-done.13 = bf16[256,256]{1,0:T(8,128)(2,1)S(1)} collective-permute-done((bf16[256,256]{1,0:T(8,128)(2,1)S(1)}, bf16[256,256]{1,0:T(8,128)(2,1)S(1)}, u32[]{:S(2)}, u32[]{:S(2)}) %collective-permute-start.13) | collective-permute-done | bytes 131104 | tf_op jit(solution)/shard_map/ppermute | solution.py:207
  227.5 0.0 collective-permute-done.7
  227.5 0.0 collective-permute-done.8
  227.6 0.1 collective-permute-done.9
  227.7 0.1 select_bitcast_fusion.1
  227.7 0.7 maximum_bitcast_fusion
  (17 shorter events, 0.0 us)
Async XLA Ops:
  1.8 12.8 %copy-start.9 = (s32[2,1,64,8]{2,3,1,0:T(8,128)S(1)}, s32[2,1,64,8]{2,3,1,0:T(8,128)}, u32[]{:S(2)}) copy-start(s32[2,1,64,8]{2,3,1,0:T(8,128)} %param.14) | copy-start | bytes 12292
  1.8 30.7 %collective-permute-start = (bf16[272,256]{1,0:T(8,128)(2,1)S(1)}, bf16[272,256]{1,0:T(8,128)(2,1)S(1)}, u32[]{:S(2)}, u32[]{:S(2)}) collective-permute-start(bf16[272,256]{1,0:T(8,128)(2,1)S(1)} %concatenate.6), channel_id=1, source_target_pairs={{0,448},{64,0},{1,449},{65,1},{2,450},{66,2},{3,451},{67,3},{4,452... | collective-permute-start | bytes 417800 | tf_op jit(solution)/shard_map/ppermute | solution.py:201
  13.3 20.5 %collective-permute-start.1 = (bf16[272,256]{1,0:T(8,128)(2,1)S(1)}, bf16[272,256]{1,0:T(8,128)(2,1)S(1)}, u32[]{:S(2)}, u32[]{:S(2)}) collective-permute-start(bf16[272,256]{1,0:T(8,128)(2,1)S(1)} %concatenate.6), channel_id=1, source_target_pairs={{64,448},{128,0},{65,449},{129,1},{66,450},{130,2},{67,451},{131,3... | collective-permute-start | bytes 417800 | tf_op jit(solution)/shard_map/ppermute | solution.py:201
  17.4 17.7 %copy-start.10 = (s32[2,1,64,8]{2,3,1,0:T(8,128)S(1)}, s32[2,1,64,8]{2,3,1,0:T(8,128)}, u32[]{:S(2)}) copy-start(s32[2,1,64,8]{2,3,1,0:T(8,128)} %param.15) | copy-start | bytes 12292
  17.4 36.9 %all-to-all-start = ((bf16[64,8,256]{2,1,0:T(8,128)(2,1)}), bf16[64,8,256]{2,1,0:T(8,128)(2,1)S(1)}, u32[]{:S(2)}, u32[]{:S(2)}) async-start(bf16[64,8,256]{2,1,0:T(8,128)(2,1)} %bitcast.32), calls=%async_computation | async-start | bytes 524288 | tf_op jit(solution)/shard_map/all_to_all | solution.py:199
  28.6 10.8 %collective-permute-start.2 = (bf16[272,256]{1,0:T(8,128)(2,1)S(1)}, bf16[272,256]{1,0:T(8,128)(2,1)S(1)}, u32[]{:S(2)}, u32[]{:S(2)}) collective-permute-start(bf16[272,256]{1,0:T(8,128)(2,1)S(1)} %concatenate.6), channel_id=1, source_target_pairs={{128,448},{192,0},{129,449},{193,1},{130,450},{194,2},{131,451},{1... | collective-permute-start | bytes 417800 | tf_op jit(solution)/shard_map/ppermute | solution.py:201
  29.9 10.6 %collective-permute-start.3 = (bf16[272,256]{1,0:T(8,128)(2,1)S(1)}, bf16[272,256]{1,0:T(8,128)(2,1)S(1)}, u32[]{:S(2)}, u32[]{:S(2)}) collective-permute-start(bf16[272,256]{1,0:T(8,128)(2,1)S(1)} %concatenate.6), channel_id=1, source_target_pairs={{192,448},{256,0},{193,449},{257,1},{194,450},{258,2},{195,451},{2... | collective-permute-start | bytes 417800 | tf_op jit(solution)/shard_map/ppermute | solution.py:201
  31.2 16.1 %collective-permute-start.4 = (bf16[272,256]{1,0:T(8,128)(2,1)S(1)}, bf16[272,256]{1,0:T(8,128)(2,1)S(1)}, u32[]{:S(2)}, u32[]{:S(2)}) collective-permute-start(bf16[272,256]{1,0:T(8,128)(2,1)S(1)} %concatenate.6), channel_id=1, source_target_pairs={{256,448},{320,0},{257,449},{321,1},{258,450},{322,2},{259,451},{3... | collective-permute-start | bytes 417800 | tf_op jit(solution)/shard_map/ppermute | solution.py:201
  32.5 20.7 %collective-permute-start.5 = (bf16[272,256]{1,0:T(8,128)(2,1)S(1)}, bf16[272,256]{1,0:T(8,128)(2,1)S(1)}, u32[]{:S(2)}, u32[]{:S(2)}) collective-permute-start(bf16[272,256]{1,0:T(8,128)(2,1)S(1)} %concatenate.6), channel_id=1, source_target_pairs={{320,448},{384,0},{321,449},{385,1},{322,450},{386,2},{323,451},{3... | collective-permute-start | bytes 417800 | tf_op jit(solution)/shard_map/ppermute | solution.py:201
  33.8 19.4 %collective-permute-start.6 = (bf16[272,256]{1,0:T(8,128)(2,1)S(1)}, bf16[272,256]{1,0:T(8,128)(2,1)S(1)}, u32[]{:S(2)}, u32[]{:S(2)}) collective-permute-start(bf16[272,256]{1,0:T(8,128)(2,1)S(1)} %concatenate.6), channel_id=1, source_target_pairs={{384,448},{448,0},{385,449},{449,1},{386,450},{450,2},{387,451},{4... | collective-permute-start | bytes 417800 | tf_op jit(solution)/shard_map/ppermute | solution.py:201
  35.1 0.7 copy-start.11
  54.3 0.7 copy-start.2
  205.9 2.5 %copy-start = (bf16[256,256]{1,0:T(8,128)(2,1)S(1)}, bf16[256,256]{1,0:T(8,128)(2,1)}, u32[]{:S(2)}) copy-start(bf16[256,256]{1,0:T(8,128)(2,1)} %get-tuple-element.31.hidden_ref) | copy-start | bytes 393220
  205.9 2.5 %copy-start.3 = (bf16[256,256]{1,0:T(8,128)(2,1)S(1)}, bf16[256,256]{1,0:T(8,128)(2,1)}, u32[]{:S(2)}) copy-start(bf16[256,256]{1,0:T(8,128)(2,1)} %get-tuple-element.33.hidden_ref) | copy-start | bytes 393220
  205.9 2.5 %copy-start.4 = (bf16[256,256]{1,0:T(8,128)(2,1)S(1)}, bf16[256,256]{1,0:T(8,128)(2,1)}, u32[]{:S(2)}) copy-start(bf16[256,256]{1,0:T(8,128)(2,1)} %get-tuple-element.35.hidden_ref) | copy-start | bytes 393220
  205.9 2.5 %copy-start.5 = (bf16[256,256]{1,0:T(8,128)(2,1)S(1)}, bf16[256,256]{1,0:T(8,128)(2,1)}, u32[]{:S(2)}) copy-start(bf16[256,256]{1,0:T(8,128)(2,1)} %get-tuple-element.37.hidden_ref) | copy-start | bytes 393220
  205.9 2.5 %copy-start.6 = (bf16[256,256]{1,0:T(8,128)(2,1)S(1)}, bf16[256,256]{1,0:T(8,128)(2,1)}, u32[]{:S(2)}) copy-start(bf16[256,256]{1,0:T(8,128)(2,1)} %get-tuple-element.39.hidden_ref) | copy-start | bytes 393220
  205.9 2.5 %copy-start.7 = (bf16[256,256]{1,0:T(8,128)(2,1)S(1)}, bf16[256,256]{1,0:T(8,128)(2,1)}, u32[]{:S(2)}) copy-start(bf16[256,256]{1,0:T(8,128)(2,1)} %get-tuple-element.41.hidden_ref) | copy-start | bytes 393220
  205.9 2.5 %copy-start.8 = (bf16[256,256]{1,0:T(8,128)(2,1)S(1)}, bf16[256,256]{1,0:T(8,128)(2,1)}, u32[]{:S(2)}) copy-start(bf16[256,256]{1,0:T(8,128)(2,1)} %get-tuple-element.43.hidden_ref) | copy-start | bytes 393220
  208.4 19.2 %copy-start.1 = (bf16[256,256]{1,0:T(8,128)(2,1)S(1)}, bf16[256,256]{1,0:T(8,128)(2,1)}, u32[]{:S(2)}) copy-start(bf16[256,256]{1,0:T(8,128)(2,1)} %last_layer.1) | copy-start | bytes 393220
  209.5 10.4 %collective-permute-start.10 = (bf16[256,256]{1,0:T(8,128)(2,1)S(1)}, bf16[256,256]{1,0:T(8,128)(2,1)S(1)}, u32[]{:S(2)}, u32[]{:S(2)}) collective-permute-start(bf16[256,256]{1,0:T(8,128)(2,1)S(1)} %get-tuple-element.58), channel_id=1, source_target_pairs={{0,256},{448,192},{1,257},{449,193},{2,258},{450,194},{3,259},{451... | collective-permute-start | bytes 393224 | tf_op jit(solution)/shard_map/ppermute | solution.py:207
  210.8 11.1 %collective-permute-start.11 = (bf16[256,256]{1,0:T(8,128)(2,1)S(1)}, bf16[256,256]{1,0:T(8,128)(2,1)S(1)}, u32[]{:S(2)}, u32[]{:S(2)}) collective-permute-start(bf16[256,256]{1,0:T(8,128)(2,1)S(1)} %get-tuple-element.57), channel_id=1, source_target_pairs={{0,192},{448,128},{1,193},{449,129},{2,194},{450,130},{3,195},{451... | collective-permute-start | bytes 393224 | tf_op jit(solution)/shard_map/ppermute | solution.py:207
  212.1 12.6 %collective-permute-start.12 = (bf16[256,256]{1,0:T(8,128)(2,1)S(1)}, bf16[256,256]{1,0:T(8,128)(2,1)S(1)}, u32[]{:S(2)}, u32[]{:S(2)}) collective-permute-start(bf16[256,256]{1,0:T(8,128)(2,1)S(1)} %get-tuple-element.56), channel_id=1, source_target_pairs={{0,128},{448,64},{1,129},{449,65},{2,130},{450,66},{3,131},{451,67... | collective-permute-start | bytes 393224 | tf_op jit(solution)/shard_map/ppermute | solution.py:207
  213.4 14.1 %collective-permute-start.13 = (bf16[256,256]{1,0:T(8,128)(2,1)S(1)}, bf16[256,256]{1,0:T(8,128)(2,1)S(1)}, u32[]{:S(2)}, u32[]{:S(2)}) collective-permute-start(bf16[256,256]{1,0:T(8,128)(2,1)S(1)} %get-tuple-element.55), channel_id=1, source_target_pairs={{0,64},{448,0},{1,65},{449,1},{2,66},{450,2},{3,67},{451,3},{4,68}... | collective-permute-start | bytes 393224 | tf_op jit(solution)/shard_map/ppermute | solution.py:207
  215.3 12.2 %collective-permute-start.7 = (bf16[256,256]{1,0:T(8,128)(2,1)S(1)}, bf16[256,256]{1,0:T(8,128)(2,1)S(1)}, u32[]{:S(2)}, u32[]{:S(2)}) collective-permute-start(bf16[256,256]{1,0:T(8,128)(2,1)S(1)} %get-tuple-element.61), channel_id=1, source_target_pairs={{0,448},{448,384},{1,449},{449,385},{2,450},{450,386},{3,451},{451... | collective-permute-start | bytes 393224 | tf_op jit(solution)/shard_map/ppermute | solution.py:218
  219.9 7.6 %collective-permute-start.8 = (bf16[256,256]{1,0:T(8,128)(2,1)S(1)}, bf16[256,256]{1,0:T(8,128)(2,1)S(1)}, u32[]{:S(2)}, u32[]{:S(2)}) collective-permute-start(bf16[256,256]{1,0:T(8,128)(2,1)S(1)} %get-tuple-element.60), channel_id=1, source_target_pairs={{0,384},{448,320},{1,385},{449,321},{2,386},{450,322},{3,387},{451... | collective-permute-start | bytes 393224 | tf_op jit(solution)/shard_map/ppermute | solution.py:207
  221.9 5.7 %collective-permute-start.9 = (bf16[256,256]{1,0:T(8,128)(2,1)S(1)}, bf16[256,256]{1,0:T(8,128)(2,1)S(1)}, u32[]{:S(2)}, u32[]{:S(2)}) collective-permute-start(bf16[256,256]{1,0:T(8,128)(2,1)S(1)} %get-tuple-element.59), channel_id=1, source_target_pairs={{0,320},{448,256},{1,321},{449,257},{2,322},{450,258},{3,323},{451... | collective-permute-start | bytes 393224 | tf_op jit(solution)/shard_map/ppermute | solution.py:207

commit v2 on v1

v2 whole, which is shorter than its diff:
```python
import functools

import jax
import jax.numpy as jnp
from jax import lax
from jax.experimental import pallas as pl
from jax.experimental.pallas import tpu as pltpu
from jax.sharding import PartitionSpec as P

PACK_ROWS = 16
KERNEL_VMEM = 8 * 2**20
VMEM = pl.BlockSpec(memory_space=pltpu.VMEM)
SMEM = pl.BlockSpec(memory_space=pltpu.SMEM)
ANYWHERE = pl.BlockSpec(memory_space=pl.ANY)
PARAMS = pltpu.CompilerParams(vmem_limit_bytes=KERNEL_VMEM)
WIDE_PARAMS = pltpu.CompilerParams(vmem_limit_bytes=56 * 2**20)
CHUNKS = 4


def slot_column(table):
    slots, count = table.shape
    rows = count * slots
    expand = (
        lax.broadcasted_iota(jnp.int32, (rows, count), 0) // slots
        == lax.broadcasted_iota(jnp.int32, (rows, count), 1)
    ).astype(jnp.bfloat16)
    spread = lax.dot_general(
        expand,
        table.astype(jnp.float32).astype(jnp.bfloat16),
        (((1,), (1,)), ((), ())),
        preferred_element_type=jnp.float32,
    )
    here = lax.broadcasted_iota(jnp.int32, (rows, slots), 0) % slots == lax.broadcasted_iota(
        jnp.int32, (rows, slots), 1
    )
    return jnp.sum(jnp.where(here, spread, 0.0), axis=1, keepdims=True)


def one_hot_rows(column, width):
    ids = lax.broadcasted_iota(jnp.int32, (column.shape[0], width), 1)
    return (column.astype(jnp.int32) == ids).astype(jnp.float32).astype(jnp.bfloat16)


def gather_out(select_ref, state, outgoing_ref, staged_ref, sems):
    size = select_ref.shape[0] // CHUNKS
    copies = []
    for chunk in range(CHUNKS):
        at = pl.ds(chunk * size, size)
        staged_ref[at, :] = jnp.dot(
            select_ref[at, :], state, preferred_element_type=jnp.float32
        ).astype(jnp.bfloat16)
        copies.append(pltpu.make_async_copy(staged_ref.at[at], outgoing_ref.at[at], sems.at[chunk]))
        copies[-1].start()
    for copy in copies:
        copy.wait()


def gather_scratch(slots, width):
    return [pltpu.VMEM((slots, width), jnp.bfloat16), pltpu.SemaphoreType.DMA((CHUNKS,))]


def first_kernel(span_ref, features_ref, send_ref, outgoing_ref, select_ref, staged_ref, sems):
    select_ref[...] = one_hot_rows(slot_column(send_ref[0, 0]), features_ref.shape[1])
    gather_out(select_ref, features_ref[0], outgoing_ref, staged_ref, sems)


def first_gather(span, features, send_rows):
    _, rows, width = features.shape
    slots, peers = send_rows.shape[2:]
    return pl.pallas_call(
        first_kernel,
        grid_spec=pltpu.PrefetchScalarGridSpec(
            num_scalar_prefetch=1,
            grid=(1,),
            in_specs=[
                pl.BlockSpec((1, rows, width), lambda i, s: (s[0], 0, 0)),
                pl.BlockSpec((1, 1, slots, peers), lambda i, s: (s[0], 0, 0, 0)),
            ],
            out_specs=ANYWHERE,
            scratch_shapes=[pltpu.VMEM((peers * slots, rows), jnp.bfloat16)]
            + gather_scratch(peers * slots, width),
        ),
        out_shape=jax.ShapeDtypeStruct((peers * slots, width), jnp.bfloat16),
        compiler_params=WIDE_PARAMS,
        name="first_gather",
    )(span, features, send_rows)


def tables_kernel(
    span_ref,
    col_ref,
    adj_ref,
    dest_ref,
    send_ref,
    features_ref,
    after_ref,
    near_ref,
    scatter_ref,
    inverse_ref,
    select_ref,
    hidden_ref,
):
    hidden_ref[...] = features_ref[0]
    select_ref[...] = one_hot_rows(slot_column(send_ref[0, 0]), hidden_ref.shape[0])
    _, blocks, tiles, side, _ = adj_ref.shape
    span = span_ref[0]
    rows = blocks * side
    scatter = one_hot_rows(slot_column(dest_ref[0, 0]), rows).astype(jnp.float32).T
    scatter_ref[...] = scatter.astype(jnp.bfloat16)
    degree = 1.0 + jnp.sum(scatter, axis=1, keepdims=True)
    for r in range(blocks):
        below = slice(r * side, (r + 1) * side)
        local_degree = jnp.zeros((side, 1), jnp.float32)
        for b in range(blocks):
            total = jnp.zeros((side, side), jnp.int32)
            for k in range(tiles):
                hit = col_ref[span, r, k] == b
                total += jnp.where(hit, adj_ref[0, r, k], 0)
            dense = total.astype(jnp.float32)
            local_degree += jnp.sum(dense, axis=1, keepdims=True)
            if b == r:
                dense += (
                    lax.broadcasted_iota(jnp.int32, (side, side), 0)
                    == lax.broadcasted_iota(jnp.int32, (side, side), 1)
                ).astype(jnp.float32)
            near_ref[below, b * side : (b + 1) * side] = dense.astype(jnp.bfloat16)
        inverse_ref[below, :] = jnp.broadcast_to(
            1.0 / (degree[below] + local_degree), (side, inverse_ref.shape[1])
        )


def build_tables(span, tile_col, tile_adj, recv_dst, send_rows, features, after):
    _, blocks, tiles, side, _ = tile_adj.shape
    _, rows, width = features.shape
    slots, peers = recv_dst.shape[2:]
    shapes = [
        ((rows, rows), jnp.bfloat16),
        ((rows, peers * slots), jnp.bfloat16),
        ((rows, side), jnp.float32),
        ((peers * slots, rows), jnp.bfloat16),
        ((rows, width), jnp.bfloat16),
    ]
    return pl.pallas_call(
        tables_kernel,
        grid_spec=pltpu.PrefetchScalarGridSpec(
            num_scalar_prefetch=1,
            grid=(1,),
            in_specs=[
                SMEM,
                pl.BlockSpec((1, blocks, tiles, side, side), lambda i, s: (s[0], 0, 0, 0, 0)),
                pl.BlockSpec((1, 1, slots, peers), lambda i, s: (s[0], 0, 0, 0)),
                pl.BlockSpec((1, 1, slots, peers), lambda i, s: (s[0], 0, 0, 0)),
                pl.BlockSpec((1, rows, width), lambda i, s: (s[0], 0, 0)),
                ANYWHERE,
            ],
            out_specs=[pl.BlockSpec(shape, lambda i, s: (0, 0)) for shape, _ in shapes],
        ),
        out_shape=[jax.ShapeDtypeStruct(shape, dtype) for shape, dtype in shapes],
        compiler_params=PARAMS,
        name="build_tables",
    )(span, tile_col, tile_adj, recv_dst, send_rows, features, after)


def pack_kernel(weight_ref, bias_ref, gain_ref, after_ref, pack_ref):
    width = weight_ref.shape[-1]
    pack_ref[0:width, :] = weight_ref[0]
    row = lax.broadcasted_iota(jnp.int32, (PACK_ROWS, width), 0)
    small = jnp.zeros((PACK_ROWS, width), jnp.float32)
    for at, ref in ((0, bias_ref), (2, gain_ref)):
        vector = ref[...]
        high = vector.astype(jnp.bfloat16).astype(jnp.float32)
        small = jnp.where(row == at, high, small)
        small = jnp.where(row == at + 1, vector - high, small)
    pack_ref[width : width + PACK_ROWS, :] = small.astype(jnp.bfloat16)


def pack_layer(weight, bias, gain, after):
    width = weight.shape[-1]
    return pl.pallas_call(
        pack_kernel,
        out_shape=jax.ShapeDtypeStruct((width + PACK_ROWS, width), jnp.bfloat16),
        in_specs=[VMEM] * 3 + [ANYWHERE],
        out_specs=VMEM,
        compiler_params=WIDE_PARAMS,
        name="pack_layer",
    )(weight, bias, gain, after)


def layer_kernel(
    step,
    layers,
    plane_ref,
    hidden_ref,
    arrived_ref,
    near_ref,
    scatter_ref,
    inverse_ref,
    select_ref,
    early_ref,
    late_ref,
    after_ref,
    state_ref,
    *refs,
):
    rows, width = hidden_ref.shape
    plane = plane_ref[0]
    begin = jnp.where(plane == 0, 0, layers - 1 - plane)
    pack = jnp.where(plane == 0, early_ref[...], late_ref[...])
    hidden = hidden_ref[...]
    total = jnp.dot(near_ref[...], hidden, preferred_element_type=jnp.float32)
    total += jnp.dot(scatter_ref[...], arrived_ref[...], preferred_element_type=jnp.float32)
    inverse = jnp.concatenate([inverse_ref[...]] * (width // inverse_ref.shape[1]), axis=1)
    mean = (total * inverse).astype(jnp.bfloat16)
    vectors = pack[width : width + PACK_ROWS, :].astype(jnp.float32)
    bias = vectors[0:1] + vectors[1:2]
    gain = vectors[2:3] + vectors[3:4]
    projected = jnp.dot(mean, pack[0:width, :], preferred_element_type=jnp.float32) + bias
    summed = hidden.astype(jnp.float32) + jnp.maximum(projected, 0.0)
    scale = lax.rsqrt(jnp.mean(summed * summed, axis=1, keepdims=True) + 1e-05)
    state = (summed * scale * gain).astype(jnp.bfloat16)
    if step < layers - 1:
        state = jnp.where(step >= begin, state, hidden)
    state_ref[...] = state
    if step < layers - 1:
        carried_ref, outgoing_ref, staged_ref, sems = refs
        carried_ref[...] = late_ref[...]
        gather_out(select_ref, state, outgoing_ref, staged_ref, sems)


def run_layer(step, layers, plane, hidden, arrived, tables, early, late, after):
    slots, width = arrived.shape
    outs = [hidden, late, arrived]
    out_specs = [VMEM, VMEM, ANYWHERE]
    scratch = gather_scratch(slots, width)
    if step == layers - 1:
        outs, out_specs, scratch = outs[:1], out_specs[:1], []
    return pl.pallas_call(
        functools.partial(layer_kernel, step, layers),
        out_shape=[jax.ShapeDtypeStruct(out.shape, jnp.bfloat16) for out in outs],
        in_specs=[SMEM] + [VMEM] * 8 + [ANYWHERE],
        out_specs=out_specs,
        scratch_shapes=scratch,
        compiler_params=PARAMS,
        name="layer",
    )(plane, hidden, arrived, *tables, early, late, after)


def local(features, weight, bias, gain, tile_col, tile_adj, send_rows, recv_dst):
    layers = lax.axis_size("layer")
    index = lax.axis_index("layer")
    peers, slots = send_rows.shape[2:]
    width = features.shape[-1]
    plane = index.reshape(1)
    span = plane % 2
    send_rows = send_rows.transpose(0, 1, 3, 2)
    recv_dst = recv_dst.transpose(0, 1, 3, 2)
    down = [(z, (z - 1) % layers) for z in range(layers)]

    outgoing = first_gather(span, features, send_rows)
    own_pack = pack_layer(weight, bias, gain, outgoing)
    *tables, hidden = build_tables(span, tile_col, tile_adj, recv_dst, send_rows, features, outgoing)
    early = carried = own_pack
    for step in range(layers):
        arrived = lax.all_to_all(outgoing.reshape(peers, slots, width), "dom", 0, 0, tiled=True)
        arrived = arrived.reshape(peers * slots, width)
        if step < layers - 1:
            late = after = lax.ppermute(carried, "layer", down)
        else:
            late = own_pack
            after = from_above = lax.ppermute(hidden, "layer", down[1:])
        hidden, *more = run_layer(step, layers, plane, hidden, arrived, tables, early, late, after)
        if more:
            carried, outgoing = more
            early = carried
        if step == 0:
            first_state = hidden
    last_state = lax.ppermute(hidden, "layer", down[:1])
    own = jnp.where(index == 0, first_state, hidden)
    other = jnp.where(index == layers - 1, last_state, from_above)
    even = index % 2 == 0
    return jnp.stack([jnp.where(even, own, other), jnp.where(even, other, own)])[None]


def solution(mesh):
    in_specs = (
        P(None, "dom", None),
        P("layer", None, None),
        P("layer", None),
        P("layer", None),
        P(None, "dom", None),
        P(None, "dom", None, None, None),
        P(None, "dom", None, None),
        P(None, "dom", None, None),
    )
    out_specs = P("layer", None, "dom", None)
    return jax.shard_map(local, mesh=mesh, in_specs=in_specs, out_specs=out_specs, check_vma=False)
```

time: 230 us -> 188 us (0.82)
  blocking collectives: 131 us -> 0 us
  starting transfers between devices: 43.4 us -> 115 us
  waiting for transfers between devices: 19 us -> 54.9 us
  Pallas kernels: 26.8 us -> 15.7 us
  local copies, waits for them, and re-layouts: 3.93 us -> 0.04 us
  other arithmetic: 3.57 us -> 0.76 us
    all_to_all x7 -> x0, blocking collectives: 131 us -> none  [local(): lax.all_to_all(outgoing.reshape(peers, slots, width), 'dom', 0, 0, tiled=...]
    all_to_all x1 -> x8, starting transfers between devices: 11.2 us -> 65.8 us  [local(): lax.all_to_all(outgoing.reshape(peers, slots, width), 'dom', 0, 0, tiled=...]
    all_to_all x1 -> x8, waiting for transfers between devices: 0.01 us -> 30.2 us  [local(): lax.all_to_all(outgoing.reshape(peers, slots, width), 'dom', 0, 0, tiled=...]
    ppermute x14 -> x9, starting transfers between devices: 32.2 us -> 49.1 us  [the longest x7 42.5 us: local(): late = after = lax.ppermute(carried, 'layer', down)]
    pallas_call x8 -> x9, Pallas kernels: 21.9 us -> 12.5 us  [the longest x8 10.9 us: run_layer(): pl.pallas_call(functools.partial(layer_kernel, step, layers), out_shape=[...]
    ppermute x14 -> x9, waiting for transfers between devices: 19 us -> 24.7 us  [the longest x7 17.1 us: local(): late = after = lax.ppermute(carried, 'layer', down)]
  transfers between devices with their start and end apart: 15 -> 17, of which waited for: 7 -> 16; matrix products, arithmetic and copies ran while one was open for 1% -> 0% of each run, Pallas kernels for 2% -> 1%
where the time goes in v2:
time: 188 us; the launch traced here: 187 us
  starting transfers between devices  115 us (61%)
  waiting for transfers between devices  54.9 us (29%)
  Pallas kernels  15.7 us (8%)
    all_to_all x8, starting transfers between devices, local(): lax.all_to_all(outgoing.reshape(peers, slots, width), 'dom', 0, 0, tiled=...  65.8 us
    ppermute x7, starting transfers between devices, local(): late = after = lax.ppermute(carried, 'layer', down)  42.5 us
    all_to_all x8, waiting for transfers between devices, local(): lax.all_to_all(outgoing.reshape(peers, slots, width), 'dom', 0, 0, tiled=...  30.2 us
    ppermute x7, waiting for transfers between devices, local(): late = after = lax.ppermute(carried, 'layer', down)  17.1 us
    pallas_call x8, Pallas kernels, run_layer(): pl.pallas_call(functools.partial(layer_kernel, step, layers), out_shape=[...  10.9 us
    ppermute x1, starting transfers between devices, local(): last_state = lax.ppermute(hidden, 'layer', down[:1])  5.32 us
    ppermute x1, waiting for transfers between devices, local(): after = from_above = lax.ppermute(hidden, 'layer', down[1:])  5.21 us
  transfers between devices with their start and end apart: 17, of which 16 were waited for; matrix products, arithmetic and copies ran while one was open for 0% of the time, Pallas kernels for 1%

profile of v2, /device:TPU:1, one launch (start us, length us, event | category | flops | bytes accessed | tf_op | source)
XLA Modules:
  0.0 186.7 jit_solution(10673443527213221376)
XLA Ops:
  0.0 0.0 copy-start.2
  0.0 2.1 %first_gather.1.after_ref = bf16[512,256]{1,0:T(8,128)(2,1)} custom-call(s32[1]{0:T(128)S(6)} %select_n.40.span_ref, bf16[2,256,256]{2,1,0:T(8,128)(2,1)} %features_ref.3, s32[2,1,8,64]{3,2,1,0:T(8,128)} %bitcast.34), custom_call_target="tpu_custom_call" | custom-call | tf_op jit(solution)/shard_map/first_gather/pallas_call | solution.py:70
  2.1 0.0 copy-start.5
  2.1 11.6 %all-to-all-start = ((bf16[64,8,256]{2,1,0:T(8,128)(2,1)}), bf16[64,8,256]{2,1,0:T(8,128)(2,1)S(1)}, u32[]{:S(2)}, u32[]{:S(2)}) async-start(bf16[64,8,256]{2,1,0:T(8,128)(2,1)} %bitcast.25), calls=%async_computation | async-start | bytes 524288 | tf_op jit(solution)/shard_map/all_to_all | solution.py:264
  13.8 0.0 copy-start
  13.8 0.0 copy-start.3
  13.8 0.0 copy-start.4
  13.8 0.0 copy-start.6
  13.8 1.6 pack_layer.1.early_ref.late_ref
  15.5 10.7 %collective-permute-start = (bf16[272,256]{1,0:T(8,128)(2,1)}, bf16[272,256]{1,0:T(8,128)(2,1)S(1)}, u32[]{:S(2)}, u32[]{:S(2)}) collective-permute-start(bf16[272,256]{1,0:T(8,128)(2,1)} %pack_layer.1.early_ref.late_ref), channel_id=1, source_target_pairs={{0,448},{64,0},{128,64},{192,128},{256,192},{320,256},{384,320},{4... | collective-permute-start | bytes 417800 | tf_op jit(solution)/shard_map/ppermute | solution.py:267
  26.1 0.0 copy-done.2
  26.1 0.0 copy-done.5
  26.1 0.0 copy-done
  26.1 0.0 copy-done.3
  26.2 0.0 copy-done.4
  26.2 0.0 copy-done.6
  26.2 0.0 copy-start.1
  26.2 1.1 build_tables.1
  27.3 1.7 collective-permute-done.late_ref.after_ref
  29.0 0.0 all-to-all-done
  29.0 0.0 copy-done.1
  29.0 1.5 layer.8
  30.5 11.3 %all-to-all-start.1 = ((bf16[64,8,256]{2,1,0:T(8,128)(2,1)}), bf16[64,8,256]{2,1,0:T(8,128)(2,1)S(1)}, u32[]{:S(2)}, u32[]{:S(2)}) async-start(bf16[64,8,256]{2,1,0:T(8,128)(2,1)} %bitcast.5), calls=%async_computation.1 | async-start | bytes 524288 | tf_op jit(solution)/shard_map/all_to_all | solution.py:264
  41.8 5.2 %collective-permute-start.1 = (bf16[272,256]{1,0:T(8,128)(2,1)S(1)}, bf16[272,256]{1,0:T(8,128)(2,1)S(1)}, u32[]{:S(2)}, u32[]{:S(2)}) collective-permute-start(bf16[272,256]{1,0:T(8,128)(2,1)S(1)} %get-tuple-element.38.early_ref), channel_id=1, source_target_pairs={{0,448},{64,0},{128,64},{192,128},{256,192},{320,256},{384,320},{4... | collective-permute-start | bytes 417800 | tf_op jit(solution)/shard_map/ppermute | solution.py:267
  47.0 2.6 %collective-permute-done.1.late_ref.after_ref = bf16[272,256]{1,0:T(8,128)(2,1)S(1)} collective-permute-done((bf16[272,256]{1,0:T(8,128)(2,1)S(1)}, bf16[272,256]{1,0:T(8,128)(2,1)S(1)}, u32[]{:S(2)}, u32[]{:S(2)}) %collective-permute-start.1) | collective-permute-done | bytes 139296 | tf_op jit(solution)/shard_map/ppermute | solution.py:267
  49.6 4.2 %all-to-all-done.1 = bf16[64,8,256]{2,1,0:T(8,128)(2,1)S(1)} async-done(((bf16[64,8,256]{2,1,0:T(8,128)(2,1)}), bf16[64,8,256]{2,1,0:T(8,128)(2,1)S(1)}, u32[]{:S(2)}, u32[]{:S(2)}) %all-to-all-start.1) | async-done | bytes 262176 | tf_op jit(solution)/shard_map/all_to_all | solution.py:264
  53.8 1.5 layer.9
  55.3 7.1 %all-to-all-start.2 = ((bf16[64,8,256]{2,1,0:T(8,128)(2,1)}), bf16[64,8,256]{2,1,0:T(8,128)(2,1)S(1)}, u32[]{:S(2)}, u32[]{:S(2)}) async-start(bf16[64,8,256]{2,1,0:T(8,128)(2,1)} %bitcast.7), calls=%async_computation.2 | async-start | bytes 524288 | tf_op jit(solution)/shard_map/all_to_all | solution.py:264
  62.3 5.3 %collective-permute-start.2 = (bf16[272,256]{1,0:T(8,128)(2,1)S(1)}, bf16[272,256]{1,0:T(8,128)(2,1)S(1)}, u32[]{:S(2)}, u32[]{:S(2)}) collective-permute-start(bf16[272,256]{1,0:T(8,128)(2,1)S(1)} %get-tuple-element.41.early_ref), channel_id=1, source_target_pairs={{0,448},{64,0},{128,64},{192,128},{256,192},{320,256},{384,320},{4... | collective-permute-start | bytes 417800 | tf_op jit(solution)/shard_map/ppermute | solution.py:267
  67.7 2.6 %collective-permute-done.2.late_ref.after_ref = bf16[272,256]{1,0:T(8,128)(2,1)S(1)} collective-permute-done((bf16[272,256]{1,0:T(8,128)(2,1)S(1)}, bf16[272,256]{1,0:T(8,128)(2,1)S(1)}, u32[]{:S(2)}, u32[]{:S(2)}) %collective-permute-start.2) | collective-permute-done | bytes 139296 | tf_op jit(solution)/shard_map/ppermute | solution.py:267
  70.2 4.1 %all-to-all-done.2 = bf16[64,8,256]{2,1,0:T(8,128)(2,1)S(1)} async-done(((bf16[64,8,256]{2,1,0:T(8,128)(2,1)}), bf16[64,8,256]{2,1,0:T(8,128)(2,1)S(1)}, u32[]{:S(2)}, u32[]{:S(2)}) %all-to-all-start.2) | async-done | bytes 262176 | tf_op jit(solution)/shard_map/all_to_all | solution.py:264
  74.3 1.5 layer.10
  75.8 7.2 %all-to-all-start.3 = ((bf16[64,8,256]{2,1,0:T(8,128)(2,1)}), bf16[64,8,256]{2,1,0:T(8,128)(2,1)S(1)}, u32[]{:S(2)}, u32[]{:S(2)}) async-start(bf16[64,8,256]{2,1,0:T(8,128)(2,1)} %bitcast.9), calls=%async_computation.3 | async-start | bytes 524288 | tf_op jit(solution)/shard_map/all_to_all | solution.py:264
  83.0 5.3 %collective-permute-start.3 = (bf16[272,256]{1,0:T(8,128)(2,1)S(1)}, bf16[272,256]{1,0:T(8,128)(2,1)S(1)}, u32[]{:S(2)}, u32[]{:S(2)}) collective-permute-start(bf16[272,256]{1,0:T(8,128)(2,1)S(1)} %get-tuple-element.44.early_ref), channel_id=1, source_target_pairs={{0,448},{64,0},{128,64},{192,128},{256,192},{320,256},{384,320},{4... | collective-permute-start | bytes 417800 | tf_op jit(solution)/shard_map/ppermute | solution.py:267
  88.3 2.6 %collective-permute-done.3.late_ref.after_ref = bf16[272,256]{1,0:T(8,128)(2,1)S(1)} collective-permute-done((bf16[272,256]{1,0:T(8,128)(2,1)S(1)}, bf16[272,256]{1,0:T(8,128)(2,1)S(1)}, u32[]{:S(2)}, u32[]{:S(2)}) %collective-permute-start.3) | collective-permute-done | bytes 139296 | tf_op jit(solution)/shard_map/ppermute | solution.py:267
  90.9 4.1 %all-to-all-done.3 = bf16[64,8,256]{2,1,0:T(8,128)(2,1)S(1)} async-done(((bf16[64,8,256]{2,1,0:T(8,128)(2,1)}), bf16[64,8,256]{2,1,0:T(8,128)(2,1)S(1)}, u32[]{:S(2)}, u32[]{:S(2)}) %all-to-all-start.3) | async-done | bytes 262176 | tf_op jit(solution)/shard_map/all_to_all | solution.py:264
  95.0 1.5 layer.11
  96.5 7.2 %all-to-all-start.4 = ((bf16[64,8,256]{2,1,0:T(8,128)(2,1)}), bf16[64,8,256]{2,1,0:T(8,128)(2,1)S(1)}, u32[]{:S(2)}, u32[]{:S(2)}) async-start(bf16[64,8,256]{2,1,0:T(8,128)(2,1)} %bitcast.11), calls=%async_computation.4 | async-start | bytes 524288 | tf_op jit(solution)/shard_map/all_to_all | solution.py:264
  103.7 5.3 %collective-permute-start.4 = (bf16[272,256]{1,0:T(8,128)(2,1)S(1)}, bf16[272,256]{1,0:T(8,128)(2,1)S(1)}, u32[]{:S(2)}, u32[]{:S(2)}) collective-permute-start(bf16[272,256]{1,0:T(8,128)(2,1)S(1)} %get-tuple-element.47.early_ref), channel_id=1, source_target_pairs={{0,448},{64,0},{128,64},{192,128},{256,192},{320,256},{384,320},{4... | collective-permute-start | bytes 417800 | tf_op jit(solution)/shard_map/ppermute | solution.py:267
  109.0 2.6 %collective-permute-done.4.late_ref.after_ref = bf16[272,256]{1,0:T(8,128)(2,1)S(1)} collective-permute-done((bf16[272,256]{1,0:T(8,128)(2,1)S(1)}, bf16[272,256]{1,0:T(8,128)(2,1)S(1)}, u32[]{:S(2)}, u32[]{:S(2)}) %collective-permute-start.4) | collective-permute-done | bytes 139296 | tf_op jit(solution)/shard_map/ppermute | solution.py:267
  111.6 4.1 %all-to-all-done.4 = bf16[64,8,256]{2,1,0:T(8,128)(2,1)S(1)} async-done(((bf16[64,8,256]{2,1,0:T(8,128)(2,1)}), bf16[64,8,256]{2,1,0:T(8,128)(2,1)S(1)}, u32[]{:S(2)}, u32[]{:S(2)}) %all-to-all-start.4) | async-done | bytes 262176 | tf_op jit(solution)/shard_map/all_to_all | solution.py:264
  115.7 1.5 layer.12
  117.2 7.2 %all-to-all-start.5 = ((bf16[64,8,256]{2,1,0:T(8,128)(2,1)}), bf16[64,8,256]{2,1,0:T(8,128)(2,1)S(1)}, u32[]{:S(2)}, u32[]{:S(2)}) async-start(bf16[64,8,256]{2,1,0:T(8,128)(2,1)} %bitcast.13), calls=%async_computation.5 | async-start | bytes 524288 | tf_op jit(solution)/shard_map/all_to_all | solution.py:264
  124.3 5.3 %collective-permute-start.5 = (bf16[272,256]{1,0:T(8,128)(2,1)S(1)}, bf16[272,256]{1,0:T(8,128)(2,1)S(1)}, u32[]{:S(2)}, u32[]{:S(2)}) collective-permute-start(bf16[272,256]{1,0:T(8,128)(2,1)S(1)} %get-tuple-element.50.early_ref), channel_id=1, source_target_pairs={{0,448},{64,0},{128,64},{192,128},{256,192},{320,256},{384,320},{4... | collective-permute-start | bytes 417800 | tf_op jit(solution)/shard_map/ppermute | solution.py:267
  129.7 2.6 %collective-permute-done.5.late_ref.after_ref = bf16[272,256]{1,0:T(8,128)(2,1)S(1)} collective-permute-done((bf16[272,256]{1,0:T(8,128)(2,1)S(1)}, bf16[272,256]{1,0:T(8,128)(2,1)S(1)}, u32[]{:S(2)}, u32[]{:S(2)}) %collective-permute-start.5) | collective-permute-done | bytes 139296 | tf_op jit(solution)/shard_map/ppermute | solution.py:267
  132.2 4.1 %all-to-all-done.5 = bf16[64,8,256]{2,1,0:T(8,128)(2,1)S(1)} async-done(((bf16[64,8,256]{2,1,0:T(8,128)(2,1)}), bf16[64,8,256]{2,1,0:T(8,128)(2,1)S(1)}, u32[]{:S(2)}, u32[]{:S(2)}) %all-to-all-start.5) | async-done | bytes 262176 | tf_op jit(solution)/shard_map/all_to_all | solution.py:264
  136.3 1.5 layer.13
  137.8 7.2 %all-to-all-start.6 = ((bf16[64,8,256]{2,1,0:T(8,128)(2,1)}), bf16[64,8,256]{2,1,0:T(8,128)(2,1)S(1)}, u32[]{:S(2)}, u32[]{:S(2)}) async-start(bf16[64,8,256]{2,1,0:T(8,128)(2,1)} %bitcast.15), calls=%async_computation.6 | async-start | bytes 524288 | tf_op jit(solution)/shard_map/all_to_all | solution.py:264
  145.0 5.3 %collective-permute-start.6 = (bf16[272,256]{1,0:T(8,128)(2,1)S(1)}, bf16[272,256]{1,0:T(8,128)(2,1)S(1)}, u32[]{:S(2)}, u32[]{:S(2)}) collective-permute-start(bf16[272,256]{1,0:T(8,128)(2,1)S(1)} %get-tuple-element.53.early_ref), channel_id=1, source_target_pairs={{0,448},{64,0},{128,64},{192,128},{256,192},{320,256},{384,320},{4... | collective-permute-start | bytes 417800 | tf_op jit(solution)/shard_map/ppermute | solution.py:267
  150.3 2.6 %collective-permute-done.6.late_ref.after_ref = bf16[272,256]{1,0:T(8,128)(2,1)S(1)} collective-permute-done((bf16[272,256]{1,0:T(8,128)(2,1)S(1)}, bf16[272,256]{1,0:T(8,128)(2,1)S(1)}, u32[]{:S(2)}, u32[]{:S(2)}) %collective-permute-start.6) | collective-permute-done | bytes 139296 | tf_op jit(solution)/shard_map/ppermute | solution.py:267
  152.9 4.1 %all-to-all-done.6 = bf16[64,8,256]{2,1,0:T(8,128)(2,1)S(1)} async-done(((bf16[64,8,256]{2,1,0:T(8,128)(2,1)}), bf16[64,8,256]{2,1,0:T(8,128)(2,1)S(1)}, u32[]{:S(2)}, u32[]{:S(2)}) %all-to-all-start.6) | async-done | bytes 262176 | tf_op jit(solution)/shard_map/all_to_all | solution.py:264
  157.0 1.5 layer.14
  158.5 7.2 %all-to-all-start.7 = ((bf16[64,8,256]{2,1,0:T(8,128)(2,1)}), bf16[64,8,256]{2,1,0:T(8,128)(2,1)S(1)}, u32[]{:S(2)}, u32[]{:S(2)}) async-start(bf16[64,8,256]{2,1,0:T(8,128)(2,1)} %bitcast.17), calls=%async_computation.7 | async-start | bytes 524288 | tf_op jit(solution)/shard_map/all_to_all | solution.py:264
  165.7 1.3 collective-permute-start.7
  167.0 5.2 %collective-permute-done.7.after_ref = bf16[256,256]{1,0:T(8,128)(2,1)S(1)} collective-permute-done((bf16[256,256]{1,0:T(8,128)(2,1)S(1)}, bf16[256,256]{1,0:T(8,128)(2,1)S(1)}, u32[]{:S(2)}, u32[]{:S(2)}) %collective-permute-start.7) | collective-permute-done | bytes 131104 | tf_op jit(solution)/shard_map/ppermute | solution.py:270
  172.2 5.5 %all-to-all-done.7 = bf16[64,8,256]{2,1,0:T(8,128)(2,1)S(1)} async-done(((bf16[64,8,256]{2,1,0:T(8,128)(2,1)}), bf16[64,8,256]{2,1,0:T(8,128)(2,1)S(1)}, u32[]{:S(2)}, u32[]{:S(2)}) %all-to-all-start.7) | async-done | bytes 262176 | tf_op jit(solution)/shard_map/all_to_all | solution.py:264
  177.7 0.5 layer.15
  178.2 5.3 %collective-permute-start.8 = (bf16[256,256]{1,0:T(8,128)(2,1)S(1)}, bf16[256,256]{1,0:T(8,128)(2,1)S(1)}, u32[]{:S(2)}, u32[]{:S(2)}) collective-permute-start(bf16[256,256]{1,0:T(8,128)(2,1)S(1)} %layer.15), channel_id=1, source_target_pairs={{0,448},{1,449},{2,450},{3,451},{4,452},{5,453},{6,454},{7,455},{8... | collective-permute-start | bytes 393224 | tf_op jit(solution)/shard_map/ppermute | solution.py:277
  183.5 2.4 %collective-permute-done.8 = bf16[256,256]{1,0:T(8,128)(2,1)S(1)} collective-permute-done((bf16[256,256]{1,0:T(8,128)(2,1)S(1)}, bf16[256,256]{1,0:T(8,128)(2,1)S(1)}, u32[]{:S(2)}, u32[]{:S(2)}) %collective-permute-start.8) | collective-permute-done | bytes 131104 | tf_op jit(solution)/shard_map/ppermute | solution.py:277
  185.9 0.7 maximum_bitcast_fusion
  (1 shorter events, 0.0 us)
Async XLA Ops:
  0.0 26.1 %copy-start.2 = (s32[2,2,4,128,128]{4,3,2,1,0:T(8,128)S(1)}, s32[2,2,4,128,128]{4,3,2,1,0:T(8,128)}, u32[]{:S(2)}) copy-start(s32[2,2,4,128,128]{4,3,2,1,0:T(8,128)} %adj_ref.1) | copy-start | bytes 3145732
  2.1 24.0 %copy-start.5 = (s32[2,1,64,8]{2,3,1,0:T(8,128)S(1)}, s32[2,1,64,8]{2,3,1,0:T(8,128)}, u32[]{:S(2)}) copy-start(s32[2,1,64,8]{2,3,1,0:T(8,128)} %param.15) | copy-start | bytes 12292
  2.1 26.9 %all-to-all-start = ((bf16[64,8,256]{2,1,0:T(8,128)(2,1)}), bf16[64,8,256]{2,1,0:T(8,128)(2,1)S(1)}, u32[]{:S(2)}, u32[]{:S(2)}) async-start(bf16[64,8,256]{2,1,0:T(8,128)(2,1)} %bitcast.25), calls=%async_computation | async-start | bytes 524288 | tf_op jit(solution)/shard_map/all_to_all | solution.py:264
  13.8 12.4 %copy-start = (bf16[512,256]{1,0:T(8,128)(2,1)S(1)}, bf16[512,256]{1,0:T(8,128)(2,1)}, u32[]{:S(2)}) copy-start(bf16[512,256]{1,0:T(8,128)(2,1)} %first_gather.1.after_ref) | copy-start | bytes 786436
  13.8 12.4 %copy-start.3 = (bf16[2,256,256]{2,1,0:T(8,128)(2,1)S(1)}, bf16[2,256,256]{2,1,0:T(8,128)(2,1)}, u32[]{:S(2)}) copy-start(bf16[2,256,256]{2,1,0:T(8,128)(2,1)} %features_ref.3) | copy-start | bytes 786436
  13.8 12.4 %copy-start.4 = (s32[2,1,64,8]{2,3,1,0:T(8,128)S(1)}, s32[2,1,64,8]{2,3,1,0:T(8,128)}, u32[]{:S(2)}) copy-start(s32[2,1,64,8]{2,3,1,0:T(8,128)} %param.14) | copy-start | bytes 12292
  13.8 12.4 %copy-start.6 = (s32[2,2,4]{2,1,0:T(2,128)S(1)}, s32[2,2,4]{2,1,0:T(2,128)}, u32[]{:S(2)}) copy-start(s32[2,2,4]{2,1,0:T(2,128)} %col_ref.1) | copy-start | bytes 196
  15.5 13.6 %collective-permute-start = (bf16[272,256]{1,0:T(8,128)(2,1)}, bf16[272,256]{1,0:T(8,128)(2,1)S(1)}, u32[]{:S(2)}, u32[]{:S(2)}) collective-permute-start(bf16[272,256]{1,0:T(8,128)(2,1)} %pack_layer.1.early_ref.late_ref), channel_id=1, source_target_pairs={{0,448},{64,0},{128,64},{192,128},{256,192},{320,256},{384,320},{4... | collective-permute-start | bytes 417800 | tf_op jit(solution)/shard_map/ppermute | solution.py:267
  26.2 2.8 %copy-start.1 = (bf16[272,256]{1,0:T(8,128)(2,1)S(1)}, bf16[272,256]{1,0:T(8,128)(2,1)}, u32[]{:S(2)}) copy-start(bf16[272,256]{1,0:T(8,128)(2,1)} %pack_layer.1.early_ref.late_ref) | copy-start | bytes 417796
  30.5 23.3 %all-to-all-start.1 = ((bf16[64,8,256]{2,1,0:T(8,128)(2,1)}), bf16[64,8,256]{2,1,0:T(8,128)(2,1)S(1)}, u32[]{:S(2)}, u32[]{:S(2)}) async-start(bf16[64,8,256]{2,1,0:T(8,128)(2,1)} %bitcast.5), calls=%async_computation.1 | async-start | bytes 524288 | tf_op jit(solution)/shard_map/all_to_all | solution.py:264
  41.8 7.8 %collective-permute-start.1 = (bf16[272,256]{1,0:T(8,128)(2,1)S(1)}, bf16[272,256]{1,0:T(8,128)(2,1)S(1)}, u32[]{:S(2)}, u32[]{:S(2)}) collective-permute-start(bf16[272,256]{1,0:T(8,128)(2,1)S(1)} %get-tuple-element.38.early_ref), channel_id=1, source_target_pairs={{0,448},{64,0},{128,64},{192,128},{256,192},{320,256},{384,320},{4... | collective-permute-start | bytes 417800 | tf_op jit(solution)/shard_map/ppermute | solution.py:267
  55.3 19.1 %all-to-all-start.2 = ((bf16[64,8,256]{2,1,0:T(8,128)(2,1)}), bf16[64,8,256]{2,1,0:T(8,128)(2,1)S(1)}, u32[]{:S(2)}, u32[]{:S(2)}) async-start(bf16[64,8,256]{2,1,0:T(8,128)(2,1)} %bitcast.7), calls=%async_computation.2 | async-start | bytes 524288 | tf_op jit(solution)/shard_map/all_to_all | solution.py:264
  62.3 7.9 %collective-permute-start.2 = (bf16[272,256]{1,0:T(8,128)(2,1)S(1)}, bf16[272,256]{1,0:T(8,128)(2,1)S(1)}, u32[]{:S(2)}, u32[]{:S(2)}) collective-permute-start(bf16[272,256]{1,0:T(8,128)(2,1)S(1)} %get-tuple-element.41.early_ref), channel_id=1, source_target_pairs={{0,448},{64,0},{128,64},{192,128},{256,192},{320,256},{384,320},{4... | collective-permute-start | bytes 417800 | tf_op jit(solution)/shard_map/ppermute | solution.py:267
  75.8 19.2 %all-to-all-start.3 = ((bf16[64,8,256]{2,1,0:T(8,128)(2,1)}), bf16[64,8,256]{2,1,0:T(8,128)(2,1)S(1)}, u32[]{:S(2)}, u32[]{:S(2)}) async-start(bf16[64,8,256]{2,1,0:T(8,128)(2,1)} %bitcast.9), calls=%async_computation.3 | async-start | bytes 524288 | tf_op jit(solution)/shard_map/all_to_all | solution.py:264
  83.0 7.9 %collective-permute-start.3 = (bf16[272,256]{1,0:T(8,128)(2,1)S(1)}, bf16[272,256]{1,0:T(8,128)(2,1)S(1)}, u32[]{:S(2)}, u32[]{:S(2)}) collective-permute-start(bf16[272,256]{1,0:T(8,128)(2,1)S(1)} %get-tuple-element.44.early_ref), channel_id=1, source_target_pairs={{0,448},{64,0},{128,64},{192,128},{256,192},{320,256},{384,320},{4... | collective-permute-start | bytes 417800 | tf_op jit(solution)/shard_map/ppermute | solution.py:267
  96.5 19.2 %all-to-all-start.4 = ((bf16[64,8,256]{2,1,0:T(8,128)(2,1)}), bf16[64,8,256]{2,1,0:T(8,128)(2,1)S(1)}, u32[]{:S(2)}, u32[]{:S(2)}) async-start(bf16[64,8,256]{2,1,0:T(8,128)(2,1)} %bitcast.11), calls=%async_computation.4 | async-start | bytes 524288 | tf_op jit(solution)/shard_map/all_to_all | solution.py:264
  103.7 7.9 %collective-permute-start.4 = (bf16[272,256]{1,0:T(8,128)(2,1)S(1)}, bf16[272,256]{1,0:T(8,128)(2,1)S(1)}, u32[]{:S(2)}, u32[]{:S(2)}) collective-permute-start(bf16[272,256]{1,0:T(8,128)(2,1)S(1)} %get-tuple-element.47.early_ref), channel_id=1, source_target_pairs={{0,448},{64,0},{128,64},{192,128},{256,192},{320,256},{384,320},{4... | collective-permute-start | bytes 417800 | tf_op jit(solution)/shard_map/ppermute | solution.py:267
  117.2 19.2 %all-to-all-start.5 = ((bf16[64,8,256]{2,1,0:T(8,128)(2,1)}), bf16[64,8,256]{2,1,0:T(8,128)(2,1)S(1)}, u32[]{:S(2)}, u32[]{:S(2)}) async-start(bf16[64,8,256]{2,1,0:T(8,128)(2,1)} %bitcast.13), calls=%async_computation.5 | async-start | bytes 524288 | tf_op jit(solution)/shard_map/all_to_all | solution.py:264
  124.3 7.9 %collective-permute-start.5 = (bf16[272,256]{1,0:T(8,128)(2,1)S(1)}, bf16[272,256]{1,0:T(8,128)(2,1)S(1)}, u32[]{:S(2)}, u32[]{:S(2)}) collective-permute-start(bf16[272,256]{1,0:T(8,128)(2,1)S(1)} %get-tuple-element.50.early_ref), channel_id=1, source_target_pairs={{0,448},{64,0},{128,64},{192,128},{256,192},{320,256},{384,320},{4... | collective-permute-start | bytes 417800 | tf_op jit(solution)/shard_map/ppermute | solution.py:267
  137.8 19.2 %all-to-all-start.6 = ((bf16[64,8,256]{2,1,0:T(8,128)(2,1)}), bf16[64,8,256]{2,1,0:T(8,128)(2,1)S(1)}, u32[]{:S(2)}, u32[]{:S(2)}) async-start(bf16[64,8,256]{2,1,0:T(8,128)(2,1)} %bitcast.15), calls=%async_computation.6 | async-start | bytes 524288 | tf_op jit(solution)/shard_map/all_to_all | solution.py:264
  145.0 7.9 %collective-permute-start.6 = (bf16[272,256]{1,0:T(8,128)(2,1)S(1)}, bf16[272,256]{1,0:T(8,128)(2,1)S(1)}, u32[]{:S(2)}, u32[]{:S(2)}) collective-permute-start(bf16[272,256]{1,0:T(8,128)(2,1)S(1)} %get-tuple-element.53.early_ref), channel_id=1, source_target_pairs={{0,448},{64,0},{128,64},{192,128},{256,192},{320,256},{384,320},{4... | collective-permute-start | bytes 417800 | tf_op jit(solution)/shard_map/ppermute | solution.py:267
  158.5 19.2 %all-to-all-start.7 = ((bf16[64,8,256]{2,1,0:T(8,128)(2,1)}), bf16[64,8,256]{2,1,0:T(8,128)(2,1)S(1)}, u32[]{:S(2)}, u32[]{:S(2)}) async-start(bf16[64,8,256]{2,1,0:T(8,128)(2,1)} %bitcast.17), calls=%async_computation.7 | async-start | bytes 524288 | tf_op jit(solution)/shard_map/all_to_all | solution.py:264
  165.7 6.5 %collective-permute-start.7 = (bf16[256,256]{1,0:T(8,128)(2,1)S(1)}, bf16[256,256]{1,0:T(8,128)(2,1)S(1)}, u32[]{:S(2)}, u32[]{:S(2)}) collective-permute-start(bf16[256,256]{1,0:T(8,128)(2,1)S(1)} %get-tuple-element.54.hidden_ref), channel_id=1, source_target_pairs={{64,0},{128,64},{192,128},{256,192},{320,256},{384,320},{448,384},... | collective-permute-start | bytes 393224 | tf_op jit(solution)/shard_map/ppermute | solution.py:270
  178.2 7.7 %collective-permute-start.8 = (bf16[256,256]{1,0:T(8,128)(2,1)S(1)}, bf16[256,256]{1,0:T(8,128)(2,1)S(1)}, u32[]{:S(2)}, u32[]{:S(2)}) collective-permute-start(bf16[256,256]{1,0:T(8,128)(2,1)S(1)} %layer.15), channel_id=1, source_target_pairs={{0,448},{1,449},{2,450},{3,451},{4,452},{5,453},{6,454},{7,455},{8... | collective-permute-start | bytes 393224 | tf_op jit(solution)/shard_map/ppermute | solution.py:277

commit v3 on v2

--- a/solution.py
+++ b/solution.py
@@ -7,7 +7,7 @@
 from jax.experimental.pallas import tpu as pltpu
 from jax.sharding import PartitionSpec as P
 
-PACK_ROWS = 16
+PACK_ROWS = 32
 KERNEL_VMEM = 8 * 2**20
 VMEM = pl.BlockSpec(memory_space=pltpu.VMEM)
 SMEM = pl.BlockSpec(memory_space=pltpu.SMEM)
@@ -59,31 +59,84 @@
     return [pltpu.VMEM((slots, width), jnp.bfloat16), pltpu.SemaphoreType.DMA((CHUNKS,))]
 
 
-def first_kernel(span_ref, features_ref, send_ref, outgoing_ref, select_ref, staged_ref, sems):
+def pack_rows(weight_ref, bias_ref, gain_ref, pack_ref):
+    width = weight_ref.shape[-1]
+    pack_ref[0:width, :] = weight_ref[0]
+    row = lax.broadcasted_iota(jnp.int32, (PACK_ROWS, width), 0)
+    small = jnp.zeros((PACK_ROWS, width), jnp.float32)
+    for at, ref in ((0, bias_ref), (2, gain_ref)):
+        vector = ref[...]
+        high = vector.astype(jnp.bfloat16).astype(jnp.float32)
+        small = jnp.where(row == at, high, small)
+        small = jnp.where(row == at + 1, vector - high, small)
+    pack_ref[width : width + PACK_ROWS, :] = small.astype(jnp.bfloat16)
+
+
+def first_kernel(
+    span_ref,
+    core_ref,
+    features_ref,
+    send_ref,
+    weight_ref,
+    bias_ref,
+    gain_ref,
+    outgoing_ref,
+    own_ref,
+    half_ref,
+    select_ref,
+    pack_ref,
+    part_ref,
+    pack_sems,
+    staged_ref,
+    sems,
+):
+    pack_rows(weight_ref, bias_ref, gain_ref, pack_ref)
+    rows = part_ref.shape[0]
+    part_ref[...] = jnp.where(core_ref[0] == 0, pack_ref[0:rows, :], pack_ref[rows : 2 * rows, :])
+    copies = [
+        pltpu.make_async_copy(part_ref, half_ref, pack_sems.at[0]),
+        pltpu.make_async_copy(pack_ref, own_ref, pack_sems.at[1]),
+    ]
+    for copy in copies:
+        copy.start()
     select_ref[...] = one_hot_rows(slot_column(send_ref[0, 0]), features_ref.shape[1])
     gather_out(select_ref, features_ref[0], outgoing_ref, staged_ref, sems)
-
-
-def first_gather(span, features, send_rows):
+    for copy in copies:
+        copy.wait()
+
+
+def first_gather(span, core, features, send_rows, weight, bias, gain):
     _, rows, width = features.shape
     slots, peers = send_rows.shape[2:]
+    pack = (width + PACK_ROWS, width)
+    half = (pack[0] // 2, width)
     return pl.pallas_call(
         first_kernel,
         grid_spec=pltpu.PrefetchScalarGridSpec(
-            num_scalar_prefetch=1,
+            num_scalar_prefetch=2,
             grid=(1,),
             in_specs=[
-                pl.BlockSpec((1, rows, width), lambda i, s: (s[0], 0, 0)),
-                pl.BlockSpec((1, 1, slots, peers), lambda i, s: (s[0], 0, 0, 0)),
+                pl.BlockSpec((1, rows, width), lambda i, s, c: (s[0], 0, 0)),
+                pl.BlockSpec((1, 1, slots, peers), lambda i, s, c: (s[0], 0, 0, 0)),
+                pl.BlockSpec(weight.shape, lambda i, s, c: (0, 0, 0)),
+                pl.BlockSpec(bias.shape, lambda i, s, c: (0, 0)),
+                pl.BlockSpec(gain.shape, lambda i, s, c: (0, 0)),
             ],
-            out_specs=ANYWHERE,
-            scratch_shapes=[pltpu.VMEM((peers * slots, rows), jnp.bfloat16)]
+            out_specs=[ANYWHERE] * 3,
+            scratch_shapes=[
+                pltpu.VMEM((peers * slots, rows), jnp.bfloat16),
+                pltpu.VMEM(pack, jnp.bfloat16),
+                pltpu.VMEM(half, jnp.bfloat16),
+                pltpu.SemaphoreType.DMA((2,)),
+            ]
             + gather_scratch(peers * slots, width),
         ),
-        out_shape=jax.ShapeDtypeStruct((peers * slots, width), jnp.bfloat16),
+        out_shape=[
+            jax.ShapeDtypeStruct(shape, jnp.bfloat16) for shape in ((peers * slots, width), pack, half)
+        ],
         compiler_params=WIDE_PARAMS,
         name="first_gather",
-    )(span, features, send_rows)
+    )(span, core, features, send_rows, weight, bias, gain)
 
 
 def tables_kernel(
@@ -161,34 +214,10 @@
     )(span, tile_col, tile_adj, recv_dst, send_rows, features, after)
 
 
-def pack_kernel(weight_ref, bias_ref, gain_ref, after_ref, pack_ref):
-    width = weight_ref.shape[-1]
-    pack_ref[0:width, :] = weight_ref[0]
-    row = lax.broadcasted_iota(jnp.int32, (PACK_ROWS, width), 0)
-    small = jnp.zeros((PACK_ROWS, width), jnp.float32)
-    for at, ref in ((0, bias_ref), (2, gain_ref)):
-        vector = ref[...]
-        high = vector.astype(jnp.bfloat16).astype(jnp.float32)
-        small = jnp.where(row == at, high, small)
-        small = jnp.where(row == at + 1, vector - high, small)
-    pack_ref[width : width + PACK_ROWS, :] = small.astype(jnp.bfloat16)
-
-
-def pack_layer(weight, bias, gain, after):
-    width = weight.shape[-1]
-    return pl.pallas_call(
-        pack_kernel,
-        out_shape=jax.ShapeDtypeStruct((width + PACK_ROWS, width), jnp.bfloat16),
-        in_specs=[VMEM] * 3 + [ANYWHERE],
-        out_specs=VMEM,
-        compiler_params=WIDE_PARAMS,
-        name="pack_layer",
-    )(weight, bias, gain, after)
-
-
 def layer_kernel(
     step,
     layers,
+    passed,
     plane_ref,
     hidden_ref,
     arrived_ref,
@@ -198,10 +227,9 @@
     select_ref,
     early_ref,
     late_ref,
-    after_ref,
-    state_ref,
     *refs,
 ):
+    passed_in, refs = refs[:passed], refs[passed:]
     rows, width = hidden_ref.shape
     plane = plane_ref[0]
     begin = jnp.where(plane == 0, 0, layers - 1 - plane)
@@ -218,31 +246,34 @@
     summed = hidden.astype(jnp.float32) + jnp.maximum(projected, 0.0)
     scale = lax.rsqrt(jnp.mean(summed * summed, axis=1, keepdims=True) + 1e-05)
     state = (summed * scale * gain).astype(jnp.bfloat16)
-    if step < layers - 1:
-        state = jnp.where(step >= begin, state, hidden)
+    if step == layers - 1:
+        own_ref, send_ref = refs
+        own_ref[...] = jnp.where(plane == 0, passed_in[0][...], state)
+        send_ref[...] = jnp.where(plane == 0, state, hidden)
+        return
+    state = jnp.where(step >= begin, state, hidden)
+    state_ref, outgoing_ref, *refs = refs
     state_ref[...] = state
-    if step < layers - 1:
-        carried_ref, outgoing_ref, staged_ref, sems = refs
-        carried_ref[...] = late_ref[...]
-        gather_out(select_ref, state, outgoing_ref, staged_ref, sems)
-
-
-def run_layer(step, layers, plane, hidden, arrived, tables, early, late, after):
-    slots, width = arrived.shape
-    outs = [hidden, late, arrived]
-    out_specs = [VMEM, VMEM, ANYWHERE]
-    scratch = gather_scratch(slots, width)
+    outgoing_ref[...] = jnp.dot(select_ref[...], state, preferred_element_type=jnp.float32).astype(jnp.bfloat16)
+    for source_ref, target_ref in zip(passed_in, refs):
+        target_ref[...] = source_ref[...]
+
+
+def run_layer(step, layers, plane, hidden, arrived, tables, early, late, passed=()):
+    outs = [jax.ShapeDtypeStruct(hidden.shape, jnp.bfloat16)]
     if step == layers - 1:
-        outs, out_specs, scratch = outs[:1], out_specs[:1], []
+        outs *= 2
+    else:
+        outs.append(pltpu.VMEM(arrived.shape, jnp.bfloat16))
+        outs += [jax.ShapeDtypeStruct(array.shape, jnp.bfloat16) for array in passed]
     return pl.pallas_call(
-        functools.partial(layer_kernel, step, layers),
-        out_shape=[jax.ShapeDtypeStruct(out.shape, jnp.bfloat16) for out in outs],
-        in_specs=[SMEM] + [VMEM] * 8 + [ANYWHERE],
-        out_specs=out_specs,
-        scratch_shapes=scratch,
+        functools.partial(layer_kernel, step, layers, len(passed)),
+        out_shape=outs,
+        in_specs=[SMEM] + [VMEM] * (8 + len(passed)),
+        out_specs=[VMEM] * len(outs),
         compiler_params=PARAMS,
         name="layer",
-    )(plane, hidden, arrived, *tables, early, late, after)
+    )(plane, hidden, arrived, *tables, early, late, *passed)
 
 
 def local(features, weight, bias, gain, tile_col, tile_adj, send_rows, recv_dst):
@@ -251,34 +282,41 @@
     peers, slots = send_rows.shape[2:]
     width = features.shape[-1]
     plane = index.reshape(1)
-    span = plane % 2
+    core = (lax.axis_index("dom") % 2).reshape(1)
+    span = (index % 2).reshape(1)
+    cores = [[2 * chip, 2 * chip + 1] for chip in range(peers // 2)]
+    down = [(z, (z - 1) % layers) for z in range(layers)]
+    two_down = [(z, (z - 2) % layers) for z in range(layers)]
     send_rows = send_rows.transpose(0, 1, 3, 2)
     recv_dst = recv_dst.transpose(0, 1, 3, 2)
-    down = [(z, (z - 1) % layers) for z in range(layers)]
-
-    outgoing = first_gather(span, features, send_rows)
-    own_pack = pack_layer(weight, bias, gain, outgoing)
+
+    outgoing, own_pack, own_half = first_gather(span, core, features, send_rows, weight, bias, gain)
     *tables, hidden = build_tables(span, tile_col, tile_adj, recv_dst, send_rows, features, outgoing)
-    early = carried = own_pack
-    for step in range(layers):
+    early = own_pack
+    for step in range(layers - 1):
         arrived = lax.all_to_all(outgoing.reshape(peers, slots, width), "dom", 0, 0, tiled=True)
         arrived = arrived.reshape(peers * slots, width)
-        if step < layers - 1:
-            late = after = lax.ppermute(carried, "layer", down)
-        else:
-            late = own_pack
-            after = from_above = lax.ppermute(hidden, "layer", down[1:])
-        hidden, *more = run_layer(step, layers, plane, hidden, arrived, tables, early, late, after)
+        if step == 0:
+            half = lax.ppermute(own_half, "layer", down)
+        late = lax.all_gather(half, "dom", axis_index_groups=cores, tiled=True)
+        passed = []
+        if step < layers - 2:
+            source, pairs = (own_half, two_down) if step == 0 else (half, down)
+            passed = [lax.ppermute(source, "layer", pairs)]
+        hidden, outgoing, *more = run_layer(
+            step, layers, plane, hidden, arrived, tables, early, late, passed
+        )
         if more:
-            carried, outgoing = more
-            early = carried
+            half = more[0]
         if step == 0:
             first_state = hidden
-    last_state = lax.ppermute(hidden, "layer", down[:1])
-    own = jnp.where(index == 0, first_state, hidden)
-    other = jnp.where(index == layers - 1, last_state, from_above)
+        early = late
+    arrived = lax.all_to_all(outgoing.reshape(peers, slots, width), "dom", 0, 0, tiled=True)
+    arrived = arrived.reshape(peers * slots, width)
+    own, send = run_layer(layers - 1, layers, plane, hidden, arrived, tables, early, own_pack, [first_state])
+    swapped = lax.ppermute(send, "layer", down)
     even = index % 2 == 0
-    return jnp.stack([jnp.where(even, own, other), jnp.where(even, other, own)])[None]
+    return jnp.stack([jnp.where(even, own, swapped), jnp.where(even, swapped, own)])[None]
 
 
 def solution(mesh):

time: 188 us -> 182 us (0.968)
  blocking collectives: 0 us -> 34 us
  starting transfers between devices: 115 us -> 94 us
  waiting for transfers between devices: 54.9 us -> 37 us
  Pallas kernels: 15.7 us -> 13.7 us
    ppermute x9 -> x8, waiting for transfers between devices: 24.7 us -> 2.41 us  [the longest x1 2.4 us: local(): swapped = lax.ppermute(send, 'layer', down)]
    all_to_all x0 -> x1, blocking collectives: none -> 17.8 us  [local(): lax.all_to_all(outgoing.reshape(peers, slots, width), 'dom', 0, 0, tiled=...]
    all_gather x0 -> x7, blocking collectives: none -> 16.2 us  [local(): late = lax.all_gather(half, 'dom', axis_index_groups=cores, tiled=True)]
    all_to_all x8 -> x7, starting transfers between devices: 65.8 us -> 52.5 us  [local(): lax.all_to_all(outgoing.reshape(peers, slots, width), 'dom', 0, 0, tiled=...]
    ppermute x9 -> x8, starting transfers between devices: 49.1 us -> 41.5 us  [the longest x6 26.1 us: local(): passed = [lax.ppermute(source, 'layer', pairs)]]
    all_to_all x8 -> x7, waiting for transfers between devices: 30.2 us -> 34.6 us  [local(): lax.all_to_all(outgoing.reshape(peers, slots, width), 'dom', 0, 0, tiled=...]
    pallas_call x9 -> x8, Pallas kernels: 12.5 us -> 10.4 us  [run_layer(): pl.pallas_call(functools.partial(layer_kernel, step, layers, len(passed))...]
  transfers between devices with their start and end apart: 17 -> 15, of which waited for: 16 -> 7; matrix products, arithmetic and copies ran while one was open for 0% -> 0% of each run, Pallas kernels for 1% -> 1%
where the time goes in v3:
time: 182 us; the launch traced here: 181 us
  starting transfers between devices  94 us (52%)
  waiting for transfers between devices  37 us (20%)
  blocking collectives  34 us (19%)
  Pallas kernels  13.7 us (8%)
    all_to_all x7, starting transfers between devices, local(): lax.all_to_all(outgoing.reshape(peers, slots, width), 'dom', 0, 0, tiled=...  52.5 us
    all_to_all x7, waiting for transfers between devices, local(): lax.all_to_all(outgoing.reshape(peers, slots, width), 'dom', 0, 0, tiled=...  34.6 us
    ppermute x6, starting transfers between devices, local(): passed = [lax.ppermute(source, 'layer', pairs)]  26.1 us
    all_to_all x1, blocking collectives, local(): lax.all_to_all(outgoing.reshape(peers, slots, width), 'dom', 0, 0, tiled=...  17.8 us
    all_gather x7, blocking collectives, local(): late = lax.all_gather(half, 'dom', axis_index_groups=cores, tiled=True)  16.2 us
    ppermute x1, starting transfers between devices, local(): half = lax.ppermute(own_half, 'layer', down)  10.7 us
    pallas_call x8, Pallas kernels, run_layer(): pl.pallas_call(functools.partial(layer_kernel, step, layers, len(passed))...  10.4 us
    ppermute x1, starting transfers between devices, local(): swapped = lax.ppermute(send, 'layer', down)  4.78 us
  transfers between devices with their start and end apart: 15, of which 7 were waited for; matrix products, arithmetic and copies ran while one was open for 0% of the time, Pallas kernels for 1%

profile of v3, /device:TPU:1, one launch (start us, length us, event | category | flops | bytes accessed | tf_op | source)
XLA Modules:
  0.0 181.1 jit_solution(12054715258155568328)
XLA Ops:
  0.0 0.0 copy-start.4
  0.0 0.0 copy-start.5
  0.0 2.2 %first_gather.1 = (bf16[512,256]{1,0:T(8,128)(2,1)}, bf16[288,256]{1,0:T(8,128)(2,1)}, bf16[144,256]{1,0:T(8,128)(2,1)}) custom-call(s32[1]{0:T(128)} %bitcast.1.span_ref, s32[1]{0:T(128)} %bitcast.4.core_ref, bf16[2,256,256]{2,1,0:T(8,128)(2,1)} %features_ref.3, s32[2,1,8,64]{3,2,1,0:T(8,128)} %bitcast.37, bf16[1,256,256]{2,1,0:T(8,128)(2,1)} %weight_ref.1, ...), custom_call_target="tpu_custom_call" | custom-call | tf_op jit(solution)/shard_map/first_gather/pallas_call | solution.py:113
  2.2 0.0 copy-start.1
  2.2 0.0 copy-start.2
  2.2 11.8 %all-to-all-start = ((bf16[64,8,256]{2,1,0:T(8,128)(2,1)}), bf16[64,8,256]{2,1,0:T(8,128)(2,1)S(1)}, u32[]{:S(2)}, u32[]{:S(2)}) async-start(bf16[64,8,256]{2,1,0:T(8,128)(2,1)} %bitcast.28), calls=%async_computation | async-start | bytes 524288 | tf_op jit(solution)/shard_map/all_to_all | solution.py:297
  14.0 0.0 copy-start.6
  14.0 10.7 %collective-permute-start = (bf16[144,256]{1,0:T(8,128)(2,1)}, bf16[144,256]{1,0:T(8,128)(2,1)S(1)}, u32[]{:S(2)}, u32[]{:S(2)}) collective-permute-start(bf16[144,256]{1,0:T(8,128)(2,1)} %get-tuple-element.42), channel_id=1, source_target_pairs={{0,448},{64,0},{128,64},{192,128},{256,192},{320,256},{384,320},{4... | collective-permute-start | bytes 221192 | tf_op jit(solution)/shard_map/ppermute | solution.py:300
  24.7 2.2 %collective-permute-start.1 = (bf16[144,256]{1,0:T(8,128)(2,1)}, bf16[144,256]{1,0:T(8,128)(2,1)S(1)}, u32[]{:S(2)}, u32[]{:S(2)}) collective-permute-start(bf16[144,256]{1,0:T(8,128)(2,1)} %get-tuple-element.42), channel_id=1, source_target_pairs={{0,384},{64,448},{128,0},{192,64},{256,128},{320,192},{384,256},{4... | collective-permute-start | bytes 221192 | tf_op jit(solution)/shard_map/ppermute | solution.py:305
  26.9 0.0 copy-done.4
  26.9 0.0 copy-done.5
  26.9 0.0 copy-done.1
  26.9 0.0 copy-done.2
  26.9 0.0 copy-done.6
  26.9 0.0 copy-start
  26.9 1.2 copy-done
  28.1 1.1 build_tables.1
  29.3 0.0 copy-start.3
  29.3 0.0 collective-permute-done
  29.3 2.7 %all_gather.21.late_ref.early_ref = bf16[288,256]{1,0:T(8,128)(2,1)S(1)} all-gather(bf16[144,256]{1,0:T(8,128)(2,1)S(1)} %collective-permute-done), channel_id=1, replica_groups={{0,1},{2,3},{4,5},{6,7},{8,9},{10,11},{12,13},{14,15},{16,17},{18,19},{..., dimensions={0}, use_global_device_ids=true | all-gather | bytes 221184 | tf_op jit(solution)/shard_map/all_gather | solution.py:301
  32.0 0.0 collective-permute-done.1.refs_0_
  32.0 0.0 all-to-all-done
  32.0 0.0 copy-done.3
  32.0 1.5 layer.8
  33.5 10.6 %all-to-all-start.1 = ((bf16[64,8,256]{2,1,0:T(8,128)(2,1)}), bf16[64,8,256]{2,1,0:T(8,128)(2,1)S(1)}, u32[]{:S(2)}, u32[]{:S(2)}) async-start(bf16[64,8,256]{2,1,0:T(8,128)(2,1)} %bitcast.7), calls=%async_computation.1 | async-start | bytes 524288 | tf_op jit(solution)/shard_map/all_to_all | solution.py:297
  44.2 4.8 %collective-permute-start.2 = (bf16[144,256]{1,0:T(8,128)(2,1)S(1)}, bf16[144,256]{1,0:T(8,128)(2,1)S(1)}, u32[]{:S(2)}, u32[]{:S(2)}) collective-permute-start(bf16[144,256]{1,0:T(8,128)(2,1)S(1)} %get-tuple-element.45), channel_id=1, source_target_pairs={{0,448},{64,0},{128,64},{192,128},{256,192},{320,256},{384,320},{4... | collective-permute-start | bytes 221192 | tf_op jit(solution)/shard_map/ppermute | solution.py:305
  49.0 2.3 %all_gather.22.late_ref.early_ref = bf16[288,256]{1,0:T(8,128)(2,1)S(1)} all-gather(bf16[144,256]{1,0:T(8,128)(2,1)S(1)} %get-tuple-element.45), channel_id=1, replica_groups={{0,1},{2,3},{4,5},{6,7},{8,9},{10,11},{12,13},{14,15},{16,17},{18,19},{..., dimensions={0}, use_global_device_ids=true | all-gather | bytes 221184 | tf_op jit(solution)/shard_map/all_gather | solution.py:301
  51.3 0.0 collective-permute-done.2.refs_0_
  51.3 4.9 %all-to-all-done.1 = bf16[64,8,256]{2,1,0:T(8,128)(2,1)S(1)} async-done(((bf16[64,8,256]{2,1,0:T(8,128)(2,1)}), bf16[64,8,256]{2,1,0:T(8,128)(2,1)S(1)}, u32[]{:S(2)}, u32[]{:S(2)}) %all-to-all-start.1) | async-done | bytes 262176 | tf_op jit(solution)/shard_map/all_to_all | solution.py:297
  56.2 1.5 layer.9
  57.7 6.0 %all-to-all-start.2 = ((bf16[64,8,256]{2,1,0:T(8,128)(2,1)}), bf16[64,8,256]{2,1,0:T(8,128)(2,1)S(1)}, u32[]{:S(2)}, u32[]{:S(2)}) async-start(bf16[64,8,256]{2,1,0:T(8,128)(2,1)} %bitcast.9), calls=%async_computation.2 | async-start | bytes 524288 | tf_op jit(solution)/shard_map/all_to_all | solution.py:297
  63.7 4.8 %collective-permute-start.3 = (bf16[144,256]{1,0:T(8,128)(2,1)S(1)}, bf16[144,256]{1,0:T(8,128)(2,1)S(1)}, u32[]{:S(2)}, u32[]{:S(2)}) collective-permute-start(bf16[144,256]{1,0:T(8,128)(2,1)S(1)} %get-tuple-element.48), channel_id=1, source_target_pairs={{0,448},{64,0},{128,64},{192,128},{256,192},{320,256},{384,320},{4... | collective-permute-start | bytes 221192 | tf_op jit(solution)/shard_map/ppermute | solution.py:305
  68.5 2.3 %all_gather.23.late_ref.early_ref = bf16[288,256]{1,0:T(8,128)(2,1)S(1)} all-gather(bf16[144,256]{1,0:T(8,128)(2,1)S(1)} %get-tuple-element.48), channel_id=1, replica_groups={{0,1},{2,3},{4,5},{6,7},{8,9},{10,11},{12,13},{14,15},{16,17},{18,19},{..., dimensions={0}, use_global_device_ids=true | all-gather | bytes 221184 | tf_op jit(solution)/shard_map/all_gather | solution.py:301
  70.8 0.0 collective-permute-done.3.refs_0_
  70.8 4.9 %all-to-all-done.2 = bf16[64,8,256]{2,1,0:T(8,128)(2,1)S(1)} async-done(((bf16[64,8,256]{2,1,0:T(8,128)(2,1)}), bf16[64,8,256]{2,1,0:T(8,128)(2,1)S(1)}, u32[]{:S(2)}, u32[]{:S(2)}) %all-to-all-start.2) | async-done | bytes 262176 | tf_op jit(solution)/shard_map/all_to_all | solution.py:297
  75.7 1.5 layer.10
  77.3 6.0 %all-to-all-start.3 = ((bf16[64,8,256]{2,1,0:T(8,128)(2,1)}), bf16[64,8,256]{2,1,0:T(8,128)(2,1)S(1)}, u32[]{:S(2)}, u32[]{:S(2)}) async-start(bf16[64,8,256]{2,1,0:T(8,128)(2,1)} %bitcast.11), calls=%async_computation.3 | async-start | bytes 524288 | tf_op jit(solution)/shard_map/all_to_all | solution.py:297
  83.3 4.8 %collective-permute-start.4 = (bf16[144,256]{1,0:T(8,128)(2,1)S(1)}, bf16[144,256]{1,0:T(8,128)(2,1)S(1)}, u32[]{:S(2)}, u32[]{:S(2)}) collective-permute-start(bf16[144,256]{1,0:T(8,128)(2,1)S(1)} %get-tuple-element.51), channel_id=1, source_target_pairs={{0,448},{64,0},{128,64},{192,128},{256,192},{320,256},{384,320},{4... | collective-permute-start | bytes 221192 | tf_op jit(solution)/shard_map/ppermute | solution.py:305
  88.1 2.3 %all_gather.24.late_ref.early_ref = bf16[288,256]{1,0:T(8,128)(2,1)S(1)} all-gather(bf16[144,256]{1,0:T(8,128)(2,1)S(1)} %get-tuple-element.51), channel_id=1, replica_groups={{0,1},{2,3},{4,5},{6,7},{8,9},{10,11},{12,13},{14,15},{16,17},{18,19},{..., dimensions={0}, use_global_device_ids=true | all-gather | bytes 221184 | tf_op jit(solution)/shard_map/all_gather | solution.py:301
  90.4 0.0 collective-permute-done.4.refs_0_
  90.4 4.9 %all-to-all-done.3 = bf16[64,8,256]{2,1,0:T(8,128)(2,1)S(1)} async-done(((bf16[64,8,256]{2,1,0:T(8,128)(2,1)}), bf16[64,8,256]{2,1,0:T(8,128)(2,1)S(1)}, u32[]{:S(2)}, u32[]{:S(2)}) %all-to-all-start.3) | async-done | bytes 262176 | tf_op jit(solution)/shard_map/all_to_all | solution.py:297
  95.3 1.5 layer.11
  96.8 6.0 %all-to-all-start.4 = ((bf16[64,8,256]{2,1,0:T(8,128)(2,1)}), bf16[64,8,256]{2,1,0:T(8,128)(2,1)S(1)}, u32[]{:S(2)}, u32[]{:S(2)}) async-start(bf16[64,8,256]{2,1,0:T(8,128)(2,1)} %bitcast.13), calls=%async_computation.4 | async-start | bytes 524288 | tf_op jit(solution)/shard_map/all_to_all | solution.py:297
  102.8 4.8 %collective-permute-start.5 = (bf16[144,256]{1,0:T(8,128)(2,1)S(1)}, bf16[144,256]{1,0:T(8,128)(2,1)S(1)}, u32[]{:S(2)}, u32[]{:S(2)}) collective-permute-start(bf16[144,256]{1,0:T(8,128)(2,1)S(1)} %get-tuple-element.54), channel_id=1, source_target_pairs={{0,448},{64,0},{128,64},{192,128},{256,192},{320,256},{384,320},{4... | collective-permute-start | bytes 221192 | tf_op jit(solution)/shard_map/ppermute | solution.py:305
  107.6 2.3 %all_gather.25.late_ref.early_ref = bf16[288,256]{1,0:T(8,128)(2,1)S(1)} all-gather(bf16[144,256]{1,0:T(8,128)(2,1)S(1)} %get-tuple-element.54), channel_id=1, replica_groups={{0,1},{2,3},{4,5},{6,7},{8,9},{10,11},{12,13},{14,15},{16,17},{18,19},{..., dimensions={0}, use_global_device_ids=true | all-gather | bytes 221184 | tf_op jit(solution)/shard_map/all_gather | solution.py:301
  109.9 0.0 collective-permute-done.5.refs_0_
  109.9 4.9 %all-to-all-done.4 = bf16[64,8,256]{2,1,0:T(8,128)(2,1)S(1)} async-done(((bf16[64,8,256]{2,1,0:T(8,128)(2,1)}), bf16[64,8,256]{2,1,0:T(8,128)(2,1)S(1)}, u32[]{:S(2)}, u32[]{:S(2)}) %all-to-all-start.4) | async-done | bytes 262176 | tf_op jit(solution)/shard_map/all_to_all | solution.py:297
  114.8 1.5 layer.12
  116.4 6.0 %all-to-all-start.5 = ((bf16[64,8,256]{2,1,0:T(8,128)(2,1)}), bf16[64,8,256]{2,1,0:T(8,128)(2,1)S(1)}, u32[]{:S(2)}, u32[]{:S(2)}) async-start(bf16[64,8,256]{2,1,0:T(8,128)(2,1)} %bitcast.15), calls=%async_computation.5 | async-start | bytes 524288 | tf_op jit(solution)/shard_map/all_to_all | solution.py:297
  122.4 4.8 %collective-permute-start.6 = (bf16[144,256]{1,0:T(8,128)(2,1)S(1)}, bf16[144,256]{1,0:T(8,128)(2,1)S(1)}, u32[]{:S(2)}, u32[]{:S(2)}) collective-permute-start(bf16[144,256]{1,0:T(8,128)(2,1)S(1)} %get-tuple-element.57), channel_id=1, source_target_pairs={{0,448},{64,0},{128,64},{192,128},{256,192},{320,256},{384,320},{4... | collective-permute-start | bytes 221192 | tf_op jit(solution)/shard_map/ppermute | solution.py:305
  127.2 2.3 %all_gather.26.late_ref.early_ref = bf16[288,256]{1,0:T(8,128)(2,1)S(1)} all-gather(bf16[144,256]{1,0:T(8,128)(2,1)S(1)} %get-tuple-element.57), channel_id=1, replica_groups={{0,1},{2,3},{4,5},{6,7},{8,9},{10,11},{12,13},{14,15},{16,17},{18,19},{..., dimensions={0}, use_global_device_ids=true | all-gather | bytes 221184 | tf_op jit(solution)/shard_map/all_gather | solution.py:301
  129.5 0.0 collective-permute-done.6.refs_0_
  129.5 4.9 %all-to-all-done.5 = bf16[64,8,256]{2,1,0:T(8,128)(2,1)S(1)} async-done(((bf16[64,8,256]{2,1,0:T(8,128)(2,1)}), bf16[64,8,256]{2,1,0:T(8,128)(2,1)S(1)}, u32[]{:S(2)}, u32[]{:S(2)}) %all-to-all-start.5) | async-done | bytes 262176 | tf_op jit(solution)/shard_map/all_to_all | solution.py:297
  134.4 1.5 layer.13
  135.9 6.0 %all-to-all-start.6 = ((bf16[64,8,256]{2,1,0:T(8,128)(2,1)}), bf16[64,8,256]{2,1,0:T(8,128)(2,1)S(1)}, u32[]{:S(2)}, u32[]{:S(2)}) async-start(bf16[64,8,256]{2,1,0:T(8,128)(2,1)} %bitcast.17), calls=%async_computation.6 | async-start | bytes 524288 | tf_op jit(solution)/shard_map/all_to_all | solution.py:297
  142.0 2.0 %all_gather.27.late_ref.early_ref = bf16[288,256]{1,0:T(8,128)(2,1)S(1)} all-gather(bf16[144,256]{1,0:T(8,128)(2,1)S(1)} %get-tuple-element.60), channel_id=1, replica_groups={{0,1},{2,3},{4,5},{6,7},{8,9},{10,11},{12,13},{14,15},{16,17},{18,19},{..., dimensions={0}, use_global_device_ids=true | all-gather | bytes 221184 | tf_op jit(solution)/shard_map/all_gather | solution.py:301
  144.0 10.0 %all-to-all-done.6 = bf16[64,8,256]{2,1,0:T(8,128)(2,1)S(1)} async-done(((bf16[64,8,256]{2,1,0:T(8,128)(2,1)}), bf16[64,8,256]{2,1,0:T(8,128)(2,1)S(1)}, u32[]{:S(2)}, u32[]{:S(2)}) %all-to-all-start.6) | async-done | bytes 262176 | tf_op jit(solution)/shard_map/all_to_all | solution.py:297
  154.0 0.8 layer.14
  154.8 17.8 %all_to_all.40 = bf16[64,8,256]{2,1,0:T(8,128)(2,1)S(1)} all-to-all(bf16[64,8,256]{2,1,0:T(8,128)(2,1)S(1)} %bitcast.36), channel_id=1, replica_groups=mesh['layer'=8,'dom'=64] {'dom'}, dimensions={0} | all-to-all | bytes 524288 | tf_op jit(solution)/shard_map/all_to_all | solution.py:314
  172.6 0.5 layer.15
  173.1 4.8 %collective-permute-start.7 = (bf16[256,256]{1,0:T(8,128)(2,1)S(1)}, bf16[256,256]{1,0:T(8,128)(2,1)S(1)}, u32[]{:S(2)}, u32[]{:S(2)}) collective-permute-start(bf16[256,256]{1,0:T(8,128)(2,1)S(1)} %get-tuple-element.64), channel_id=1, source_target_pairs={{0,448},{64,0},{128,64},{192,128},{256,192},{320,256},{384,320},{4... | collective-permute-start | bytes 393224 | tf_op jit(solution)/shard_map/ppermute | solution.py:317
  177.9 2.4 %collective-permute-done.7 = bf16[256,256]{1,0:T(8,128)(2,1)S(1)} collective-permute-done((bf16[256,256]{1,0:T(8,128)(2,1)S(1)}, bf16[256,256]{1,0:T(8,128)(2,1)S(1)}, u32[]{:S(2)}, u32[]{:S(2)}) %collective-permute-start.7) | collective-permute-done | bytes 131104 | tf_op jit(solution)/shard_map/ppermute | solution.py:317
  180.3 0.7 maximum_bitcast_fusion
  (1 shorter events, 0.0 us)
Async XLA Ops:
  0.0 26.9 %copy-start.4 = (s32[2,1,64,8]{2,3,1,0:T(8,128)S(1)}, s32[2,1,64,8]{2,3,1,0:T(8,128)}, u32[]{:S(2)}) copy-start(s32[2,1,64,8]{2,3,1,0:T(8,128)} %param.14) | copy-start | bytes 12292
  0.0 26.9 %copy-start.5 = (s32[2,1,64,8]{2,3,1,0:T(8,128)S(1)}, s32[2,1,64,8]{2,3,1,0:T(8,128)}, u32[]{:S(2)}) copy-start(s32[2,1,64,8]{2,3,1,0:T(8,128)} %param.15) | copy-start | bytes 12292
  2.2 24.7 %copy-start.1 = (bf16[2,256,256]{2,1,0:T(8,128)(2,1)S(1)}, bf16[2,256,256]{2,1,0:T(8,128)(2,1)}, u32[]{:S(2)}) copy-start(bf16[2,256,256]{2,1,0:T(8,128)(2,1)} %features_ref.3) | copy-start | bytes 786436
  2.2 24.7 %copy-start.2 = (bf16[512,256]{1,0:T(8,128)(2,1)S(1)}, bf16[512,256]{1,0:T(8,128)(2,1)}, u32[]{:S(2)}) copy-start(bf16[512,256]{1,0:T(8,128)(2,1)} %get-tuple-element.35.after_ref) | copy-start | bytes 786436
  2.2 29.8 %all-to-all-start = ((bf16[64,8,256]{2,1,0:T(8,128)(2,1)}), bf16[64,8,256]{2,1,0:T(8,128)(2,1)S(1)}, u32[]{:S(2)}, u32[]{:S(2)}) async-start(bf16[64,8,256]{2,1,0:T(8,128)(2,1)} %bitcast.28), calls=%async_computation | async-start | bytes 524288 | tf_op jit(solution)/shard_map/all_to_all | solution.py:297
  14.0 12.9 %copy-start.6 = (s32[2,2,4]{2,1,0:T(2,128)S(1)}, s32[2,2,4]{2,1,0:T(2,128)}, u32[]{:S(2)}) copy-start(s32[2,2,4]{2,1,0:T(2,128)} %col_ref.1) | copy-start | bytes 196
  14.0 15.3 %collective-permute-start = (bf16[144,256]{1,0:T(8,128)(2,1)}, bf16[144,256]{1,0:T(8,128)(2,1)S(1)}, u32[]{:S(2)}, u32[]{:S(2)}) collective-permute-start(bf16[144,256]{1,0:T(8,128)(2,1)} %get-tuple-element.42), channel_id=1, source_target_pairs={{0,448},{64,0},{128,64},{192,128},{256,192},{320,256},{384,320},{4... | collective-permute-start | bytes 221192 | tf_op jit(solution)/shard_map/ppermute | solution.py:300
  24.7 7.3 %collective-permute-start.1 = (bf16[144,256]{1,0:T(8,128)(2,1)}, bf16[144,256]{1,0:T(8,128)(2,1)S(1)}, u32[]{:S(2)}, u32[]{:S(2)}) collective-permute-start(bf16[144,256]{1,0:T(8,128)(2,1)} %get-tuple-element.42), channel_id=1, source_target_pairs={{0,384},{64,448},{128,0},{192,64},{256,128},{320,192},{384,256},{4... | collective-permute-start | bytes 221192 | tf_op jit(solution)/shard_map/ppermute | solution.py:305
  26.9 1.2 copy-start
  29.3 2.7 %copy-start.3 = (bf16[288,256]{1,0:T(8,128)(2,1)S(1)}, bf16[288,256]{1,0:T(8,128)(2,1)}, u32[]{:S(2)}) copy-start(bf16[288,256]{1,0:T(8,128)(2,1)} %get-tuple-element.41.early_ref.late_ref) | copy-start | bytes 442372
  33.5 22.6 %all-to-all-start.1 = ((bf16[64,8,256]{2,1,0:T(8,128)(2,1)}), bf16[64,8,256]{2,1,0:T(8,128)(2,1)S(1)}, u32[]{:S(2)}, u32[]{:S(2)}) async-start(bf16[64,8,256]{2,1,0:T(8,128)(2,1)} %bitcast.7), calls=%async_computation.1 | async-start | bytes 524288 | tf_op jit(solution)/shard_map/all_to_all | solution.py:297
  44.2 7.1 %collective-permute-start.2 = (bf16[144,256]{1,0:T(8,128)(2,1)S(1)}, bf16[144,256]{1,0:T(8,128)(2,1)S(1)}, u32[]{:S(2)}, u32[]{:S(2)}) collective-permute-start(bf16[144,256]{1,0:T(8,128)(2,1)S(1)} %get-tuple-element.45), channel_id=1, source_target_pairs={{0,448},{64,0},{128,64},{192,128},{256,192},{320,256},{384,320},{4... | collective-permute-start | bytes 221192 | tf_op jit(solution)/shard_map/ppermute | solution.py:305
  57.7 18.0 %all-to-all-start.2 = ((bf16[64,8,256]{2,1,0:T(8,128)(2,1)}), bf16[64,8,256]{2,1,0:T(8,128)(2,1)S(1)}, u32[]{:S(2)}, u32[]{:S(2)}) async-start(bf16[64,8,256]{2,1,0:T(8,128)(2,1)} %bitcast.9), calls=%async_computation.2 | async-start | bytes 524288 | tf_op jit(solution)/shard_map/all_to_all | solution.py:297
  63.7 7.1 %collective-permute-start.3 = (bf16[144,256]{1,0:T(8,128)(2,1)S(1)}, bf16[144,256]{1,0:T(8,128)(2,1)S(1)}, u32[]{:S(2)}, u32[]{:S(2)}) collective-permute-start(bf16[144,256]{1,0:T(8,128)(2,1)S(1)} %get-tuple-element.48), channel_id=1, source_target_pairs={{0,448},{64,0},{128,64},{192,128},{256,192},{320,256},{384,320},{4... | collective-permute-start | bytes 221192 | tf_op jit(solution)/shard_map/ppermute | solution.py:305
  77.3 18.0 %all-to-all-start.3 = ((bf16[64,8,256]{2,1,0:T(8,128)(2,1)}), bf16[64,8,256]{2,1,0:T(8,128)(2,1)S(1)}, u32[]{:S(2)}, u32[]{:S(2)}) async-start(bf16[64,8,256]{2,1,0:T(8,128)(2,1)} %bitcast.11), calls=%async_computation.3 | async-start | bytes 524288 | tf_op jit(solution)/shard_map/all_to_all | solution.py:297
  83.3 7.1 %collective-permute-start.4 = (bf16[144,256]{1,0:T(8,128)(2,1)S(1)}, bf16[144,256]{1,0:T(8,128)(2,1)S(1)}, u32[]{:S(2)}, u32[]{:S(2)}) collective-permute-start(bf16[144,256]{1,0:T(8,128)(2,1)S(1)} %get-tuple-element.51), channel_id=1, source_target_pairs={{0,448},{64,0},{128,64},{192,128},{256,192},{320,256},{384,320},{4... | collective-permute-start | bytes 221192 | tf_op jit(solution)/shard_map/ppermute | solution.py:305
  96.8 18.0 %all-to-all-start.4 = ((bf16[64,8,256]{2,1,0:T(8,128)(2,1)}), bf16[64,8,256]{2,1,0:T(8,128)(2,1)S(1)}, u32[]{:S(2)}, u32[]{:S(2)}) async-start(bf16[64,8,256]{2,1,0:T(8,128)(2,1)} %bitcast.13), calls=%async_computation.4 | async-start | bytes 524288 | tf_op jit(solution)/shard_map/all_to_all | solution.py:297
  102.8 7.1 %collective-permute-start.5 = (bf16[144,256]{1,0:T(8,128)(2,1)S(1)}, bf16[144,256]{1,0:T(8,128)(2,1)S(1)}, u32[]{:S(2)}, u32[]{:S(2)}) collective-permute-start(bf16[144,256]{1,0:T(8,128)(2,1)S(1)} %get-tuple-element.54), channel_id=1, source_target_pairs={{0,448},{64,0},{128,64},{192,128},{256,192},{320,256},{384,320},{4... | collective-permute-start | bytes 221192 | tf_op jit(solution)/shard_map/ppermute | solution.py:305
  116.4 18.0 %all-to-all-start.5 = ((bf16[64,8,256]{2,1,0:T(8,128)(2,1)}), bf16[64,8,256]{2,1,0:T(8,128)(2,1)S(1)}, u32[]{:S(2)}, u32[]{:S(2)}) async-start(bf16[64,8,256]{2,1,0:T(8,128)(2,1)} %bitcast.15), calls=%async_computation.5 | async-start | bytes 524288 | tf_op jit(solution)/shard_map/all_to_all | solution.py:297
  122.4 7.1 %collective-permute-start.6 = (bf16[144,256]{1,0:T(8,128)(2,1)S(1)}, bf16[144,256]{1,0:T(8,128)(2,1)S(1)}, u32[]{:S(2)}, u32[]{:S(2)}) collective-permute-start(bf16[144,256]{1,0:T(8,128)(2,1)S(1)} %get-tuple-element.57), channel_id=1, source_target_pairs={{0,448},{64,0},{128,64},{192,128},{256,192},{320,256},{384,320},{4... | collective-permute-start | bytes 221192 | tf_op jit(solution)/shard_map/ppermute | solution.py:305
  135.9 18.0 %all-to-all-start.6 = ((bf16[64,8,256]{2,1,0:T(8,128)(2,1)}), bf16[64,8,256]{2,1,0:T(8,128)(2,1)S(1)}, u32[]{:S(2)}, u32[]{:S(2)}) async-start(bf16[64,8,256]{2,1,0:T(8,128)(2,1)} %bitcast.17), calls=%async_computation.6 | async-start | bytes 524288 | tf_op jit(solution)/shard_map/all_to_all | solution.py:297
  173.1 7.2 %collective-permute-start.7 = (bf16[256,256]{1,0:T(8,128)(2,1)S(1)}, bf16[256,256]{1,0:T(8,128)(2,1)S(1)}, u32[]{:S(2)}, u32[]{:S(2)}) collective-permute-start(bf16[256,256]{1,0:T(8,128)(2,1)S(1)} %get-tuple-element.64), channel_id=1, source_target_pairs={{0,448},{64,0},{128,64},{192,128},{256,192},{320,256},{384,320},{4... | collective-permute-start | bytes 393224 | tf_op jit(solution)/shard_map/ppermute | solution.py:317

commit v4 on v3

--- a/solution.py
+++ b/solution.py
@@ -246,13 +246,12 @@
     summed = hidden.astype(jnp.float32) + jnp.maximum(projected, 0.0)
     scale = lax.rsqrt(jnp.mean(summed * summed, axis=1, keepdims=True) + 1e-05)
     state = (summed * scale * gain).astype(jnp.bfloat16)
+    state_ref, *refs = refs
     if step == layers - 1:
-        own_ref, send_ref = refs
-        own_ref[...] = jnp.where(plane == 0, passed_in[0][...], state)
-        send_ref[...] = jnp.where(plane == 0, state, hidden)
+        state_ref[...] = state
         return
+    outgoing_ref, *refs = refs
     state = jnp.where(step >= begin, state, hidden)
-    state_ref, outgoing_ref, *refs = refs
     state_ref[...] = state
     outgoing_ref[...] = jnp.dot(select_ref[...], state, preferred_element_type=jnp.float32).astype(jnp.bfloat16)
     for source_ref, target_ref in zip(passed_in, refs):
@@ -261,9 +260,7 @@
 
 def run_layer(step, layers, plane, hidden, arrived, tables, early, late, passed=()):
     outs = [jax.ShapeDtypeStruct(hidden.shape, jnp.bfloat16)]
-    if step == layers - 1:
-        outs *= 2
-    else:
+    if step < layers - 1:
         outs.append(pltpu.VMEM(arrived.shape, jnp.bfloat16))
         outs += [jax.ShapeDtypeStruct(array.shape, jnp.bfloat16) for array in passed]
     return pl.pallas_call(
@@ -311,12 +308,24 @@
         if step == 0:
             first_state = hidden
         early = late
-    arrived = lax.all_to_all(outgoing.reshape(peers, slots, width), "dom", 0, 0, tiled=True)
-    arrived = arrived.reshape(peers * slots, width)
-    own, send = run_layer(layers - 1, layers, plane, hidden, arrived, tables, early, own_pack, [first_state])
-    swapped = lax.ppermute(send, "layer", down)
+    last = layers - 1
+    from_above = lax.ppermute(hidden, "layer", down[1:])
+
+    def finish(outgoing, hidden):
+        arrived = lax.all_to_all(outgoing.reshape(peers, slots, width), "dom", 0, 0, tiled=True)
+        arrived = arrived.reshape(peers * slots, width)
+        return run_layer(last, layers, plane, hidden, arrived, tables, early, own_pack)[0]
+
+    def idle(outgoing, hidden):
+        return jnp.zeros_like(hidden)
+
+    state = lax.cond(index < last, finish, idle, outgoing, hidden)
+    full = lax.ppermute(jnp.where(index == 0, state, from_above), "layer", down[:1])
+    last_state = lax.cond(index == last, finish, idle, outgoing, hidden)
+    own = jnp.where(index == 0, first_state, jnp.where(index == last, last_state, state))
+    other = jnp.where(index == last, full, from_above)
     even = index % 2 == 0
-    return jnp.stack([jnp.where(even, own, swapped), jnp.where(even, swapped, own)])[None]
+    return jnp.stack([jnp.where(even, own, other), jnp.where(even, other, own)])[None]
 
 
 def solution(mesh):

time: 182 us -> 180 us (0.989)
  starting transfers between devices: 94 us -> 92 us
    ppermute x1 -> x2, starting transfers between devices: 4.78 us -> 2.59 us  [the longest x1 1.3 us: local(): lax.ppermute(jnp.where(index == 0, state, from_above), 'layer', down[:1])]
  transfers between devices with their start and end apart: 15 -> 16, of which waited for: 7 -> 7; matrix products, arithmetic and copies ran while one was open for 0% -> 0% of each run, Pallas kernels for 1% -> 1%
where the time goes in v4:
time: 180 us; the launch traced here: 179 us
  starting transfers between devices  92 us (51%)
  waiting for transfers between devices  37.1 us (21%)
  blocking collectives  34.1 us (19%)
  Pallas kernels  13.9 us (8%)
    all_to_all x7, starting transfers between devices, local(): lax.all_to_all(outgoing.reshape(peers, slots, width), 'dom', 0, 0, tiled=...  52.7 us
    all_to_all x7, waiting for transfers between devices, local(): lax.all_to_all(outgoing.reshape(peers, slots, width), 'dom', 0, 0, tiled=...  34.4 us
    ppermute x6, starting transfers between devices, local(): passed = [lax.ppermute(source, 'layer', pairs)]  26 us
    all_to_all x1, blocking collectives, finish(): lax.all_to_all(outgoing.reshape(peers, slots, width), 'dom', 0, 0, tiled=...  17.8 us
    all_gather x7, blocking collectives, local(): late = lax.all_gather(half, 'dom', axis_index_groups=cores, tiled=True)  16.2 us
    ppermute x1, starting transfers between devices, local(): half = lax.ppermute(own_half, 'layer', down)  10.7 us
    pallas_call x8, Pallas kernels, run_layer(): pl.pallas_call(functools.partial(layer_kernel, step, layers, len(passed))...  10.4 us
  transfers between devices with their start and end apart: 16, of which 7 were waited for; matrix products, arithmetic and copies ran while one was open for 0% of the time, Pallas kernels for 1%

profile of v4, /device:TPU:1, one launch (start us, length us, event | category | flops | bytes accessed | tf_op | source)
XLA Modules:
  0.0 179.5 jit_solution(4317054822445035739)
XLA Ops:
  0.0 0.0 copy-start.3
  0.0 0.0 copy-start.4
  0.0 2.4 %first_gather.1 = (bf16[512,256]{1,0:T(8,128)(2,1)}, bf16[288,256]{1,0:T(8,128)(2,1)S(1)}, bf16[144,256]{1,0:T(8,128)(2,1)}) custom-call(s32[1]{0:T(128)} %bitcast.5.span_ref, s32[1]{0:T(128)} %bitcast.8.core_ref, bf16[2,256,256]{2,1,0:T(8,128)(2,1)} %features_ref.3, s32[2,1,8,64]{3,2,1,0:T(8,128)} %bitcast.41, bf16[1,256,256]{2,1,0:T(8,128)(2,1)} %weight_ref.1, ...), custom_call_target="tpu_custom_call" | custom-call | tf_op jit(solution)/shard_map/first_gather/pallas_call | solution.py:113
  2.4 0.0 copy-start.1
  2.4 0.0 copy-start.2
  2.4 11.8 %all-to-all-start.2 = ((bf16[64,8,256]{2,1,0:T(8,128)(2,1)}), bf16[64,8,256]{2,1,0:T(8,128)(2,1)S(1)}, u32[]{:S(2)}, u32[]{:S(2)}) async-start(bf16[64,8,256]{2,1,0:T(8,128)(2,1)} %bitcast.32), calls=%async_computation.2 | async-start | bytes 524288 | tf_op jit(solution)/shard_map/all_to_all | solution.py:294
  14.2 0.0 copy-start.5
  14.2 10.7 %collective-permute-start = (bf16[144,256]{1,0:T(8,128)(2,1)}, bf16[144,256]{1,0:T(8,128)(2,1)S(1)}, u32[]{:S(2)}, u32[]{:S(2)}) collective-permute-start(bf16[144,256]{1,0:T(8,128)(2,1)} %get-tuple-element.100), channel_id=1, source_target_pairs={{0,448},{64,0},{128,64},{192,128},{256,192},{320,256},{384,320},{4... | collective-permute-start | bytes 221192 | tf_op jit(solution)/shard_map/ppermute | solution.py:297
  24.8 2.2 %collective-permute-start.1 = (bf16[144,256]{1,0:T(8,128)(2,1)}, bf16[144,256]{1,0:T(8,128)(2,1)S(1)}, u32[]{:S(2)}, u32[]{:S(2)}) collective-permute-start(bf16[144,256]{1,0:T(8,128)(2,1)} %get-tuple-element.100), channel_id=1, source_target_pairs={{0,384},{64,448},{128,0},{192,64},{256,128},{320,192},{384,256},{4... | collective-permute-start | bytes 221192 | tf_op jit(solution)/shard_map/ppermute | solution.py:302
  27.0 0.0 copy-done.3
  27.0 0.0 copy-done.4
  27.0 0.0 copy-done.1
  27.1 0.0 copy-done.2
  27.1 0.0 copy-done.5
  27.1 0.0 copy-start
  27.1 1.2 copy-done
  28.3 1.1 build_tables.1
  29.4 0.0 collective-permute-done
  29.5 2.6 %all_gather.21.late_ref.early_ref = bf16[288,256]{1,0:T(8,128)(2,1)S(1)} all-gather(bf16[144,256]{1,0:T(8,128)(2,1)S(1)} %collective-permute-done), channel_id=1, replica_groups={{0,1},{2,3},{4,5},{6,7},{8,9},{10,11},{12,13},{14,15},{16,17},{18,19},{..., dimensions={0}, use_global_device_ids=true | all-gather | bytes 221184 | tf_op jit(solution)/shard_map/all_gather | solution.py:298
  32.0 0.0 collective-permute-done.1.refs_0_
  32.0 0.0 all-to-all-done.2
  32.0 1.5 layer.11
  33.6 10.8 %all-to-all-start.3 = ((bf16[64,8,256]{2,1,0:T(8,128)(2,1)}), bf16[64,8,256]{2,1,0:T(8,128)(2,1)S(1)}, u32[]{:S(2)}, u32[]{:S(2)}) async-start(bf16[64,8,256]{2,1,0:T(8,128)(2,1)} %bitcast.11), calls=%async_computation.3 | async-start | bytes 524288 | tf_op jit(solution)/shard_map/all_to_all | solution.py:294
  44.3 4.8 %collective-permute-start.2 = (bf16[144,256]{1,0:T(8,128)(2,1)S(1)}, bf16[144,256]{1,0:T(8,128)(2,1)S(1)}, u32[]{:S(2)}, u32[]{:S(2)}) collective-permute-start(bf16[144,256]{1,0:T(8,128)(2,1)S(1)} %get-tuple-element.103), channel_id=1, source_target_pairs={{0,448},{64,0},{128,64},{192,128},{256,192},{320,256},{384,320},{4... | collective-permute-start | bytes 221192 | tf_op jit(solution)/shard_map/ppermute | solution.py:302
  49.1 2.3 %all_gather.22.late_ref.early_ref = bf16[288,256]{1,0:T(8,128)(2,1)S(1)} all-gather(bf16[144,256]{1,0:T(8,128)(2,1)S(1)} %get-tuple-element.103), channel_id=1, replica_groups={{0,1},{2,3},{4,5},{6,7},{8,9},{10,11},{12,13},{14,15},{16,17},{18,19},{..., dimensions={0}, use_global_device_ids=true | all-gather | bytes 221184 | tf_op jit(solution)/shard_map/all_gather | solution.py:298
  51.4 0.0 collective-permute-done.2.refs_0_
  51.4 4.9 %all-to-all-done.3 = bf16[64,8,256]{2,1,0:T(8,128)(2,1)S(1)} async-done(((bf16[64,8,256]{2,1,0:T(8,128)(2,1)}), bf16[64,8,256]{2,1,0:T(8,128)(2,1)S(1)}, u32[]{:S(2)}, u32[]{:S(2)}) %all-to-all-start.3) | async-done | bytes 262176 | tf_op jit(solution)/shard_map/all_to_all | solution.py:294
  56.3 1.5 layer.12
  57.9 6.0 %all-to-all-start.4 = ((bf16[64,8,256]{2,1,0:T(8,128)(2,1)}), bf16[64,8,256]{2,1,0:T(8,128)(2,1)S(1)}, u32[]{:S(2)}, u32[]{:S(2)}) async-start(bf16[64,8,256]{2,1,0:T(8,128)(2,1)} %bitcast.13), calls=%async_computation.4 | async-start | bytes 524288 | tf_op jit(solution)/shard_map/all_to_all | solution.py:294
  63.9 4.8 %collective-permute-start.3 = (bf16[144,256]{1,0:T(8,128)(2,1)S(1)}, bf16[144,256]{1,0:T(8,128)(2,1)S(1)}, u32[]{:S(2)}, u32[]{:S(2)}) collective-permute-start(bf16[144,256]{1,0:T(8,128)(2,1)S(1)} %get-tuple-element.106), channel_id=1, source_target_pairs={{0,448},{64,0},{128,64},{192,128},{256,192},{320,256},{384,320},{4... | collective-permute-start | bytes 221192 | tf_op jit(solution)/shard_map/ppermute | solution.py:302
  68.7 2.3 %all_gather.23.late_ref.early_ref = bf16[288,256]{1,0:T(8,128)(2,1)S(1)} all-gather(bf16[144,256]{1,0:T(8,128)(2,1)S(1)} %get-tuple-element.106), channel_id=1, replica_groups={{0,1},{2,3},{4,5},{6,7},{8,9},{10,11},{12,13},{14,15},{16,17},{18,19},{..., dimensions={0}, use_global_device_ids=true | all-gather | bytes 221184 | tf_op jit(solution)/shard_map/all_gather | solution.py:298
  71.0 0.0 collective-permute-done.3.refs_0_
  71.0 4.9 %all-to-all-done.4 = bf16[64,8,256]{2,1,0:T(8,128)(2,1)S(1)} async-done(((bf16[64,8,256]{2,1,0:T(8,128)(2,1)}), bf16[64,8,256]{2,1,0:T(8,128)(2,1)S(1)}, u32[]{:S(2)}, u32[]{:S(2)}) %all-to-all-start.4) | async-done | bytes 262176 | tf_op jit(solution)/shard_map/all_to_all | solution.py:294
  75.9 1.5 layer.13
  77.4 6.0 %all-to-all-start.5 = ((bf16[64,8,256]{2,1,0:T(8,128)(2,1)}), bf16[64,8,256]{2,1,0:T(8,128)(2,1)S(1)}, u32[]{:S(2)}, u32[]{:S(2)}) async-start(bf16[64,8,256]{2,1,0:T(8,128)(2,1)} %bitcast.15), calls=%async_computation.5 | async-start | bytes 524288 | tf_op jit(solution)/shard_map/all_to_all | solution.py:294
  83.4 4.8 %collective-permute-start.4 = (bf16[144,256]{1,0:T(8,128)(2,1)S(1)}, bf16[144,256]{1,0:T(8,128)(2,1)S(1)}, u32[]{:S(2)}, u32[]{:S(2)}) collective-permute-start(bf16[144,256]{1,0:T(8,128)(2,1)S(1)} %get-tuple-element.109), channel_id=1, source_target_pairs={{0,448},{64,0},{128,64},{192,128},{256,192},{320,256},{384,320},{4... | collective-permute-start | bytes 221192 | tf_op jit(solution)/shard_map/ppermute | solution.py:302
  88.2 2.3 %all_gather.24.late_ref.early_ref = bf16[288,256]{1,0:T(8,128)(2,1)S(1)} all-gather(bf16[144,256]{1,0:T(8,128)(2,1)S(1)} %get-tuple-element.109), channel_id=1, replica_groups={{0,1},{2,3},{4,5},{6,7},{8,9},{10,11},{12,13},{14,15},{16,17},{18,19},{..., dimensions={0}, use_global_device_ids=true | all-gather | bytes 221184 | tf_op jit(solution)/shard_map/all_gather | solution.py:298
  90.5 0.0 collective-permute-done.4.refs_0_
  90.5 4.9 %all-to-all-done.5 = bf16[64,8,256]{2,1,0:T(8,128)(2,1)S(1)} async-done(((bf16[64,8,256]{2,1,0:T(8,128)(2,1)}), bf16[64,8,256]{2,1,0:T(8,128)(2,1)S(1)}, u32[]{:S(2)}, u32[]{:S(2)}) %all-to-all-start.5) | async-done | bytes 262176 | tf_op jit(solution)/shard_map/all_to_all | solution.py:294
  95.4 1.5 layer.14
  97.0 6.0 %all-to-all-start.6 = ((bf16[64,8,256]{2,1,0:T(8,128)(2,1)}), bf16[64,8,256]{2,1,0:T(8,128)(2,1)S(1)}, u32[]{:S(2)}, u32[]{:S(2)}) async-start(bf16[64,8,256]{2,1,0:T(8,128)(2,1)} %bitcast.17), calls=%async_computation.6 | async-start | bytes 524288 | tf_op jit(solution)/shard_map/all_to_all | solution.py:294
  103.0 4.8 %collective-permute-start.5 = (bf16[144,256]{1,0:T(8,128)(2,1)S(1)}, bf16[144,256]{1,0:T(8,128)(2,1)S(1)}, u32[]{:S(2)}, u32[]{:S(2)}) collective-permute-start(bf16[144,256]{1,0:T(8,128)(2,1)S(1)} %get-tuple-element.112), channel_id=1, source_target_pairs={{0,448},{64,0},{128,64},{192,128},{256,192},{320,256},{384,320},{4... | collective-permute-start | bytes 221192 | tf_op jit(solution)/shard_map/ppermute | solution.py:302
  107.8 2.3 %all_gather.25.late_ref.early_ref = bf16[288,256]{1,0:T(8,128)(2,1)S(1)} all-gather(bf16[144,256]{1,0:T(8,128)(2,1)S(1)} %get-tuple-element.112), channel_id=1, replica_groups={{0,1},{2,3},{4,5},{6,7},{8,9},{10,11},{12,13},{14,15},{16,17},{18,19},{..., dimensions={0}, use_global_device_ids=true | all-gather | bytes 221184 | tf_op jit(solution)/shard_map/all_gather | solution.py:298
  110.1 0.0 collective-permute-done.5.refs_0_
  110.1 4.9 %all-to-all-done.6 = bf16[64,8,256]{2,1,0:T(8,128)(2,1)S(1)} async-done(((bf16[64,8,256]{2,1,0:T(8,128)(2,1)}), bf16[64,8,256]{2,1,0:T(8,128)(2,1)S(1)}, u32[]{:S(2)}, u32[]{:S(2)}) %all-to-all-start.6) | async-done | bytes 262176 | tf_op jit(solution)/shard_map/all_to_all | solution.py:294
  115.0 1.5 layer.15
  116.5 6.0 %all-to-all-start.7 = ((bf16[64,8,256]{2,1,0:T(8,128)(2,1)}), bf16[64,8,256]{2,1,0:T(8,128)(2,1)S(1)}, u32[]{:S(2)}, u32[]{:S(2)}) async-start(bf16[64,8,256]{2,1,0:T(8,128)(2,1)} %bitcast.19), calls=%async_computation.7 | async-start | bytes 524288 | tf_op jit(solution)/shard_map/all_to_all | solution.py:294
  122.6 4.8 %collective-permute-start.6 = (bf16[144,256]{1,0:T(8,128)(2,1)S(1)}, bf16[144,256]{1,0:T(8,128)(2,1)S(1)}, u32[]{:S(2)}, u32[]{:S(2)}) collective-permute-start(bf16[144,256]{1,0:T(8,128)(2,1)S(1)} %get-tuple-element.115), channel_id=1, source_target_pairs={{0,448},{64,0},{128,64},{192,128},{256,192},{320,256},{384,320},{4... | collective-permute-start | bytes 221192 | tf_op jit(solution)/shard_map/ppermute | solution.py:302
  127.3 2.3 %all_gather.26.late_ref.early_ref = bf16[288,256]{1,0:T(8,128)(2,1)S(1)} all-gather(bf16[144,256]{1,0:T(8,128)(2,1)S(1)} %get-tuple-element.115), channel_id=1, replica_groups={{0,1},{2,3},{4,5},{6,7},{8,9},{10,11},{12,13},{14,15},{16,17},{18,19},{..., dimensions={0}, use_global_device_ids=true | all-gather | bytes 221184 | tf_op jit(solution)/shard_map/all_gather | solution.py:298
  129.6 0.0 collective-permute-done.6.refs_0_
  129.6 4.9 %all-to-all-done.7 = bf16[64,8,256]{2,1,0:T(8,128)(2,1)S(1)} async-done(((bf16[64,8,256]{2,1,0:T(8,128)(2,1)}), bf16[64,8,256]{2,1,0:T(8,128)(2,1)S(1)}, u32[]{:S(2)}, u32[]{:S(2)}) %all-to-all-start.7) | async-done | bytes 262176 | tf_op jit(solution)/shard_map/all_to_all | solution.py:294
  134.6 1.5 layer.16
  136.1 6.0 %all-to-all-start.8 = ((bf16[64,8,256]{2,1,0:T(8,128)(2,1)}), bf16[64,8,256]{2,1,0:T(8,128)(2,1)S(1)}, u32[]{:S(2)}, u32[]{:S(2)}) async-start(bf16[64,8,256]{2,1,0:T(8,128)(2,1)} %bitcast.21), calls=%async_computation.8 | async-start | bytes 524288 | tf_op jit(solution)/shard_map/all_to_all | solution.py:294
  142.1 2.2 %all_gather.27.late_ref = bf16[288,256]{1,0:T(8,128)(2,1)S(1)} all-gather(bf16[144,256]{1,0:T(8,128)(2,1)S(1)} %get-tuple-element.118), channel_id=1, replica_groups={{0,1},{2,3},{4,5},{6,7},{8,9},{10,11},{12,13},{14,15},{16,17},{18,19},{..., dimensions={0}, use_global_device_ids=true | all-gather | bytes 221184 | tf_op jit(solution)/shard_map/all_gather | solution.py:298
  144.3 9.8 %all-to-all-done.8 = bf16[64,8,256]{2,1,0:T(8,128)(2,1)S(1)} async-done(((bf16[64,8,256]{2,1,0:T(8,128)(2,1)}), bf16[64,8,256]{2,1,0:T(8,128)(2,1)S(1)}, u32[]{:S(2)}, u32[]{:S(2)}) %all-to-all-start.8) | async-done | bytes 262176 | tf_op jit(solution)/shard_map/all_to_all | solution.py:294
  154.1 0.8 layer.17
  154.9 1.3 collective-permute-start.7
  156.2 18.4 %conditional.3 = (bf16[256,256]{1,0:T(8,128)(2,1)S(1)}) conditional(s32[]{:T(128)} %convert_element_type.7, () %tuple.19, (bf16[512,256]{1,0:T(8,128)(2,1)S(1)}, s32[1]{0:T(128)}, bf16[256,256]{1,0:T(8,128)(2,1)S(1)}, bf16[256,256]{1,0:T(8,128)(2,1)S(1)}, bf16[256,512]{1,0:T(8,128)(2,1)S(1)}, /*index=5*/f32[256,128]{1,0:T(8,128)S(1)}, ...), branch_computations={%region_2.3_spmd, %region_3.4_spmd} | conditional | bytes 524296 | solution.py:322
  156.2 17.8 %all_to_all.44 = bf16[64,8,256]{2,1,0:T(8,128)(2,1)S(1)} all-to-all(bf16[64,8,256]{2,1,0:T(8,128)(2,1)S(1)} %bitcast.29), channel_id=1, replica_groups=mesh['layer'=8,'dom'=64] {'dom'}, dimensions={0} | all-to-all | bytes 524288 | tf_op jit(solution)/shard_map/cond/branch_1_fun/all_to_all | solution.py:315
  174.1 0.5 layer.10
  174.6 0.0 collective-permute-done.7
  174.6 1.3 collective-permute-start.8
  176.0 2.7 %collective-permute-done.8 = bf16[256,256]{1,0:T(8,128)(2,1)S(1)} collective-permute-done((bf16[256,256]{1,0:T(8,128)(2,1)S(1)}, bf16[256,256]{1,0:T(8,128)(2,1)S(1)}, u32[]{:S(2)}, u32[]{:S(2)}) %collective-permute-start.8) | collective-permute-done | bytes 131104 | tf_op jit(solution)/shard_map/ppermute | solution.py:323
  178.7 0.7 maximum_bitcast_fusion
  (5 shorter events, 0.1 us)
Async XLA Ops:
  0.0 27.0 %copy-start.3 = (s32[2,1,64,8]{2,3,1,0:T(8,128)S(1)}, s32[2,1,64,8]{2,3,1,0:T(8,128)}, u32[]{:S(2)}) copy-start(s32[2,1,64,8]{2,3,1,0:T(8,128)} %param.18) | copy-start | bytes 12292
  0.0 27.0 %copy-start.4 = (s32[2,1,64,8]{2,3,1,0:T(8,128)S(1)}, s32[2,1,64,8]{2,3,1,0:T(8,128)}, u32[]{:S(2)}) copy-start(s32[2,1,64,8]{2,3,1,0:T(8,128)} %param.19) | copy-start | bytes 12292
  2.4 24.7 %copy-start.1 = (bf16[2,256,256]{2,1,0:T(8,128)(2,1)S(1)}, bf16[2,256,256]{2,1,0:T(8,128)(2,1)}, u32[]{:S(2)}) copy-start(bf16[2,256,256]{2,1,0:T(8,128)(2,1)} %features_ref.3) | copy-start | bytes 786436
  2.4 24.7 %copy-start.2 = (bf16[512,256]{1,0:T(8,128)(2,1)S(1)}, bf16[512,256]{1,0:T(8,128)(2,1)}, u32[]{:S(2)}) copy-start(bf16[512,256]{1,0:T(8,128)(2,1)} %get-tuple-element.93.after_ref) | copy-start | bytes 786436
  2.4 29.6 %all-to-all-start.2 = ((bf16[64,8,256]{2,1,0:T(8,128)(2,1)}), bf16[64,8,256]{2,1,0:T(8,128)(2,1)S(1)}, u32[]{:S(2)}, u32[]{:S(2)}) async-start(bf16[64,8,256]{2,1,0:T(8,128)(2,1)} %bitcast.32), calls=%async_computation.2 | async-start | bytes 524288 | tf_op jit(solution)/shard_map/all_to_all | solution.py:294
  14.2 12.9 %copy-start.5 = (s32[2,2,4]{2,1,0:T(2,128)S(1)}, s32[2,2,4]{2,1,0:T(2,128)}, u32[]{:S(2)}) copy-start(s32[2,2,4]{2,1,0:T(2,128)} %col_ref.1) | copy-start | bytes 196
  14.2 15.3 %collective-permute-start = (bf16[144,256]{1,0:T(8,128)(2,1)}, bf16[144,256]{1,0:T(8,128)(2,1)S(1)}, u32[]{:S(2)}, u32[]{:S(2)}) collective-permute-start(bf16[144,256]{1,0:T(8,128)(2,1)} %get-tuple-element.100), channel_id=1, source_target_pairs={{0,448},{64,0},{128,64},{192,128},{256,192},{320,256},{384,320},{4... | collective-permute-start | bytes 221192 | tf_op jit(solution)/shard_map/ppermute | solution.py:297
  24.8 7.2 %collective-permute-start.1 = (bf16[144,256]{1,0:T(8,128)(2,1)}, bf16[144,256]{1,0:T(8,128)(2,1)S(1)}, u32[]{:S(2)}, u32[]{:S(2)}) collective-permute-start(bf16[144,256]{1,0:T(8,128)(2,1)} %get-tuple-element.100), channel_id=1, source_target_pairs={{0,384},{64,448},{128,0},{192,64},{256,128},{320,192},{384,256},{4... | collective-permute-start | bytes 221192 | tf_op jit(solution)/shard_map/ppermute | solution.py:302
  27.1 1.2 copy-start
  33.6 22.8 %all-to-all-start.3 = ((bf16[64,8,256]{2,1,0:T(8,128)(2,1)}), bf16[64,8,256]{2,1,0:T(8,128)(2,1)S(1)}, u32[]{:S(2)}, u32[]{:S(2)}) async-start(bf16[64,8,256]{2,1,0:T(8,128)(2,1)} %bitcast.11), calls=%async_computation.3 | async-start | bytes 524288 | tf_op jit(solution)/shard_map/all_to_all | solution.py:294
  44.3 7.1 %collective-permute-start.2 = (bf16[144,256]{1,0:T(8,128)(2,1)S(1)}, bf16[144,256]{1,0:T(8,128)(2,1)S(1)}, u32[]{:S(2)}, u32[]{:S(2)}) collective-permute-start(bf16[144,256]{1,0:T(8,128)(2,1)S(1)} %get-tuple-element.103), channel_id=1, source_target_pairs={{0,448},{64,0},{128,64},{192,128},{256,192},{320,256},{384,320},{4... | collective-permute-start | bytes 221192 | tf_op jit(solution)/shard_map/ppermute | solution.py:302
  57.9 18.0 %all-to-all-start.4 = ((bf16[64,8,256]{2,1,0:T(8,128)(2,1)}), bf16[64,8,256]{2,1,0:T(8,128)(2,1)S(1)}, u32[]{:S(2)}, u32[]{:S(2)}) async-start(bf16[64,8,256]{2,1,0:T(8,128)(2,1)} %bitcast.13), calls=%async_computation.4 | async-start | bytes 524288 | tf_op jit(solution)/shard_map/all_to_all | solution.py:294
  63.9 7.1 %collective-permute-start.3 = (bf16[144,256]{1,0:T(8,128)(2,1)S(1)}, bf16[144,256]{1,0:T(8,128)(2,1)S(1)}, u32[]{:S(2)}, u32[]{:S(2)}) collective-permute-start(bf16[144,256]{1,0:T(8,128)(2,1)S(1)} %get-tuple-element.106), channel_id=1, source_target_pairs={{0,448},{64,0},{128,64},{192,128},{256,192},{320,256},{384,320},{4... | collective-permute-start | bytes 221192 | tf_op jit(solution)/shard_map/ppermute | solution.py:302
  77.4 18.0 %all-to-all-start.5 = ((bf16[64,8,256]{2,1,0:T(8,128)(2,1)}), bf16[64,8,256]{2,1,0:T(8,128)(2,1)S(1)}, u32[]{:S(2)}, u32[]{:S(2)}) async-start(bf16[64,8,256]{2,1,0:T(8,128)(2,1)} %bitcast.15), calls=%async_computation.5 | async-start | bytes 524288 | tf_op jit(solution)/shard_map/all_to_all | solution.py:294
  83.4 7.1 %collective-permute-start.4 = (bf16[144,256]{1,0:T(8,128)(2,1)S(1)}, bf16[144,256]{1,0:T(8,128)(2,1)S(1)}, u32[]{:S(2)}, u32[]{:S(2)}) collective-permute-start(bf16[144,256]{1,0:T(8,128)(2,1)S(1)} %get-tuple-element.109), channel_id=1, source_target_pairs={{0,448},{64,0},{128,64},{192,128},{256,192},{320,256},{384,320},{4... | collective-permute-start | bytes 221192 | tf_op jit(solution)/shard_map/ppermute | solution.py:302
  97.0 18.0 %all-to-all-start.6 = ((bf16[64,8,256]{2,1,0:T(8,128)(2,1)}), bf16[64,8,256]{2,1,0:T(8,128)(2,1)S(1)}, u32[]{:S(2)}, u32[]{:S(2)}) async-start(bf16[64,8,256]{2,1,0:T(8,128)(2,1)} %bitcast.17), calls=%async_computation.6 | async-start | bytes 524288 | tf_op jit(solution)/shard_map/all_to_all | solution.py:294
  103.0 7.1 %collective-permute-start.5 = (bf16[144,256]{1,0:T(8,128)(2,1)S(1)}, bf16[144,256]{1,0:T(8,128)(2,1)S(1)}, u32[]{:S(2)}, u32[]{:S(2)}) collective-permute-start(bf16[144,256]{1,0:T(8,128)(2,1)S(1)} %get-tuple-element.112), channel_id=1, source_target_pairs={{0,448},{64,0},{128,64},{192,128},{256,192},{320,256},{384,320},{4... | collective-permute-start | bytes 221192 | tf_op jit(solution)/shard_map/ppermute | solution.py:302
  116.5 18.0 %all-to-all-start.7 = ((bf16[64,8,256]{2,1,0:T(8,128)(2,1)}), bf16[64,8,256]{2,1,0:T(8,128)(2,1)S(1)}, u32[]{:S(2)}, u32[]{:S(2)}) async-start(bf16[64,8,256]{2,1,0:T(8,128)(2,1)} %bitcast.19), calls=%async_computation.7 | async-start | bytes 524288 | tf_op jit(solution)/shard_map/all_to_all | solution.py:294
  122.6 7.1 %collective-permute-start.6 = (bf16[144,256]{1,0:T(8,128)(2,1)S(1)}, bf16[144,256]{1,0:T(8,128)(2,1)S(1)}, u32[]{:S(2)}, u32[]{:S(2)}) collective-permute-start(bf16[144,256]{1,0:T(8,128)(2,1)S(1)} %get-tuple-element.115), channel_id=1, source_target_pairs={{0,448},{64,0},{128,64},{192,128},{256,192},{320,256},{384,320},{4... | collective-permute-start | bytes 221192 | tf_op jit(solution)/shard_map/ppermute | solution.py:302
  136.1 18.0 %all-to-all-start.8 = ((bf16[64,8,256]{2,1,0:T(8,128)(2,1)}), bf16[64,8,256]{2,1,0:T(8,128)(2,1)S(1)}, u32[]{:S(2)}, u32[]{:S(2)}) async-start(bf16[64,8,256]{2,1,0:T(8,128)(2,1)} %bitcast.21), calls=%async_computation.8 | async-start | bytes 524288 | tf_op jit(solution)/shard_map/all_to_all | solution.py:294
  154.9 19.7 %collective-permute-start.7 = (bf16[256,256]{1,0:T(8,128)(2,1)S(1)}, bf16[256,256]{1,0:T(8,128)(2,1)S(1)}, u32[]{:S(2)}, u32[]{:S(2)}) collective-permute-start(bf16[256,256]{1,0:T(8,128)(2,1)S(1)} %get-tuple-element.120), channel_id=1, source_target_pairs={{64,0},{128,64},{192,128},{256,192},{320,256},{384,320},{448,384},... | collective-permute-start | bytes 393224 | tf_op jit(solution)/shard_map/ppermute | solution.py:312
  174.6 4.0 %collective-permute-start.8 = (bf16[256,256]{1,0:T(8,128)(2,1)S(1)}, bf16[256,256]{1,0:T(8,128)(2,1)S(1)}, u32[]{:S(2)}, u32[]{:S(2)}) collective-permute-start(bf16[256,256]{1,0:T(8,128)(2,1)S(1)} %broadcast_select_fusion.1), channel_id=1, source_target_pairs={{0,448},{1,449},{2,450},{3,451},{4,452},{5,453},{6,454},{7,455},{8... | collective-permute-start | bytes 393224 | tf_op jit(solution)/shard_map/ppermute | solution.py:323

commit v5 on v4

--- a/solution.py
+++ b/solution.py
@@ -15,6 +15,7 @@
 PARAMS = pltpu.CompilerParams(vmem_limit_bytes=KERNEL_VMEM)
 WIDE_PARAMS = pltpu.CompilerParams(vmem_limit_bytes=56 * 2**20)
 CHUNKS = 4
+FIRST = 40
 
 
 def slot_column(table):
@@ -22,7 +23,7 @@
     rows = count * slots
     expand = (
         lax.broadcasted_iota(jnp.int32, (rows, count), 0) // slots
-        == lax.broadcasted_iota(jnp.int32, (rows, count), 1)
+        == (lax.broadcasted_iota(jnp.int32, (rows, count), 1) ^ FIRST)
     ).astype(jnp.bfloat16)
     spread = lax.dot_general(
         expand,
@@ -279,6 +280,7 @@
     peers, slots = send_rows.shape[2:]
     width = features.shape[-1]
     plane = index.reshape(1)
+    order = [[i ^ FIRST for i in range(peers)]]
     core = (lax.axis_index("dom") % 2).reshape(1)
     span = (index % 2).reshape(1)
     cores = [[2 * chip, 2 * chip + 1] for chip in range(peers // 2)]
@@ -291,7 +293,7 @@
     *tables, hidden = build_tables(span, tile_col, tile_adj, recv_dst, send_rows, features, outgoing)
     early = own_pack
     for step in range(layers - 1):
-        arrived = lax.all_to_all(outgoing.reshape(peers, slots, width), "dom", 0, 0, tiled=True)
+        arrived = lax.all_to_all(outgoing.reshape(peers, slots, width), "dom", 0, 0, axis_index_groups=order, tiled=True)
         arrived = arrived.reshape(peers * slots, width)
         if step == 0:
             half = lax.ppermute(own_half, "layer", down)
@@ -312,7 +314,7 @@
     from_above = lax.ppermute(hidden, "layer", down[1:])
 
     def finish(outgoing, hidden):
-        arrived = lax.all_to_all(outgoing.reshape(peers, slots, width), "dom", 0, 0, tiled=True)
+        arrived = lax.all_to_all(outgoing.reshape(peers, slots, width), "dom", 0, 0, axis_index_groups=order, tiled=True)
         arrived = arrived.reshape(peers * slots, width)
         return run_layer(last, layers, plane, hidden, arrived, tables, early, own_pack)[0]
 

time: 180 us -> 177 us (0.983)
  waiting for transfers between devices: 37.1 us -> 7.33 us
  starting transfers between devices: 92 us -> 119 us
    all_to_all x7, waiting for transfers between devices: 34.4 us -> 4.58 us  [local(): lax.all_to_all(outgoing.reshape(peers, slots, width), 'dom', 0, 0, axis_i...]
    all_to_all x7, starting transfers between devices: 52.7 us -> 82.5 us  [local(): lax.all_to_all(outgoing.reshape(peers, slots, width), 'dom', 0, 0, axis_i...]
    ppermute x1, starting transfers between devices: 10.7 us -> 7.58 us  [local(): half = lax.ppermute(own_half, 'layer', down)]
  transfers between devices with their start and end apart: 16 -> 16, of which waited for: 7 -> 2; matrix products, arithmetic and copies ran while one was open for 0% -> 0% of each run, Pallas kernels for 1% -> 1%
where the time goes in v5:
time: 177 us; the launch traced here: 176 us
  starting transfers between devices  119 us (67%)
  blocking collectives  33.3 us (19%)
  Pallas kernels  13.9 us (8%)
  waiting for transfers between devices  7.33 us (4%)
    all_to_all x7, starting transfers between devices, local(): lax.all_to_all(outgoing.reshape(peers, slots, width), 'dom', 0, 0, axis_i...  82.5 us
    ppermute x6, starting transfers between devices, local(): passed = [lax.ppermute(source, 'layer', pairs)]  26.1 us
    all_to_all x1, blocking collectives, finish(): lax.all_to_all(outgoing.reshape(peers, slots, width), 'dom', 0, 0, axis_i...  17.7 us
    all_gather x7, blocking collectives, local(): late = lax.all_gather(half, 'dom', axis_index_groups=cores, tiled=True)  15.6 us
    pallas_call x8, Pallas kernels, run_layer(): pl.pallas_call(functools.partial(layer_kernel, step, layers, len(passed))...  10.4 us
    ppermute x1, starting transfers between devices, local(): half = lax.ppermute(own_half, 'layer', down)  7.58 us
    all_to_all x7, waiting for transfers between devices, local(): lax.all_to_all(outgoing.reshape(peers, slots, width), 'dom', 0, 0, axis_i...  4.58 us
  transfers between devices with their start and end apart: 16, of which 2 were waited for; matrix products, arithmetic and copies ran while one was open for 0% of the time, Pallas kernels for 1%

profile of v5, /device:TPU:1, one launch (start us, length us, event | category | flops | bytes accessed | tf_op | source)
XLA Modules:
  0.0 175.6 jit_solution(5647692173131721025)
XLA Ops:
  0.0 0.0 copy-start.3
  0.0 0.0 copy-start.4
  0.0 2.4 %first_gather.1 = (bf16[512,256]{1,0:T(8,128)(2,1)}, bf16[288,256]{1,0:T(8,128)(2,1)S(1)}, bf16[144,256]{1,0:T(8,128)(2,1)}) custom-call(s32[1]{0:T(128)} %bitcast.5.span_ref, s32[1]{0:T(128)} %bitcast.8.core_ref, bf16[2,256,256]{2,1,0:T(8,128)(2,1)} %features_ref.3, s32[2,1,8,64]{3,2,1,0:T(8,128)} %bitcast.41, bf16[1,256,256]{2,1,0:T(8,128)(2,1)} %weight_ref.1, ...), custom_call_target="tpu_custom_call" | custom-call | tf_op jit(solution)/shard_map/first_gather/pallas_call | solution.py:114
  2.4 0.0 copy-start.1
  2.4 0.0 copy-start.2
  2.4 17.0 %all-to-all-start.2 = ((bf16[64,8,256]{2,1,0:T(8,128)(2,1)}), bf16[64,8,256]{2,1,0:T(8,128)(2,1)S(1)}, u32[]{:S(2)}, u32[]{:S(2)}) async-start(bf16[64,8,256]{2,1,0:T(8,128)(2,1)} %bitcast.32), calls=%async_computation.2 | async-start | bytes 524288 | tf_op jit(solution)/shard_map/all_to_all | solution.py:296
  19.4 0.0 copy-start.5
  19.4 7.6 %collective-permute-start = (bf16[144,256]{1,0:T(8,128)(2,1)}, bf16[144,256]{1,0:T(8,128)(2,1)S(1)}, u32[]{:S(2)}, u32[]{:S(2)}) collective-permute-start(bf16[144,256]{1,0:T(8,128)(2,1)} %get-tuple-element.100), channel_id=1, source_target_pairs={{0,448},{64,0},{128,64},{192,128},{256,192},{320,256},{384,320},{4... | collective-permute-start | bytes 221192 | tf_op jit(solution)/shard_map/ppermute | solution.py:299
  27.0 2.2 %collective-permute-start.1 = (bf16[144,256]{1,0:T(8,128)(2,1)}, bf16[144,256]{1,0:T(8,128)(2,1)S(1)}, u32[]{:S(2)}, u32[]{:S(2)}) collective-permute-start(bf16[144,256]{1,0:T(8,128)(2,1)} %get-tuple-element.100), channel_id=1, source_target_pairs={{0,384},{64,448},{128,0},{192,64},{256,128},{320,192},{384,256},{4... | collective-permute-start | bytes 221192 | tf_op jit(solution)/shard_map/ppermute | solution.py:304
  29.2 0.0 copy-done.3
  29.2 0.0 copy-done.4
  29.2 0.0 copy-done.1
  29.2 0.0 copy-done.2
  29.2 0.0 copy-done.5
  29.2 0.0 copy-start
  29.2 1.2 copy-done
  30.4 1.1 build_tables.1
  31.6 0.0 collective-permute-done
  31.6 2.5 %all_gather.21.late_ref.early_ref = bf16[288,256]{1,0:T(8,128)(2,1)S(1)} all-gather(bf16[144,256]{1,0:T(8,128)(2,1)S(1)} %collective-permute-done), channel_id=1, replica_groups={{0,1},{2,3},{4,5},{6,7},{8,9},{10,11},{12,13},{14,15},{16,17},{18,19},{..., dimensions={0}, use_global_device_ids=true | all-gather | bytes 221184 | tf_op jit(solution)/shard_map/all_gather | solution.py:300
  34.1 0.0 collective-permute-done.1.refs_0_
  34.1 0.0 all-to-all-done.2
  34.1 1.5 layer.11
  35.6 10.9 %all-to-all-start.3 = ((bf16[64,8,256]{2,1,0:T(8,128)(2,1)}), bf16[64,8,256]{2,1,0:T(8,128)(2,1)S(1)}, u32[]{:S(2)}, u32[]{:S(2)}) async-start(bf16[64,8,256]{2,1,0:T(8,128)(2,1)} %bitcast.11), calls=%async_computation.3 | async-start | bytes 524288 | tf_op jit(solution)/shard_map/all_to_all | solution.py:296
  46.5 4.8 %collective-permute-start.2 = (bf16[144,256]{1,0:T(8,128)(2,1)S(1)}, bf16[144,256]{1,0:T(8,128)(2,1)S(1)}, u32[]{:S(2)}, u32[]{:S(2)}) collective-permute-start(bf16[144,256]{1,0:T(8,128)(2,1)S(1)} %get-tuple-element.103), channel_id=1, source_target_pairs={{0,448},{64,0},{128,64},{192,128},{256,192},{320,256},{384,320},{4... | collective-permute-start | bytes 221192 | tf_op jit(solution)/shard_map/ppermute | solution.py:304
  51.3 2.2 %all_gather.22.late_ref.early_ref = bf16[288,256]{1,0:T(8,128)(2,1)S(1)} all-gather(bf16[144,256]{1,0:T(8,128)(2,1)S(1)} %get-tuple-element.103), channel_id=1, replica_groups={{0,1},{2,3},{4,5},{6,7},{8,9},{10,11},{12,13},{14,15},{16,17},{18,19},{..., dimensions={0}, use_global_device_ids=true | all-gather | bytes 221184 | tf_op jit(solution)/shard_map/all_gather | solution.py:300
  53.5 0.0 collective-permute-done.2.refs_0_
  53.5 0.0 all-to-all-done.3
  53.5 1.5 layer.12
  55.0 10.9 %all-to-all-start.4 = ((bf16[64,8,256]{2,1,0:T(8,128)(2,1)}), bf16[64,8,256]{2,1,0:T(8,128)(2,1)S(1)}, u32[]{:S(2)}, u32[]{:S(2)}) async-start(bf16[64,8,256]{2,1,0:T(8,128)(2,1)} %bitcast.13), calls=%async_computation.4 | async-start | bytes 524288 | tf_op jit(solution)/shard_map/all_to_all | solution.py:296
  65.9 4.8 %collective-permute-start.3 = (bf16[144,256]{1,0:T(8,128)(2,1)S(1)}, bf16[144,256]{1,0:T(8,128)(2,1)S(1)}, u32[]{:S(2)}, u32[]{:S(2)}) collective-permute-start(bf16[144,256]{1,0:T(8,128)(2,1)S(1)} %get-tuple-element.106), channel_id=1, source_target_pairs={{0,448},{64,0},{128,64},{192,128},{256,192},{320,256},{384,320},{4... | collective-permute-start | bytes 221192 | tf_op jit(solution)/shard_map/ppermute | solution.py:304
  70.7 2.2 %all_gather.23.late_ref.early_ref = bf16[288,256]{1,0:T(8,128)(2,1)S(1)} all-gather(bf16[144,256]{1,0:T(8,128)(2,1)S(1)} %get-tuple-element.106), channel_id=1, replica_groups={{0,1},{2,3},{4,5},{6,7},{8,9},{10,11},{12,13},{14,15},{16,17},{18,19},{..., dimensions={0}, use_global_device_ids=true | all-gather | bytes 221184 | tf_op jit(solution)/shard_map/all_gather | solution.py:300
  72.9 0.0 collective-permute-done.3.refs_0_
  72.9 0.0 all-to-all-done.4
  72.9 1.5 layer.13
  74.4 10.9 %all-to-all-start.5 = ((bf16[64,8,256]{2,1,0:T(8,128)(2,1)}), bf16[64,8,256]{2,1,0:T(8,128)(2,1)S(1)}, u32[]{:S(2)}, u32[]{:S(2)}) async-start(bf16[64,8,256]{2,1,0:T(8,128)(2,1)} %bitcast.15), calls=%async_computation.5 | async-start | bytes 524288 | tf_op jit(solution)/shard_map/all_to_all | solution.py:296
  85.4 4.8 %collective-permute-start.4 = (bf16[144,256]{1,0:T(8,128)(2,1)S(1)}, bf16[144,256]{1,0:T(8,128)(2,1)S(1)}, u32[]{:S(2)}, u32[]{:S(2)}) collective-permute-start(bf16[144,256]{1,0:T(8,128)(2,1)S(1)} %get-tuple-element.109), channel_id=1, source_target_pairs={{0,448},{64,0},{128,64},{192,128},{256,192},{320,256},{384,320},{4... | collective-permute-start | bytes 221192 | tf_op jit(solution)/shard_map/ppermute | solution.py:304
  90.1 2.2 %all_gather.24.late_ref.early_ref = bf16[288,256]{1,0:T(8,128)(2,1)S(1)} all-gather(bf16[144,256]{1,0:T(8,128)(2,1)S(1)} %get-tuple-element.109), channel_id=1, replica_groups={{0,1},{2,3},{4,5},{6,7},{8,9},{10,11},{12,13},{14,15},{16,17},{18,19},{..., dimensions={0}, use_global_device_ids=true | all-gather | bytes 221184 | tf_op jit(solution)/shard_map/all_gather | solution.py:300
  92.3 0.0 collective-permute-done.4.refs_0_
  92.3 0.0 all-to-all-done.5
  92.4 1.5 layer.14
  93.9 10.9 %all-to-all-start.6 = ((bf16[64,8,256]{2,1,0:T(8,128)(2,1)}), bf16[64,8,256]{2,1,0:T(8,128)(2,1)S(1)}, u32[]{:S(2)}, u32[]{:S(2)}) async-start(bf16[64,8,256]{2,1,0:T(8,128)(2,1)} %bitcast.17), calls=%async_computation.6 | async-start | bytes 524288 | tf_op jit(solution)/shard_map/all_to_all | solution.py:296
  104.8 4.8 %collective-permute-start.5 = (bf16[144,256]{1,0:T(8,128)(2,1)S(1)}, bf16[144,256]{1,0:T(8,128)(2,1)S(1)}, u32[]{:S(2)}, u32[]{:S(2)}) collective-permute-start(bf16[144,256]{1,0:T(8,128)(2,1)S(1)} %get-tuple-element.112), channel_id=1, source_target_pairs={{0,448},{64,0},{128,64},{192,128},{256,192},{320,256},{384,320},{4... | collective-permute-start | bytes 221192 | tf_op jit(solution)/shard_map/ppermute | solution.py:304
  109.6 2.2 %all_gather.25.late_ref.early_ref = bf16[288,256]{1,0:T(8,128)(2,1)S(1)} all-gather(bf16[144,256]{1,0:T(8,128)(2,1)S(1)} %get-tuple-element.112), channel_id=1, replica_groups={{0,1},{2,3},{4,5},{6,7},{8,9},{10,11},{12,13},{14,15},{16,17},{18,19},{..., dimensions={0}, use_global_device_ids=true | all-gather | bytes 221184 | tf_op jit(solution)/shard_map/all_gather | solution.py:300
  111.8 0.0 collective-permute-done.5.refs_0_
  111.8 0.0 all-to-all-done.6
  111.8 1.5 layer.15
  113.3 10.9 %all-to-all-start.7 = ((bf16[64,8,256]{2,1,0:T(8,128)(2,1)}), bf16[64,8,256]{2,1,0:T(8,128)(2,1)S(1)}, u32[]{:S(2)}, u32[]{:S(2)}) async-start(bf16[64,8,256]{2,1,0:T(8,128)(2,1)} %bitcast.19), calls=%async_computation.7 | async-start | bytes 524288 | tf_op jit(solution)/shard_map/all_to_all | solution.py:296
  124.2 4.8 %collective-permute-start.6 = (bf16[144,256]{1,0:T(8,128)(2,1)S(1)}, bf16[144,256]{1,0:T(8,128)(2,1)S(1)}, u32[]{:S(2)}, u32[]{:S(2)}) collective-permute-start(bf16[144,256]{1,0:T(8,128)(2,1)S(1)} %get-tuple-element.115), channel_id=1, source_target_pairs={{0,448},{64,0},{128,64},{192,128},{256,192},{320,256},{384,320},{4... | collective-permute-start | bytes 221192 | tf_op jit(solution)/shard_map/ppermute | solution.py:304
  129.0 2.2 %all_gather.26.late_ref.early_ref = bf16[288,256]{1,0:T(8,128)(2,1)S(1)} all-gather(bf16[144,256]{1,0:T(8,128)(2,1)S(1)} %get-tuple-element.115), channel_id=1, replica_groups={{0,1},{2,3},{4,5},{6,7},{8,9},{10,11},{12,13},{14,15},{16,17},{18,19},{..., dimensions={0}, use_global_device_ids=true | all-gather | bytes 221184 | tf_op jit(solution)/shard_map/all_gather | solution.py:300
  131.2 0.0 collective-permute-done.6.refs_0_
  131.2 0.0 all-to-all-done.7
  131.2 1.5 layer.16
  132.8 10.9 %all-to-all-start.8 = ((bf16[64,8,256]{2,1,0:T(8,128)(2,1)}), bf16[64,8,256]{2,1,0:T(8,128)(2,1)S(1)}, u32[]{:S(2)}, u32[]{:S(2)}) async-start(bf16[64,8,256]{2,1,0:T(8,128)(2,1)} %bitcast.21), calls=%async_computation.8 | async-start | bytes 524288 | tf_op jit(solution)/shard_map/all_to_all | solution.py:296
  143.7 2.1 %all_gather.27.late_ref = bf16[288,256]{1,0:T(8,128)(2,1)S(1)} all-gather(bf16[144,256]{1,0:T(8,128)(2,1)S(1)} %get-tuple-element.118), channel_id=1, replica_groups={{0,1},{2,3},{4,5},{6,7},{8,9},{10,11},{12,13},{14,15},{16,17},{18,19},{..., dimensions={0}, use_global_device_ids=true | all-gather | bytes 221184 | tf_op jit(solution)/shard_map/all_gather | solution.py:300
  145.8 4.6 %all-to-all-done.8 = bf16[64,8,256]{2,1,0:T(8,128)(2,1)S(1)} async-done(((bf16[64,8,256]{2,1,0:T(8,128)(2,1)}), bf16[64,8,256]{2,1,0:T(8,128)(2,1)S(1)}, u32[]{:S(2)}, u32[]{:S(2)}) %all-to-all-start.8) | async-done | bytes 262176 | tf_op jit(solution)/shard_map/all_to_all | solution.py:296
  150.4 0.8 layer.17
  151.2 1.3 collective-permute-start.7
  152.5 18.2 %conditional.3 = (bf16[256,256]{1,0:T(8,128)(2,1)S(1)}) conditional(s32[]{:T(128)} %convert_element_type.7, () %tuple.19, (bf16[512,256]{1,0:T(8,128)(2,1)S(1)}, s32[1]{0:T(128)}, bf16[256,256]{1,0:T(8,128)(2,1)S(1)}, bf16[256,256]{1,0:T(8,128)(2,1)S(1)}, bf16[256,512]{1,0:T(8,128)(2,1)S(1)}, /*index=5*/f32[256,128]{1,0:T(8,128)S(1)}, ...), branch_computations={%region_2.3_spmd, %region_3.4_spmd} | conditional | bytes 524296 | solution.py:324
  152.5 17.7 %all_to_all.44 = bf16[64,8,256]{2,1,0:T(8,128)(2,1)S(1)} all-to-all(bf16[64,8,256]{2,1,0:T(8,128)(2,1)S(1)} %bitcast.29), channel_id=1, replica_groups={{40,41,42,43,44,45,46,47,32,33,34,35,36,37,38,39,56,57,58,59,60,61,62,6..., dimensions={0} | all-to-all | bytes 524288 | tf_op jit(solution)/shard_map/cond/branch_1_fun/all_to_all | solution.py:317
  170.2 0.5 layer.10
  170.7 0.0 collective-permute-done.7
  170.8 1.3 collective-permute-start.8
  172.1 2.7 %collective-permute-done.8 = bf16[256,256]{1,0:T(8,128)(2,1)S(1)} collective-permute-done((bf16[256,256]{1,0:T(8,128)(2,1)S(1)}, bf16[256,256]{1,0:T(8,128)(2,1)S(1)}, u32[]{:S(2)}, u32[]{:S(2)}) %collective-permute-start.8) | collective-permute-done | bytes 131104 | tf_op jit(solution)/shard_map/ppermute | solution.py:325
  174.9 0.7 maximum_bitcast_fusion
  (5 shorter events, 0.1 us)
Async XLA Ops:
  0.0 29.2 %copy-start.3 = (s32[2,1,64,8]{2,3,1,0:T(8,128)S(1)}, s32[2,1,64,8]{2,3,1,0:T(8,128)}, u32[]{:S(2)}) copy-start(s32[2,1,64,8]{2,3,1,0:T(8,128)} %param.18) | copy-start | bytes 12292
  0.0 29.2 %copy-start.4 = (s32[2,1,64,8]{2,3,1,0:T(8,128)S(1)}, s32[2,1,64,8]{2,3,1,0:T(8,128)}, u32[]{:S(2)}) copy-start(s32[2,1,64,8]{2,3,1,0:T(8,128)} %param.19) | copy-start | bytes 12292
  2.4 26.8 %copy-start.1 = (bf16[2,256,256]{2,1,0:T(8,128)(2,1)S(1)}, bf16[2,256,256]{2,1,0:T(8,128)(2,1)}, u32[]{:S(2)}) copy-start(bf16[2,256,256]{2,1,0:T(8,128)(2,1)} %features_ref.3) | copy-start | bytes 786436
  2.4 26.8 %copy-start.2 = (bf16[512,256]{1,0:T(8,128)(2,1)S(1)}, bf16[512,256]{1,0:T(8,128)(2,1)}, u32[]{:S(2)}) copy-start(bf16[512,256]{1,0:T(8,128)(2,1)} %get-tuple-element.93.after_ref) | copy-start | bytes 786436
  2.4 31.7 %all-to-all-start.2 = ((bf16[64,8,256]{2,1,0:T(8,128)(2,1)}), bf16[64,8,256]{2,1,0:T(8,128)(2,1)S(1)}, u32[]{:S(2)}, u32[]{:S(2)}) async-start(bf16[64,8,256]{2,1,0:T(8,128)(2,1)} %bitcast.32), calls=%async_computation.2 | async-start | bytes 524288 | tf_op jit(solution)/shard_map/all_to_all | solution.py:296
  19.4 9.8 %copy-start.5 = (s32[2,2,4]{2,1,0:T(2,128)S(1)}, s32[2,2,4]{2,1,0:T(2,128)}, u32[]{:S(2)}) copy-start(s32[2,2,4]{2,1,0:T(2,128)} %col_ref.1) | copy-start | bytes 196
  19.4 12.2 %collective-permute-start = (bf16[144,256]{1,0:T(8,128)(2,1)}, bf16[144,256]{1,0:T(8,128)(2,1)S(1)}, u32[]{:S(2)}, u32[]{:S(2)}) collective-permute-start(bf16[144,256]{1,0:T(8,128)(2,1)} %get-tuple-element.100), channel_id=1, source_target_pairs={{0,448},{64,0},{128,64},{192,128},{256,192},{320,256},{384,320},{4... | collective-permute-start | bytes 221192 | tf_op jit(solution)/shard_map/ppermute | solution.py:299
  27.0 7.1 %collective-permute-start.1 = (bf16[144,256]{1,0:T(8,128)(2,1)}, bf16[144,256]{1,0:T(8,128)(2,1)S(1)}, u32[]{:S(2)}, u32[]{:S(2)}) collective-permute-start(bf16[144,256]{1,0:T(8,128)(2,1)} %get-tuple-element.100), channel_id=1, source_target_pairs={{0,384},{64,448},{128,0},{192,64},{256,128},{320,192},{384,256},{4... | collective-permute-start | bytes 221192 | tf_op jit(solution)/shard_map/ppermute | solution.py:304
  29.2 1.2 copy-start
  35.6 17.9 %all-to-all-start.3 = ((bf16[64,8,256]{2,1,0:T(8,128)(2,1)}), bf16[64,8,256]{2,1,0:T(8,128)(2,1)S(1)}, u32[]{:S(2)}, u32[]{:S(2)}) async-start(bf16[64,8,256]{2,1,0:T(8,128)(2,1)} %bitcast.11), calls=%async_computation.3 | async-start | bytes 524288 | tf_op jit(solution)/shard_map/all_to_all | solution.py:296
  46.5 7.0 %collective-permute-start.2 = (bf16[144,256]{1,0:T(8,128)(2,1)S(1)}, bf16[144,256]{1,0:T(8,128)(2,1)S(1)}, u32[]{:S(2)}, u32[]{:S(2)}) collective-permute-start(bf16[144,256]{1,0:T(8,128)(2,1)S(1)} %get-tuple-element.103), channel_id=1, source_target_pairs={{0,448},{64,0},{128,64},{192,128},{256,192},{320,256},{384,320},{4... | collective-permute-start | bytes 221192 | tf_op jit(solution)/shard_map/ppermute | solution.py:304
  55.0 17.9 %all-to-all-start.4 = ((bf16[64,8,256]{2,1,0:T(8,128)(2,1)}), bf16[64,8,256]{2,1,0:T(8,128)(2,1)S(1)}, u32[]{:S(2)}, u32[]{:S(2)}) async-start(bf16[64,8,256]{2,1,0:T(8,128)(2,1)} %bitcast.13), calls=%async_computation.4 | async-start | bytes 524288 | tf_op jit(solution)/shard_map/all_to_all | solution.py:296
  65.9 7.0 %collective-permute-start.3 = (bf16[144,256]{1,0:T(8,128)(2,1)S(1)}, bf16[144,256]{1,0:T(8,128)(2,1)S(1)}, u32[]{:S(2)}, u32[]{:S(2)}) collective-permute-start(bf16[144,256]{1,0:T(8,128)(2,1)S(1)} %get-tuple-element.106), channel_id=1, source_target_pairs={{0,448},{64,0},{128,64},{192,128},{256,192},{320,256},{384,320},{4... | collective-permute-start | bytes 221192 | tf_op jit(solution)/shard_map/ppermute | solution.py:304
  74.4 17.9 %all-to-all-start.5 = ((bf16[64,8,256]{2,1,0:T(8,128)(2,1)}), bf16[64,8,256]{2,1,0:T(8,128)(2,1)S(1)}, u32[]{:S(2)}, u32[]{:S(2)}) async-start(bf16[64,8,256]{2,1,0:T(8,128)(2,1)} %bitcast.15), calls=%async_computation.5 | async-start | bytes 524288 | tf_op jit(solution)/shard_map/all_to_all | solution.py:296
  85.4 7.0 %collective-permute-start.4 = (bf16[144,256]{1,0:T(8,128)(2,1)S(1)}, bf16[144,256]{1,0:T(8,128)(2,1)S(1)}, u32[]{:S(2)}, u32[]{:S(2)}) collective-permute-start(bf16[144,256]{1,0:T(8,128)(2,1)S(1)} %get-tuple-element.109), channel_id=1, source_target_pairs={{0,448},{64,0},{128,64},{192,128},{256,192},{320,256},{384,320},{4... | collective-permute-start | bytes 221192 | tf_op jit(solution)/shard_map/ppermute | solution.py:304
  93.9 17.9 %all-to-all-start.6 = ((bf16[64,8,256]{2,1,0:T(8,128)(2,1)}), bf16[64,8,256]{2,1,0:T(8,128)(2,1)S(1)}, u32[]{:S(2)}, u32[]{:S(2)}) async-start(bf16[64,8,256]{2,1,0:T(8,128)(2,1)} %bitcast.17), calls=%async_computation.6 | async-start | bytes 524288 | tf_op jit(solution)/shard_map/all_to_all | solution.py:296
  104.8 7.0 %collective-permute-start.5 = (bf16[144,256]{1,0:T(8,128)(2,1)S(1)}, bf16[144,256]{1,0:T(8,128)(2,1)S(1)}, u32[]{:S(2)}, u32[]{:S(2)}) collective-permute-start(bf16[144,256]{1,0:T(8,128)(2,1)S(1)} %get-tuple-element.112), channel_id=1, source_target_pairs={{0,448},{64,0},{128,64},{192,128},{256,192},{320,256},{384,320},{4... | collective-permute-start | bytes 221192 | tf_op jit(solution)/shard_map/ppermute | solution.py:304
  113.3 17.9 %all-to-all-start.7 = ((bf16[64,8,256]{2,1,0:T(8,128)(2,1)}), bf16[64,8,256]{2,1,0:T(8,128)(2,1)S(1)}, u32[]{:S(2)}, u32[]{:S(2)}) async-start(bf16[64,8,256]{2,1,0:T(8,128)(2,1)} %bitcast.19), calls=%async_computation.7 | async-start | bytes 524288 | tf_op jit(solution)/shard_map/all_to_all | solution.py:296
  124.2 7.0 %collective-permute-start.6 = (bf16[144,256]{1,0:T(8,128)(2,1)S(1)}, bf16[144,256]{1,0:T(8,128)(2,1)S(1)}, u32[]{:S(2)}, u32[]{:S(2)}) collective-permute-start(bf16[144,256]{1,0:T(8,128)(2,1)S(1)} %get-tuple-element.115), channel_id=1, source_target_pairs={{0,448},{64,0},{128,64},{192,128},{256,192},{320,256},{384,320},{4... | collective-permute-start | bytes 221192 | tf_op jit(solution)/shard_map/ppermute | solution.py:304
  132.8 17.6 %all-to-all-start.8 = ((bf16[64,8,256]{2,1,0:T(8,128)(2,1)}), bf16[64,8,256]{2,1,0:T(8,128)(2,1)S(1)}, u32[]{:S(2)}, u32[]{:S(2)}) async-start(bf16[64,8,256]{2,1,0:T(8,128)(2,1)} %bitcast.21), calls=%async_computation.8 | async-start | bytes 524288 | tf_op jit(solution)/shard_map/all_to_all | solution.py:296
  151.2 19.6 %collective-permute-start.7 = (bf16[256,256]{1,0:T(8,128)(2,1)S(1)}, bf16[256,256]{1,0:T(8,128)(2,1)S(1)}, u32[]{:S(2)}, u32[]{:S(2)}) collective-permute-start(bf16[256,256]{1,0:T(8,128)(2,1)S(1)} %get-tuple-element.120), channel_id=1, source_target_pairs={{64,0},{128,64},{192,128},{256,192},{320,256},{384,320},{448,384},... | collective-permute-start | bytes 393224 | tf_op jit(solution)/shard_map/ppermute | solution.py:314
  170.8 4.1 %collective-permute-start.8 = (bf16[256,256]{1,0:T(8,128)(2,1)S(1)}, bf16[256,256]{1,0:T(8,128)(2,1)S(1)}, u32[]{:S(2)}, u32[]{:S(2)}) collective-permute-start(bf16[256,256]{1,0:T(8,128)(2,1)S(1)} %broadcast_select_fusion.1), channel_id=1, source_target_pairs={{0,448},{1,449},{2,450},{3,451},{4,452},{5,453},{6,454},{7,455},{8... | collective-permute-start | bytes 393224 | tf_op jit(solution)/shard_map/ppermute | solution.py:325

commit v6 on v4

--- a/solution.py
+++ b/solution.py
@@ -15,14 +15,15 @@
 PARAMS = pltpu.CompilerParams(vmem_limit_bytes=KERNEL_VMEM)
 WIDE_PARAMS = pltpu.CompilerParams(vmem_limit_bytes=56 * 2**20)
 CHUNKS = 4
-
-
-def slot_column(table):
+FIRST, LATER = 40, 20
+
+
+def slot_column(table, order):
     slots, count = table.shape
     rows = count * slots
     expand = (
         lax.broadcasted_iota(jnp.int32, (rows, count), 0) // slots
-        == lax.broadcasted_iota(jnp.int32, (rows, count), 1)
+        == (lax.broadcasted_iota(jnp.int32, (rows, count), 1) ^ order)
     ).astype(jnp.bfloat16)
     spread = lax.dot_general(
         expand,
@@ -99,7 +100,7 @@
     ]
     for copy in copies:
         copy.start()
-    select_ref[...] = one_hot_rows(slot_column(send_ref[0, 0]), features_ref.shape[1])
+    select_ref[...] = one_hot_rows(slot_column(send_ref[0, 0], FIRST), features_ref.shape[1])
     gather_out(select_ref, features_ref[0], outgoing_ref, staged_ref, sems)
     for copy in copies:
         copy.wait()
@@ -147,19 +148,21 @@
     send_ref,
     features_ref,
     after_ref,
+    scatter_ref,
+    later_ref,
     near_ref,
-    scatter_ref,
     inverse_ref,
     select_ref,
     hidden_ref,
 ):
     hidden_ref[...] = features_ref[0]
-    select_ref[...] = one_hot_rows(slot_column(send_ref[0, 0]), hidden_ref.shape[0])
+    select_ref[...] = one_hot_rows(slot_column(send_ref[0, 0], LATER), hidden_ref.shape[0])
     _, blocks, tiles, side, _ = adj_ref.shape
     span = span_ref[0]
     rows = blocks * side
-    scatter = one_hot_rows(slot_column(dest_ref[0, 0]), rows).astype(jnp.float32).T
-    scatter_ref[...] = scatter.astype(jnp.bfloat16)
+    for ref, order in ((scatter_ref, FIRST), (later_ref, LATER)):
+        scatter = one_hot_rows(slot_column(dest_ref[0, 0], order), rows).astype(jnp.float32).T
+        ref[...] = scatter.astype(jnp.bfloat16)
     degree = 1.0 + jnp.sum(scatter, axis=1, keepdims=True)
     for r in range(blocks):
         below = slice(r * side, (r + 1) * side)
@@ -187,8 +190,9 @@
     _, rows, width = features.shape
     slots, peers = recv_dst.shape[2:]
     shapes = [
+        ((rows, peers * slots), jnp.bfloat16),
+        ((rows, peers * slots), jnp.bfloat16),
         ((rows, rows), jnp.bfloat16),
-        ((rows, peers * slots), jnp.bfloat16),
         ((rows, side), jnp.float32),
         ((peers * slots, rows), jnp.bfloat16),
         ((rows, width), jnp.bfloat16),
@@ -273,12 +277,70 @@
     )(plane, hidden, arrived, *tables, early, late, *passed)
 
 
+def place_kernel(layers, plane_ref, first_ref, state_ref, last_ref, above_ref, out_ref, sems):
+    plane = plane_ref[0]
+    own, other = plane % 2, 1 - plane % 2
+
+    def place(*moves):
+        copies = [pltpu.make_async_copy(ref, out_ref.at[at], sems.at[i]) for i, (ref, at) in enumerate(moves)]
+        for copy in copies:
+            copy.start()
+        for copy in copies:
+            copy.wait()
+
+    @pl.when(plane == 0)
+    def _():
+        place((first_ref, own), (above_ref, other))
+
+    @pl.when((plane > 0) & (plane < layers - 1))
+    def _():
+        place((state_ref, own), (above_ref, other))
+
+    @pl.when(plane == layers - 1)
+    def _():
+        place((last_ref, own))
+
+
+def place_states(layers, plane, first, state, last, above):
+    return pl.pallas_call(
+        functools.partial(place_kernel, layers),
+        out_shape=jax.ShapeDtypeStruct((2,) + state.shape, state.dtype),
+        in_specs=[SMEM] + [ANYWHERE] * 4,
+        out_specs=ANYWHERE,
+        scratch_shapes=[pltpu.SemaphoreType.DMA((2,))],
+        compiler_params=PARAMS,
+        name="place_states",
+    )(plane, first, state, last, above)
+
+
+def full_kernel(layers, plane_ref, full_ref, before_ref, out_ref, sem):
+    @pl.when(plane_ref[0] == layers - 1)
+    def _():
+        copy = pltpu.make_async_copy(full_ref, out_ref.at[layers % 2], sem)
+        copy.start()
+        copy.wait()
+
+
+def place_full(layers, plane, full, out):
+    return pl.pallas_call(
+        functools.partial(full_kernel, layers),
+        out_shape=jax.ShapeDtypeStruct(out.shape, out.dtype),
+        in_specs=[SMEM] + [ANYWHERE] * 2,
+        out_specs=ANYWHERE,
+        scratch_shapes=[pltpu.SemaphoreType.DMA],
+        input_output_aliases={2: 0},
+        compiler_params=PARAMS,
+        name="place_full",
+    )(plane, full, out)
+
+
 def local(features, weight, bias, gain, tile_col, tile_adj, send_rows, recv_dst):
     layers = lax.axis_size("layer")
     index = lax.axis_index("layer")
     peers, slots = send_rows.shape[2:]
     width = features.shape[-1]
     plane = index.reshape(1)
+    orders = [[[i ^ order for i in range(peers)]] for order in (FIRST, LATER)]
     core = (lax.axis_index("dom") % 2).reshape(1)
     span = (index % 2).reshape(1)
     cores = [[2 * chip, 2 * chip + 1] for chip in range(peers // 2)]
@@ -288,11 +350,12 @@
     recv_dst = recv_dst.transpose(0, 1, 3, 2)
 
     outgoing, own_pack, own_half = first_gather(span, core, features, send_rows, weight, bias, gain)
-    *tables, hidden = build_tables(span, tile_col, tile_adj, recv_dst, send_rows, features, outgoing)
+    *scatters, near, inverse, select, hidden = build_tables(span, tile_col, tile_adj, recv_dst, send_rows, features, outgoing)
     early = own_pack
     for step in range(layers - 1):
-        arrived = lax.all_to_all(outgoing.reshape(peers, slots, width), "dom", 0, 0, tiled=True)
+        arrived = lax.all_to_all(outgoing.reshape(peers, slots, width), "dom", 0, 0, axis_index_groups=orders[step > 0], tiled=True)
         arrived = arrived.reshape(peers * slots, width)
+        tables = near, scatters[step > 0], inverse, select
         if step == 0:
             half = lax.ppermute(own_half, "layer", down)
         late = lax.all_gather(half, "dom", axis_index_groups=cores, tiled=True)
@@ -312,7 +375,7 @@
     from_above = lax.ppermute(hidden, "layer", down[1:])
 
     def finish(outgoing, hidden):
-        arrived = lax.all_to_all(outgoing.reshape(peers, slots, width), "dom", 0, 0, tiled=True)
+        arrived = lax.all_to_all(outgoing.reshape(peers, slots, width), "dom", 0, 0, axis_index_groups=orders[1], tiled=True)
         arrived = arrived.reshape(peers * slots, width)
         return run_layer(last, layers, plane, hidden, arrived, tables, early, own_pack)[0]
 
@@ -322,10 +385,8 @@
     state = lax.cond(index < last, finish, idle, outgoing, hidden)
     full = lax.ppermute(jnp.where(index == 0, state, from_above), "layer", down[:1])
     last_state = lax.cond(index == last, finish, idle, outgoing, hidden)
-    own = jnp.where(index == 0, first_state, jnp.where(index == last, last_state, state))
-    other = jnp.where(index == last, full, from_above)
-    even = index % 2 == 0
-    return jnp.stack([jnp.where(even, own, other), jnp.where(even, other, own)])[None]
+    out = place_states(layers, plane, first_state, state, last_state, from_above)
+    return place_full(layers, plane, full, out)[None]
 
 
 def solution(mesh):

time: 180 us -> 175 us (0.972)
  waiting for transfers between devices: 37.1 us -> 32.7 us
    ppermute x1, starting transfers between devices: 10.7 us -> 7.58 us  [local(): half = lax.ppermute(own_half, 'layer', down)]
    all_to_all x7, starting transfers between devices: 52.7 us -> 55.6 us  [local(): lax.all_to_all(outgoing.reshape(peers, slots, width), 'dom', 0, 0, axis_i...]
    all_to_all x7, waiting for transfers between devices: 34.4 us -> 31.5 us  [local(): lax.all_to_all(outgoing.reshape(peers, slots, width), 'dom', 0, 0, axis_i...]
  transfers between devices with their start and end apart: 16 -> 16, of which waited for: 7 -> 7; matrix products, arithmetic and copies ran while one was open for 0% -> 0% of each run, Pallas kernels for 1% -> 2%
where the time goes in v6:
time: 175 us; the launch traced here: 174 us
  starting transfers between devices  91.9 us (53%)
  blocking collectives  33.1 us (19%)
  waiting for transfers between devices  32.7 us (19%)
  Pallas kernels  15 us (9%)
    all_to_all x7, starting transfers between devices, local(): lax.all_to_all(outgoing.reshape(peers, slots, width), 'dom', 0, 0, axis_i...  55.6 us
    all_to_all x7, waiting for transfers between devices, local(): lax.all_to_all(outgoing.reshape(peers, slots, width), 'dom', 0, 0, axis_i...  31.5 us
    ppermute x6, starting transfers between devices, local(): passed = [lax.ppermute(source, 'layer', pairs)]  26.1 us
    all_to_all x1, blocking collectives, finish(): lax.all_to_all(outgoing.reshape(peers, slots, width), 'dom', 0, 0, axis_i...  17.7 us
    all_gather x7, blocking collectives, local(): late = lax.all_gather(half, 'dom', axis_index_groups=cores, tiled=True)  15.4 us
    pallas_call x8, Pallas kernels, run_layer(): pl.pallas_call(functools.partial(layer_kernel, step, layers, len(passed))...  10.4 us
    ppermute x1, starting transfers between devices, local(): half = lax.ppermute(own_half, 'layer', down)  7.58 us
  transfers between devices with their start and end apart: 16, of which 7 were waited for; matrix products, arithmetic and copies ran while one was open for 0% of the time, Pallas kernels for 2%

profile of v6, /device:TPU:1, one launch (start us, length us, event | category | flops | bytes accessed | tf_op | source)
XLA Modules:
  0.0 174.4 jit_solution(4285581039761555749)
XLA Ops:
  0.0 0.0 copy-start.3
  0.0 0.0 copy-start.4
  0.0 2.4 %first_gather.1 = (bf16[512,256]{1,0:T(8,128)(2,1)}, bf16[288,256]{1,0:T(8,128)(2,1)S(1)}, bf16[144,256]{1,0:T(8,128)(2,1)}) custom-call(s32[1]{0:T(128)} %bitcast.5.span_ref, s32[1]{0:T(128)} %bitcast.8.core_ref, bf16[2,256,256]{2,1,0:T(8,128)(2,1)} %features_ref.3, s32[2,1,8,64]{3,2,1,0:T(8,128)} %bitcast.36, bf16[1,256,256]{2,1,0:T(8,128)(2,1)} %weight_ref.1, ...), custom_call_target="tpu_custom_call" | custom-call | tf_op jit(solution)/shard_map/first_gather/pallas_call | solution.py:114
  2.4 0.0 copy-start.1
  2.4 0.0 copy-start.2
  2.4 17.0 %all-to-all-start.2 = ((bf16[64,8,256]{2,1,0:T(8,128)(2,1)}), bf16[64,8,256]{2,1,0:T(8,128)(2,1)S(1)}, u32[]{:S(2)}, u32[]{:S(2)}) async-start(bf16[64,8,256]{2,1,0:T(8,128)(2,1)} %bitcast.27), calls=%async_computation.2 | async-start | bytes 524288 | tf_op jit(solution)/shard_map/all_to_all | solution.py:356
  19.4 0.0 copy-start.5
  19.4 7.6 %collective-permute-start = (bf16[144,256]{1,0:T(8,128)(2,1)}, bf16[144,256]{1,0:T(8,128)(2,1)S(1)}, u32[]{:S(2)}, u32[]{:S(2)}) collective-permute-start(bf16[144,256]{1,0:T(8,128)(2,1)} %get-tuple-element.101), channel_id=1, source_target_pairs={{0,448},{64,0},{128,64},{192,128},{256,192},{320,256},{384,320},{4... | collective-permute-start | bytes 221192 | tf_op jit(solution)/shard_map/ppermute | solution.py:360
  27.0 2.2 %collective-permute-start.1 = (bf16[144,256]{1,0:T(8,128)(2,1)}, bf16[144,256]{1,0:T(8,128)(2,1)S(1)}, u32[]{:S(2)}, u32[]{:S(2)}) collective-permute-start(bf16[144,256]{1,0:T(8,128)(2,1)} %get-tuple-element.101), channel_id=1, source_target_pairs={{0,384},{64,448},{128,0},{192,64},{256,128},{320,192},{384,256},{4... | collective-permute-start | bytes 221192 | tf_op jit(solution)/shard_map/ppermute | solution.py:365
  29.2 0.0 copy-done.3
  29.2 0.0 copy-done.4
  29.2 0.0 copy-done.1
  29.2 0.0 copy-done.2
  29.2 0.0 copy-done.5
  29.2 0.0 copy-start
  29.2 1.2 copy-done
  30.4 1.4 build_tables.1
  31.9 0.0 collective-permute-done
  31.9 2.5 %all_gather.21.late_ref.early_ref = bf16[288,256]{1,0:T(8,128)(2,1)S(1)} all-gather(bf16[144,256]{1,0:T(8,128)(2,1)S(1)} %collective-permute-done), channel_id=1, replica_groups={{0,1},{2,3},{4,5},{6,7},{8,9},{10,11},{12,13},{14,15},{16,17},{18,19},{..., dimensions={0}, use_global_device_ids=true | all-gather | bytes 221184 | tf_op jit(solution)/shard_map/all_gather | solution.py:361
  34.4 0.0 collective-permute-done.1.refs_0_
  34.4 0.0 all-to-all-done.2
  34.4 1.5 layer.11
  35.9 5.9 %all-to-all-start.3 = ((bf16[64,8,256]{2,1,0:T(8,128)(2,1)}), bf16[64,8,256]{2,1,0:T(8,128)(2,1)S(1)}, u32[]{:S(2)}, u32[]{:S(2)}) async-start(bf16[64,8,256]{2,1,0:T(8,128)(2,1)} %bitcast.11), calls=%async_computation.3 | async-start | bytes 524288 | tf_op jit(solution)/shard_map/all_to_all | solution.py:356
  41.8 4.8 %collective-permute-start.2 = (bf16[144,256]{1,0:T(8,128)(2,1)S(1)}, bf16[144,256]{1,0:T(8,128)(2,1)S(1)}, u32[]{:S(2)}, u32[]{:S(2)}) collective-permute-start(bf16[144,256]{1,0:T(8,128)(2,1)S(1)} %get-tuple-element.105), channel_id=1, source_target_pairs={{0,448},{64,0},{128,64},{192,128},{256,192},{320,256},{384,320},{4... | collective-permute-start | bytes 221192 | tf_op jit(solution)/shard_map/ppermute | solution.py:365
  46.6 2.2 %all_gather.22.late_ref.early_ref = bf16[288,256]{1,0:T(8,128)(2,1)S(1)} all-gather(bf16[144,256]{1,0:T(8,128)(2,1)S(1)} %get-tuple-element.105), channel_id=1, replica_groups={{0,1},{2,3},{4,5},{6,7},{8,9},{10,11},{12,13},{14,15},{16,17},{18,19},{..., dimensions={0}, use_global_device_ids=true | all-gather | bytes 221184 | tf_op jit(solution)/shard_map/all_gather | solution.py:361
  48.8 0.0 collective-permute-done.2.refs_0_
  48.8 4.4 %all-to-all-done.3 = bf16[64,8,256]{2,1,0:T(8,128)(2,1)S(1)} async-done(((bf16[64,8,256]{2,1,0:T(8,128)(2,1)}), bf16[64,8,256]{2,1,0:T(8,128)(2,1)S(1)}, u32[]{:S(2)}, u32[]{:S(2)}) %all-to-all-start.3) | async-done | bytes 262176 | tf_op jit(solution)/shard_map/all_to_all | solution.py:356
  53.2 1.5 layer.12
  54.7 6.5 %all-to-all-start.4 = ((bf16[64,8,256]{2,1,0:T(8,128)(2,1)}), bf16[64,8,256]{2,1,0:T(8,128)(2,1)S(1)}, u32[]{:S(2)}, u32[]{:S(2)}) async-start(bf16[64,8,256]{2,1,0:T(8,128)(2,1)} %bitcast.13), calls=%async_computation.4 | async-start | bytes 524288 | tf_op jit(solution)/shard_map/all_to_all | solution.py:356
  61.3 4.8 %collective-permute-start.3 = (bf16[144,256]{1,0:T(8,128)(2,1)S(1)}, bf16[144,256]{1,0:T(8,128)(2,1)S(1)}, u32[]{:S(2)}, u32[]{:S(2)}) collective-permute-start(bf16[144,256]{1,0:T(8,128)(2,1)S(1)} %get-tuple-element.108), channel_id=1, source_target_pairs={{0,448},{64,0},{128,64},{192,128},{256,192},{320,256},{384,320},{4... | collective-permute-start | bytes 221192 | tf_op jit(solution)/shard_map/ppermute | solution.py:365
  66.1 2.2 %all_gather.23.late_ref.early_ref = bf16[288,256]{1,0:T(8,128)(2,1)S(1)} all-gather(bf16[144,256]{1,0:T(8,128)(2,1)S(1)} %get-tuple-element.108), channel_id=1, replica_groups={{0,1},{2,3},{4,5},{6,7},{8,9},{10,11},{12,13},{14,15},{16,17},{18,19},{..., dimensions={0}, use_global_device_ids=true | all-gather | bytes 221184 | tf_op jit(solution)/shard_map/all_gather | solution.py:361
  68.3 0.0 collective-permute-done.3.refs_0_
  68.3 4.4 %all-to-all-done.4 = bf16[64,8,256]{2,1,0:T(8,128)(2,1)S(1)} async-done(((bf16[64,8,256]{2,1,0:T(8,128)(2,1)}), bf16[64,8,256]{2,1,0:T(8,128)(2,1)S(1)}, u32[]{:S(2)}, u32[]{:S(2)}) %all-to-all-start.4) | async-done | bytes 262176 | tf_op jit(solution)/shard_map/all_to_all | solution.py:356
  72.7 1.5 layer.13
  74.2 6.6 %all-to-all-start.5 = ((bf16[64,8,256]{2,1,0:T(8,128)(2,1)}), bf16[64,8,256]{2,1,0:T(8,128)(2,1)S(1)}, u32[]{:S(2)}, u32[]{:S(2)}) async-start(bf16[64,8,256]{2,1,0:T(8,128)(2,1)} %bitcast.15), calls=%async_computation.5 | async-start | bytes 524288 | tf_op jit(solution)/shard_map/all_to_all | solution.py:356
  80.8 4.8 %collective-permute-start.4 = (bf16[144,256]{1,0:T(8,128)(2,1)S(1)}, bf16[144,256]{1,0:T(8,128)(2,1)S(1)}, u32[]{:S(2)}, u32[]{:S(2)}) collective-permute-start(bf16[144,256]{1,0:T(8,128)(2,1)S(1)} %get-tuple-element.111), channel_id=1, source_target_pairs={{0,448},{64,0},{128,64},{192,128},{256,192},{320,256},{384,320},{4... | collective-permute-start | bytes 221192 | tf_op jit(solution)/shard_map/ppermute | solution.py:365
  85.6 2.2 %all_gather.24.late_ref.early_ref = bf16[288,256]{1,0:T(8,128)(2,1)S(1)} all-gather(bf16[144,256]{1,0:T(8,128)(2,1)S(1)} %get-tuple-element.111), channel_id=1, replica_groups={{0,1},{2,3},{4,5},{6,7},{8,9},{10,11},{12,13},{14,15},{16,17},{18,19},{..., dimensions={0}, use_global_device_ids=true | all-gather | bytes 221184 | tf_op jit(solution)/shard_map/all_gather | solution.py:361
  87.8 0.0 collective-permute-done.4.refs_0_
  87.8 4.4 %all-to-all-done.5 = bf16[64,8,256]{2,1,0:T(8,128)(2,1)S(1)} async-done(((bf16[64,8,256]{2,1,0:T(8,128)(2,1)}), bf16[64,8,256]{2,1,0:T(8,128)(2,1)S(1)}, u32[]{:S(2)}, u32[]{:S(2)}) %all-to-all-start.5) | async-done | bytes 262176 | tf_op jit(solution)/shard_map/all_to_all | solution.py:356
  92.2 1.5 layer.14
  93.7 6.5 %all-to-all-start.6 = ((bf16[64,8,256]{2,1,0:T(8,128)(2,1)}), bf16[64,8,256]{2,1,0:T(8,128)(2,1)S(1)}, u32[]{:S(2)}, u32[]{:S(2)}) async-start(bf16[64,8,256]{2,1,0:T(8,128)(2,1)} %bitcast.17), calls=%async_computation.6 | async-start | bytes 524288 | tf_op jit(solution)/shard_map/all_to_all | solution.py:356
  100.2 4.8 %collective-permute-start.5 = (bf16[144,256]{1,0:T(8,128)(2,1)S(1)}, bf16[144,256]{1,0:T(8,128)(2,1)S(1)}, u32[]{:S(2)}, u32[]{:S(2)}) collective-permute-start(bf16[144,256]{1,0:T(8,128)(2,1)S(1)} %get-tuple-element.114), channel_id=1, source_target_pairs={{0,448},{64,0},{128,64},{192,128},{256,192},{320,256},{384,320},{4... | collective-permute-start | bytes 221192 | tf_op jit(solution)/shard_map/ppermute | solution.py:365
  105.0 2.2 %all_gather.25.late_ref.early_ref = bf16[288,256]{1,0:T(8,128)(2,1)S(1)} all-gather(bf16[144,256]{1,0:T(8,128)(2,1)S(1)} %get-tuple-element.114), channel_id=1, replica_groups={{0,1},{2,3},{4,5},{6,7},{8,9},{10,11},{12,13},{14,15},{16,17},{18,19},{..., dimensions={0}, use_global_device_ids=true | all-gather | bytes 221184 | tf_op jit(solution)/shard_map/all_gather | solution.py:361
  107.2 0.0 collective-permute-done.5.refs_0_
  107.2 4.4 %all-to-all-done.6 = bf16[64,8,256]{2,1,0:T(8,128)(2,1)S(1)} async-done(((bf16[64,8,256]{2,1,0:T(8,128)(2,1)}), bf16[64,8,256]{2,1,0:T(8,128)(2,1)S(1)}, u32[]{:S(2)}, u32[]{:S(2)}) %all-to-all-start.6) | async-done | bytes 262176 | tf_op jit(solution)/shard_map/all_to_all | solution.py:356
  111.6 1.5 layer.15
  113.2 6.5 %all-to-all-start.7 = ((bf16[64,8,256]{2,1,0:T(8,128)(2,1)}), bf16[64,8,256]{2,1,0:T(8,128)(2,1)S(1)}, u32[]{:S(2)}, u32[]{:S(2)}) async-start(bf16[64,8,256]{2,1,0:T(8,128)(2,1)} %bitcast.19), calls=%async_computation.7 | async-start | bytes 524288 | tf_op jit(solution)/shard_map/all_to_all | solution.py:356
  119.7 4.8 %collective-permute-start.6 = (bf16[144,256]{1,0:T(8,128)(2,1)S(1)}, bf16[144,256]{1,0:T(8,128)(2,1)S(1)}, u32[]{:S(2)}, u32[]{:S(2)}) collective-permute-start(bf16[144,256]{1,0:T(8,128)(2,1)S(1)} %get-tuple-element.117), channel_id=1, source_target_pairs={{0,448},{64,0},{128,64},{192,128},{256,192},{320,256},{384,320},{4... | collective-permute-start | bytes 221192 | tf_op jit(solution)/shard_map/ppermute | solution.py:365
  124.5 2.2 %all_gather.26.late_ref.early_ref = bf16[288,256]{1,0:T(8,128)(2,1)S(1)} all-gather(bf16[144,256]{1,0:T(8,128)(2,1)S(1)} %get-tuple-element.117), channel_id=1, replica_groups={{0,1},{2,3},{4,5},{6,7},{8,9},{10,11},{12,13},{14,15},{16,17},{18,19},{..., dimensions={0}, use_global_device_ids=true | all-gather | bytes 221184 | tf_op jit(solution)/shard_map/all_gather | solution.py:361
  126.7 0.0 collective-permute-done.6.refs_0_
  126.7 4.4 %all-to-all-done.7 = bf16[64,8,256]{2,1,0:T(8,128)(2,1)S(1)} async-done(((bf16[64,8,256]{2,1,0:T(8,128)(2,1)}), bf16[64,8,256]{2,1,0:T(8,128)(2,1)S(1)}, u32[]{:S(2)}, u32[]{:S(2)}) %all-to-all-start.7) | async-done | bytes 262176 | tf_op jit(solution)/shard_map/all_to_all | solution.py:356
  131.1 1.5 layer.16
  132.6 6.5 %all-to-all-start.8 = ((bf16[64,8,256]{2,1,0:T(8,128)(2,1)}), bf16[64,8,256]{2,1,0:T(8,128)(2,1)S(1)}, u32[]{:S(2)}, u32[]{:S(2)}) async-start(bf16[64,8,256]{2,1,0:T(8,128)(2,1)} %bitcast.21), calls=%async_computation.8 | async-start | bytes 524288 | tf_op jit(solution)/shard_map/all_to_all | solution.py:356
  139.2 1.9 %all_gather.27.late_ref = bf16[288,256]{1,0:T(8,128)(2,1)S(1)} all-gather(bf16[144,256]{1,0:T(8,128)(2,1)S(1)} %get-tuple-element.120), channel_id=1, replica_groups={{0,1},{2,3},{4,5},{6,7},{8,9},{10,11},{12,13},{14,15},{16,17},{18,19},{..., dimensions={0}, use_global_device_ids=true | all-gather | bytes 221184 | tf_op jit(solution)/shard_map/all_gather | solution.py:361
  141.1 9.5 %all-to-all-done.8 = bf16[64,8,256]{2,1,0:T(8,128)(2,1)S(1)} async-done(((bf16[64,8,256]{2,1,0:T(8,128)(2,1)}), bf16[64,8,256]{2,1,0:T(8,128)(2,1)S(1)}, u32[]{:S(2)}, u32[]{:S(2)}) %all-to-all-start.8) | async-done | bytes 262176 | tf_op jit(solution)/shard_map/all_to_all | solution.py:356
  150.6 0.8 layer.17
  151.4 1.3 collective-permute-start.7
  152.7 18.3 %conditional.2 = (bf16[256,256]{1,0:T(8,128)(2,1)S(1)}) conditional(s32[]{:T(128)} %convert_element_type.6, () %tuple.17, (bf16[512,256]{1,0:T(8,128)(2,1)S(1)}, s32[1]{0:T(128)}, bf16[256,256]{1,0:T(8,128)(2,1)S(1)}, bf16[256,256]{1,0:T(8,128)(2,1)S(1)}, bf16[256,512]{1,0:T(8,128)(2,1)S(1)}, /*index=5*/f32[256,128]{1,0:T(8,128)S(1)}, ...), branch_computations={%region_0.1_spmd, %region_1.2_spmd} | conditional | bytes 524296 | solution.py:385
  152.7 17.7 %all_to_all.43 = bf16[64,8,256]{2,1,0:T(8,128)(2,1)S(1)} all-to-all(bf16[64,8,256]{2,1,0:T(8,128)(2,1)S(1)} %bitcast.24), channel_id=1, replica_groups={{20,21,22,23,16,17,18,19,28,29,30,31,24,25,26,27,4,5,6,7,0,1,2,3,12,13,..., dimensions={0} | all-to-all | bytes 524288 | tf_op jit(solution)/shard_map/cond/branch_1_fun/all_to_all | solution.py:378
  170.5 0.5 layer.9
  171.0 0.0 collective-permute-done.7.above_ref
  171.0 1.3 collective-permute-start.8
  172.4 0.7 place_states.1.before_ref
  173.1 1.1 collective-permute-done.8.full_ref
  (4 shorter events, 0.1 us)
Async XLA Ops:
  0.0 29.2 %copy-start.3 = (s32[2,1,64,8]{2,3,1,0:T(8,128)S(1)}, s32[2,1,64,8]{2,3,1,0:T(8,128)}, u32[]{:S(2)}) copy-start(s32[2,1,64,8]{2,3,1,0:T(8,128)} %param.18) | copy-start | bytes 12292
  0.0 29.2 %copy-start.4 = (s32[2,1,64,8]{2,3,1,0:T(8,128)S(1)}, s32[2,1,64,8]{2,3,1,0:T(8,128)}, u32[]{:S(2)}) copy-start(s32[2,1,64,8]{2,3,1,0:T(8,128)} %param.19) | copy-start | bytes 12292
  2.4 26.8 %copy-start.1 = (bf16[2,256,256]{2,1,0:T(8,128)(2,1)S(1)}, bf16[2,256,256]{2,1,0:T(8,128)(2,1)}, u32[]{:S(2)}) copy-start(bf16[2,256,256]{2,1,0:T(8,128)(2,1)} %features_ref.3) | copy-start | bytes 786436
  2.4 26.8 %copy-start.2 = (bf16[512,256]{1,0:T(8,128)(2,1)S(1)}, bf16[512,256]{1,0:T(8,128)(2,1)}, u32[]{:S(2)}) copy-start(bf16[512,256]{1,0:T(8,128)(2,1)} %get-tuple-element.94.after_ref) | copy-start | bytes 786436
  2.4 32.0 %all-to-all-start.2 = ((bf16[64,8,256]{2,1,0:T(8,128)(2,1)}), bf16[64,8,256]{2,1,0:T(8,128)(2,1)S(1)}, u32[]{:S(2)}, u32[]{:S(2)}) async-start(bf16[64,8,256]{2,1,0:T(8,128)(2,1)} %bitcast.27), calls=%async_computation.2 | async-start | bytes 524288 | tf_op jit(solution)/shard_map/all_to_all | solution.py:356
  19.4 9.8 %copy-start.5 = (s32[2,2,4]{2,1,0:T(2,128)S(1)}, s32[2,2,4]{2,1,0:T(2,128)}, u32[]{:S(2)}) copy-start(s32[2,2,4]{2,1,0:T(2,128)} %col_ref.1) | copy-start | bytes 196
  19.4 12.5 %collective-permute-start = (bf16[144,256]{1,0:T(8,128)(2,1)}, bf16[144,256]{1,0:T(8,128)(2,1)S(1)}, u32[]{:S(2)}, u32[]{:S(2)}) collective-permute-start(bf16[144,256]{1,0:T(8,128)(2,1)} %get-tuple-element.101), channel_id=1, source_target_pairs={{0,448},{64,0},{128,64},{192,128},{256,192},{320,256},{384,320},{4... | collective-permute-start | bytes 221192 | tf_op jit(solution)/shard_map/ppermute | solution.py:360
  27.0 7.4 %collective-permute-start.1 = (bf16[144,256]{1,0:T(8,128)(2,1)}, bf16[144,256]{1,0:T(8,128)(2,1)S(1)}, u32[]{:S(2)}, u32[]{:S(2)}) collective-permute-start(bf16[144,256]{1,0:T(8,128)(2,1)} %get-tuple-element.101), channel_id=1, source_target_pairs={{0,384},{64,448},{128,0},{192,64},{256,128},{320,192},{384,256},{4... | collective-permute-start | bytes 221192 | tf_op jit(solution)/shard_map/ppermute | solution.py:365
  29.2 1.2 copy-start
  35.9 17.3 %all-to-all-start.3 = ((bf16[64,8,256]{2,1,0:T(8,128)(2,1)}), bf16[64,8,256]{2,1,0:T(8,128)(2,1)S(1)}, u32[]{:S(2)}, u32[]{:S(2)}) async-start(bf16[64,8,256]{2,1,0:T(8,128)(2,1)} %bitcast.11), calls=%async_computation.3 | async-start | bytes 524288 | tf_op jit(solution)/shard_map/all_to_all | solution.py:356
  41.8 7.0 %collective-permute-start.2 = (bf16[144,256]{1,0:T(8,128)(2,1)S(1)}, bf16[144,256]{1,0:T(8,128)(2,1)S(1)}, u32[]{:S(2)}, u32[]{:S(2)}) collective-permute-start(bf16[144,256]{1,0:T(8,128)(2,1)S(1)} %get-tuple-element.105), channel_id=1, source_target_pairs={{0,448},{64,0},{128,64},{192,128},{256,192},{320,256},{384,320},{4... | collective-permute-start | bytes 221192 | tf_op jit(solution)/shard_map/ppermute | solution.py:365
  54.7 18.0 %all-to-all-start.4 = ((bf16[64,8,256]{2,1,0:T(8,128)(2,1)}), bf16[64,8,256]{2,1,0:T(8,128)(2,1)S(1)}, u32[]{:S(2)}, u32[]{:S(2)}) async-start(bf16[64,8,256]{2,1,0:T(8,128)(2,1)} %bitcast.13), calls=%async_computation.4 | async-start | bytes 524288 | tf_op jit(solution)/shard_map/all_to_all | solution.py:356
  61.3 7.0 %collective-permute-start.3 = (bf16[144,256]{1,0:T(8,128)(2,1)S(1)}, bf16[144,256]{1,0:T(8,128)(2,1)S(1)}, u32[]{:S(2)}, u32[]{:S(2)}) collective-permute-start(bf16[144,256]{1,0:T(8,128)(2,1)S(1)} %get-tuple-element.108), channel_id=1, source_target_pairs={{0,448},{64,0},{128,64},{192,128},{256,192},{320,256},{384,320},{4... | collective-permute-start | bytes 221192 | tf_op jit(solution)/shard_map/ppermute | solution.py:365
  74.2 18.0 %all-to-all-start.5 = ((bf16[64,8,256]{2,1,0:T(8,128)(2,1)}), bf16[64,8,256]{2,1,0:T(8,128)(2,1)S(1)}, u32[]{:S(2)}, u32[]{:S(2)}) async-start(bf16[64,8,256]{2,1,0:T(8,128)(2,1)} %bitcast.15), calls=%async_computation.5 | async-start | bytes 524288 | tf_op jit(solution)/shard_map/all_to_all | solution.py:356
  80.8 7.0 %collective-permute-start.4 = (bf16[144,256]{1,0:T(8,128)(2,1)S(1)}, bf16[144,256]{1,0:T(8,128)(2,1)S(1)}, u32[]{:S(2)}, u32[]{:S(2)}) collective-permute-start(bf16[144,256]{1,0:T(8,128)(2,1)S(1)} %get-tuple-element.111), channel_id=1, source_target_pairs={{0,448},{64,0},{128,64},{192,128},{256,192},{320,256},{384,320},{4... | collective-permute-start | bytes 221192 | tf_op jit(solution)/shard_map/ppermute | solution.py:365
  93.7 18.0 %all-to-all-start.6 = ((bf16[64,8,256]{2,1,0:T(8,128)(2,1)}), bf16[64,8,256]{2,1,0:T(8,128)(2,1)S(1)}, u32[]{:S(2)}, u32[]{:S(2)}) async-start(bf16[64,8,256]{2,1,0:T(8,128)(2,1)} %bitcast.17), calls=%async_computation.6 | async-start | bytes 524288 | tf_op jit(solution)/shard_map/all_to_all | solution.py:356
  100.2 7.0 %collective-permute-start.5 = (bf16[144,256]{1,0:T(8,128)(2,1)S(1)}, bf16[144,256]{1,0:T(8,128)(2,1)S(1)}, u32[]{:S(2)}, u32[]{:S(2)}) collective-permute-start(bf16[144,256]{1,0:T(8,128)(2,1)S(1)} %get-tuple-element.114), channel_id=1, source_target_pairs={{0,448},{64,0},{128,64},{192,128},{256,192},{320,256},{384,320},{4... | collective-permute-start | bytes 221192 | tf_op jit(solution)/shard_map/ppermute | solution.py:365
  113.2 18.0 %all-to-all-start.7 = ((bf16[64,8,256]{2,1,0:T(8,128)(2,1)}), bf16[64,8,256]{2,1,0:T(8,128)(2,1)S(1)}, u32[]{:S(2)}, u32[]{:S(2)}) async-start(bf16[64,8,256]{2,1,0:T(8,128)(2,1)} %bitcast.19), calls=%async_computation.7 | async-start | bytes 524288 | tf_op jit(solution)/shard_map/all_to_all | solution.py:356
  119.7 7.0 %collective-permute-start.6 = (bf16[144,256]{1,0:T(8,128)(2,1)S(1)}, bf16[144,256]{1,0:T(8,128)(2,1)S(1)}, u32[]{:S(2)}, u32[]{:S(2)}) collective-permute-start(bf16[144,256]{1,0:T(8,128)(2,1)S(1)} %get-tuple-element.117), channel_id=1, source_target_pairs={{0,448},{64,0},{128,64},{192,128},{256,192},{320,256},{384,320},{4... | collective-permute-start | bytes 221192 | tf_op jit(solution)/shard_map/ppermute | solution.py:365
  132.6 18.0 %all-to-all-start.8 = ((bf16[64,8,256]{2,1,0:T(8,128)(2,1)}), bf16[64,8,256]{2,1,0:T(8,128)(2,1)S(1)}, u32[]{:S(2)}, u32[]{:S(2)}) async-start(bf16[64,8,256]{2,1,0:T(8,128)(2,1)} %bitcast.21), calls=%async_computation.8 | async-start | bytes 524288 | tf_op jit(solution)/shard_map/all_to_all | solution.py:356
  151.4 19.6 %collective-permute-start.7 = (bf16[256,256]{1,0:T(8,128)(2,1)S(1)}, bf16[256,256]{1,0:T(8,128)(2,1)S(1)}, u32[]{:S(2)}, u32[]{:S(2)}) collective-permute-start(bf16[256,256]{1,0:T(8,128)(2,1)S(1)} %get-tuple-element.122), channel_id=1, source_target_pairs={{64,0},{128,64},{192,128},{256,192},{320,256},{384,320},{448,384},... | collective-permute-start | bytes 393224 | tf_op jit(solution)/shard_map/ppermute | solution.py:375
  171.0 3.2 %collective-permute-start.8 = (bf16[256,256]{1,0:T(8,128)(2,1)S(1)}, bf16[256,256]{1,0:T(8,128)(2,1)S(1)}, u32[]{:S(2)}, u32[]{:S(2)}) collective-permute-start(bf16[256,256]{1,0:T(8,128)(2,1)S(1)} %broadcast_select_fusion), channel_id=1, source_target_pairs={{0,448},{1,449},{2,450},{3,451},{4,452},{5,453},{6,454},{7,455},{8... | collective-permute-start | bytes 393224 | tf_op jit(solution)/shard_map/ppermute | solution.py:386

commit v7 on v6

--- a/solution.py
+++ b/solution.py
@@ -15,7 +15,7 @@
 PARAMS = pltpu.CompilerParams(vmem_limit_bytes=KERNEL_VMEM)
 WIDE_PARAMS = pltpu.CompilerParams(vmem_limit_bytes=56 * 2**20)
 CHUNKS = 4
-FIRST, LATER = 40, 20
+FIRST, LATER = 42, 20
 
 
 def slot_column(table, order):

time: 175 us -> 175 us (level)
  no operation moved by 1% of the time
where the time goes in v7:
time: 175 us; the launch traced here: 174 us
  starting transfers between devices  91.1 us (52%)
  blocking collectives  33.2 us (19%)
  waiting for transfers between devices  32.7 us (19%)
  Pallas kernels  15 us (9%)
    all_to_all x7, starting transfers between devices, local(): lax.all_to_all(outgoing.reshape(peers, slots, width), 'dom', 0, 0, axis_i...  54.7 us
    all_to_all x7, waiting for transfers between devices, local(): lax.all_to_all(outgoing.reshape(peers, slots, width), 'dom', 0, 0, axis_i...  31.5 us
    ppermute x6, starting transfers between devices, local(): passed = [lax.ppermute(source, 'layer', pairs)]  26.1 us
    all_to_all x1, blocking collectives, finish(): lax.all_to_all(outgoing.reshape(peers, slots, width), 'dom', 0, 0, axis_i...  17.7 us
    all_gather x7, blocking collectives, local(): late = lax.all_gather(half, 'dom', axis_index_groups=cores, tiled=True)  15.4 us
    pallas_call x8, Pallas kernels, run_layer(): pl.pallas_call(functools.partial(layer_kernel, step, layers, len(passed))...  10.4 us
    ppermute x1, starting transfers between devices, local(): half = lax.ppermute(own_half, 'layer', down)  7.69 us
  transfers between devices with their start and end apart: 16, of which 7 were waited for; matrix products, arithmetic and copies ran while one was open for 0% of the time, Pallas kernels for 2%

profile of v7, /device:TPU:1, one launch (start us, length us, event | category | flops | bytes accessed | tf_op | source)
XLA Modules:
  0.0 173.7 jit_solution(1441099257769400051)
XLA Ops:
  0.0 0.0 copy-start.3
  0.0 0.0 copy-start.4
  0.0 2.4 %first_gather.1 = (bf16[512,256]{1,0:T(8,128)(2,1)}, bf16[288,256]{1,0:T(8,128)(2,1)S(1)}, bf16[144,256]{1,0:T(8,128)(2,1)}) custom-call(s32[1]{0:T(128)} %bitcast.5.span_ref, s32[1]{0:T(128)} %bitcast.8.core_ref, bf16[2,256,256]{2,1,0:T(8,128)(2,1)} %features_ref.3, s32[2,1,8,64]{3,2,1,0:T(8,128)} %bitcast.36, bf16[1,256,256]{2,1,0:T(8,128)(2,1)} %weight_ref.1, ...), custom_call_target="tpu_custom_call" | custom-call | tf_op jit(solution)/shard_map/first_gather/pallas_call | solution.py:114
  2.4 0.0 copy-start.1
  2.4 0.0 copy-start.2
  2.4 16.1 %all-to-all-start.2 = ((bf16[64,8,256]{2,1,0:T(8,128)(2,1)}), bf16[64,8,256]{2,1,0:T(8,128)(2,1)S(1)}, u32[]{:S(2)}, u32[]{:S(2)}) async-start(bf16[64,8,256]{2,1,0:T(8,128)(2,1)} %bitcast.27), calls=%async_computation.2 | async-start | bytes 524288 | tf_op jit(solution)/shard_map/all_to_all | solution.py:356
  18.5 0.0 copy-start.5
  18.5 7.7 %collective-permute-start = (bf16[144,256]{1,0:T(8,128)(2,1)}, bf16[144,256]{1,0:T(8,128)(2,1)S(1)}, u32[]{:S(2)}, u32[]{:S(2)}) collective-permute-start(bf16[144,256]{1,0:T(8,128)(2,1)} %get-tuple-element.101), channel_id=1, source_target_pairs={{0,448},{64,0},{128,64},{192,128},{256,192},{320,256},{384,320},{4... | collective-permute-start | bytes 221192 | tf_op jit(solution)/shard_map/ppermute | solution.py:360
  26.2 2.2 %collective-permute-start.1 = (bf16[144,256]{1,0:T(8,128)(2,1)}, bf16[144,256]{1,0:T(8,128)(2,1)S(1)}, u32[]{:S(2)}, u32[]{:S(2)}) collective-permute-start(bf16[144,256]{1,0:T(8,128)(2,1)} %get-tuple-element.101), channel_id=1, source_target_pairs={{0,384},{64,448},{128,0},{192,64},{256,128},{320,192},{384,256},{4... | collective-permute-start | bytes 221192 | tf_op jit(solution)/shard_map/ppermute | solution.py:365
  28.4 0.0 copy-done.3
  28.4 0.0 copy-done.4
  28.4 0.0 copy-done.1
  28.4 0.0 copy-done.2
  28.4 0.0 copy-done.5
  28.4 0.0 copy-start
  28.4 1.2 copy-done
  29.7 1.4 build_tables.1
  31.1 0.0 collective-permute-done
  31.1 2.5 %all_gather.21.late_ref.early_ref = bf16[288,256]{1,0:T(8,128)(2,1)S(1)} all-gather(bf16[144,256]{1,0:T(8,128)(2,1)S(1)} %collective-permute-done), channel_id=1, replica_groups={{0,1},{2,3},{4,5},{6,7},{8,9},{10,11},{12,13},{14,15},{16,17},{18,19},{..., dimensions={0}, use_global_device_ids=true | all-gather | bytes 221184 | tf_op jit(solution)/shard_map/all_gather | solution.py:361
  33.6 0.0 collective-permute-done.1.refs_0_
  33.6 0.0 all-to-all-done.2
  33.6 1.5 layer.11
  35.1 5.9 %all-to-all-start.3 = ((bf16[64,8,256]{2,1,0:T(8,128)(2,1)}), bf16[64,8,256]{2,1,0:T(8,128)(2,1)S(1)}, u32[]{:S(2)}, u32[]{:S(2)}) async-start(bf16[64,8,256]{2,1,0:T(8,128)(2,1)} %bitcast.11), calls=%async_computation.3 | async-start | bytes 524288 | tf_op jit(solution)/shard_map/all_to_all | solution.py:356
  41.0 4.8 %collective-permute-start.2 = (bf16[144,256]{1,0:T(8,128)(2,1)S(1)}, bf16[144,256]{1,0:T(8,128)(2,1)S(1)}, u32[]{:S(2)}, u32[]{:S(2)}) collective-permute-start(bf16[144,256]{1,0:T(8,128)(2,1)S(1)} %get-tuple-element.105), channel_id=1, source_target_pairs={{0,448},{64,0},{128,64},{192,128},{256,192},{320,256},{384,320},{4... | collective-permute-start | bytes 221192 | tf_op jit(solution)/shard_map/ppermute | solution.py:365
  45.8 2.2 %all_gather.22.late_ref.early_ref = bf16[288,256]{1,0:T(8,128)(2,1)S(1)} all-gather(bf16[144,256]{1,0:T(8,128)(2,1)S(1)} %get-tuple-element.105), channel_id=1, replica_groups={{0,1},{2,3},{4,5},{6,7},{8,9},{10,11},{12,13},{14,15},{16,17},{18,19},{..., dimensions={0}, use_global_device_ids=true | all-gather | bytes 221184 | tf_op jit(solution)/shard_map/all_gather | solution.py:361
  48.0 0.0 collective-permute-done.2.refs_0_
  48.0 4.4 %all-to-all-done.3 = bf16[64,8,256]{2,1,0:T(8,128)(2,1)S(1)} async-done(((bf16[64,8,256]{2,1,0:T(8,128)(2,1)}), bf16[64,8,256]{2,1,0:T(8,128)(2,1)S(1)}, u32[]{:S(2)}, u32[]{:S(2)}) %all-to-all-start.3) | async-done | bytes 262176 | tf_op jit(solution)/shard_map/all_to_all | solution.py:356
  52.4 1.5 layer.12
  54.0 6.6 %all-to-all-start.4 = ((bf16[64,8,256]{2,1,0:T(8,128)(2,1)}), bf16[64,8,256]{2,1,0:T(8,128)(2,1)S(1)}, u32[]{:S(2)}, u32[]{:S(2)}) async-start(bf16[64,8,256]{2,1,0:T(8,128)(2,1)} %bitcast.13), calls=%async_computation.4 | async-start | bytes 524288 | tf_op jit(solution)/shard_map/all_to_all | solution.py:356
  60.5 4.8 %collective-permute-start.3 = (bf16[144,256]{1,0:T(8,128)(2,1)S(1)}, bf16[144,256]{1,0:T(8,128)(2,1)S(1)}, u32[]{:S(2)}, u32[]{:S(2)}) collective-permute-start(bf16[144,256]{1,0:T(8,128)(2,1)S(1)} %get-tuple-element.108), channel_id=1, source_target_pairs={{0,448},{64,0},{128,64},{192,128},{256,192},{320,256},{384,320},{4... | collective-permute-start | bytes 221192 | tf_op jit(solution)/shard_map/ppermute | solution.py:365
  65.3 2.2 %all_gather.23.late_ref.early_ref = bf16[288,256]{1,0:T(8,128)(2,1)S(1)} all-gather(bf16[144,256]{1,0:T(8,128)(2,1)S(1)} %get-tuple-element.108), channel_id=1, replica_groups={{0,1},{2,3},{4,5},{6,7},{8,9},{10,11},{12,13},{14,15},{16,17},{18,19},{..., dimensions={0}, use_global_device_ids=true | all-gather | bytes 221184 | tf_op jit(solution)/shard_map/all_gather | solution.py:361
  67.5 0.0 collective-permute-done.3.refs_0_
  67.5 4.4 %all-to-all-done.4 = bf16[64,8,256]{2,1,0:T(8,128)(2,1)S(1)} async-done(((bf16[64,8,256]{2,1,0:T(8,128)(2,1)}), bf16[64,8,256]{2,1,0:T(8,128)(2,1)S(1)}, u32[]{:S(2)}, u32[]{:S(2)}) %all-to-all-start.4) | async-done | bytes 262176 | tf_op jit(solution)/shard_map/all_to_all | solution.py:356
  71.9 1.5 layer.13
  73.4 6.5 %all-to-all-start.5 = ((bf16[64,8,256]{2,1,0:T(8,128)(2,1)}), bf16[64,8,256]{2,1,0:T(8,128)(2,1)S(1)}, u32[]{:S(2)}, u32[]{:S(2)}) async-start(bf16[64,8,256]{2,1,0:T(8,128)(2,1)} %bitcast.15), calls=%async_computation.5 | async-start | bytes 524288 | tf_op jit(solution)/shard_map/all_to_all | solution.py:356
  80.0 4.8 %collective-permute-start.4 = (bf16[144,256]{1,0:T(8,128)(2,1)S(1)}, bf16[144,256]{1,0:T(8,128)(2,1)S(1)}, u32[]{:S(2)}, u32[]{:S(2)}) collective-permute-start(bf16[144,256]{1,0:T(8,128)(2,1)S(1)} %get-tuple-element.111), channel_id=1, source_target_pairs={{0,448},{64,0},{128,64},{192,128},{256,192},{320,256},{384,320},{4... | collective-permute-start | bytes 221192 | tf_op jit(solution)/shard_map/ppermute | solution.py:365
  84.8 2.2 %all_gather.24.late_ref.early_ref = bf16[288,256]{1,0:T(8,128)(2,1)S(1)} all-gather(bf16[144,256]{1,0:T(8,128)(2,1)S(1)} %get-tuple-element.111), channel_id=1, replica_groups={{0,1},{2,3},{4,5},{6,7},{8,9},{10,11},{12,13},{14,15},{16,17},{18,19},{..., dimensions={0}, use_global_device_ids=true | all-gather | bytes 221184 | tf_op jit(solution)/shard_map/all_gather | solution.py:361
  87.0 0.0 collective-permute-done.4.refs_0_
  87.0 4.4 %all-to-all-done.5 = bf16[64,8,256]{2,1,0:T(8,128)(2,1)S(1)} async-done(((bf16[64,8,256]{2,1,0:T(8,128)(2,1)}), bf16[64,8,256]{2,1,0:T(8,128)(2,1)S(1)}, u32[]{:S(2)}, u32[]{:S(2)}) %all-to-all-start.5) | async-done | bytes 262176 | tf_op jit(solution)/shard_map/all_to_all | solution.py:356
  91.4 1.5 layer.14
  92.9 6.5 %all-to-all-start.6 = ((bf16[64,8,256]{2,1,0:T(8,128)(2,1)}), bf16[64,8,256]{2,1,0:T(8,128)(2,1)S(1)}, u32[]{:S(2)}, u32[]{:S(2)}) async-start(bf16[64,8,256]{2,1,0:T(8,128)(2,1)} %bitcast.17), calls=%async_computation.6 | async-start | bytes 524288 | tf_op jit(solution)/shard_map/all_to_all | solution.py:356
  99.5 4.8 %collective-permute-start.5 = (bf16[144,256]{1,0:T(8,128)(2,1)S(1)}, bf16[144,256]{1,0:T(8,128)(2,1)S(1)}, u32[]{:S(2)}, u32[]{:S(2)}) collective-permute-start(bf16[144,256]{1,0:T(8,128)(2,1)S(1)} %get-tuple-element.114), channel_id=1, source_target_pairs={{0,448},{64,0},{128,64},{192,128},{256,192},{320,256},{384,320},{4... | collective-permute-start | bytes 221192 | tf_op jit(solution)/shard_map/ppermute | solution.py:365
  104.3 2.2 %all_gather.25.late_ref.early_ref = bf16[288,256]{1,0:T(8,128)(2,1)S(1)} all-gather(bf16[144,256]{1,0:T(8,128)(2,1)S(1)} %get-tuple-element.114), channel_id=1, replica_groups={{0,1},{2,3},{4,5},{6,7},{8,9},{10,11},{12,13},{14,15},{16,17},{18,19},{..., dimensions={0}, use_global_device_ids=true | all-gather | bytes 221184 | tf_op jit(solution)/shard_map/all_gather | solution.py:361
  106.5 0.0 collective-permute-done.5.refs_0_
  106.5 4.4 %all-to-all-done.6 = bf16[64,8,256]{2,1,0:T(8,128)(2,1)S(1)} async-done(((bf16[64,8,256]{2,1,0:T(8,128)(2,1)}), bf16[64,8,256]{2,1,0:T(8,128)(2,1)S(1)}, u32[]{:S(2)}, u32[]{:S(2)}) %all-to-all-start.6) | async-done | bytes 262176 | tf_op jit(solution)/shard_map/all_to_all | solution.py:356
  110.9 1.5 layer.15
  112.4 6.5 %all-to-all-start.7 = ((bf16[64,8,256]{2,1,0:T(8,128)(2,1)}), bf16[64,8,256]{2,1,0:T(8,128)(2,1)S(1)}, u32[]{:S(2)}, u32[]{:S(2)}) async-start(bf16[64,8,256]{2,1,0:T(8,128)(2,1)} %bitcast.19), calls=%async_computation.7 | async-start | bytes 524288 | tf_op jit(solution)/shard_map/all_to_all | solution.py:356
  118.9 4.8 %collective-permute-start.6 = (bf16[144,256]{1,0:T(8,128)(2,1)S(1)}, bf16[144,256]{1,0:T(8,128)(2,1)S(1)}, u32[]{:S(2)}, u32[]{:S(2)}) collective-permute-start(bf16[144,256]{1,0:T(8,128)(2,1)S(1)} %get-tuple-element.117), channel_id=1, source_target_pairs={{0,448},{64,0},{128,64},{192,128},{256,192},{320,256},{384,320},{4... | collective-permute-start | bytes 221192 | tf_op jit(solution)/shard_map/ppermute | solution.py:365
  123.7 2.2 %all_gather.26.late_ref.early_ref = bf16[288,256]{1,0:T(8,128)(2,1)S(1)} all-gather(bf16[144,256]{1,0:T(8,128)(2,1)S(1)} %get-tuple-element.117), channel_id=1, replica_groups={{0,1},{2,3},{4,5},{6,7},{8,9},{10,11},{12,13},{14,15},{16,17},{18,19},{..., dimensions={0}, use_global_device_ids=true | all-gather | bytes 221184 | tf_op jit(solution)/shard_map/all_gather | solution.py:361
  125.9 0.0 collective-permute-done.6.refs_0_
  125.9 4.4 %all-to-all-done.7 = bf16[64,8,256]{2,1,0:T(8,128)(2,1)S(1)} async-done(((bf16[64,8,256]{2,1,0:T(8,128)(2,1)}), bf16[64,8,256]{2,1,0:T(8,128)(2,1)S(1)}, u32[]{:S(2)}, u32[]{:S(2)}) %all-to-all-start.7) | async-done | bytes 262176 | tf_op jit(solution)/shard_map/all_to_all | solution.py:356
  130.3 1.5 layer.16
  131.9 6.5 %all-to-all-start.8 = ((bf16[64,8,256]{2,1,0:T(8,128)(2,1)}), bf16[64,8,256]{2,1,0:T(8,128)(2,1)S(1)}, u32[]{:S(2)}, u32[]{:S(2)}) async-start(bf16[64,8,256]{2,1,0:T(8,128)(2,1)} %bitcast.21), calls=%async_computation.8 | async-start | bytes 524288 | tf_op jit(solution)/shard_map/all_to_all | solution.py:356
  138.4 1.9 %all_gather.27.late_ref = bf16[288,256]{1,0:T(8,128)(2,1)S(1)} all-gather(bf16[144,256]{1,0:T(8,128)(2,1)S(1)} %get-tuple-element.120), channel_id=1, replica_groups={{0,1},{2,3},{4,5},{6,7},{8,9},{10,11},{12,13},{14,15},{16,17},{18,19},{..., dimensions={0}, use_global_device_ids=true | all-gather | bytes 221184 | tf_op jit(solution)/shard_map/all_gather | solution.py:361
  140.3 9.5 %all-to-all-done.8 = bf16[64,8,256]{2,1,0:T(8,128)(2,1)S(1)} async-done(((bf16[64,8,256]{2,1,0:T(8,128)(2,1)}), bf16[64,8,256]{2,1,0:T(8,128)(2,1)S(1)}, u32[]{:S(2)}, u32[]{:S(2)}) %all-to-all-start.8) | async-done | bytes 262176 | tf_op jit(solution)/shard_map/all_to_all | solution.py:356
  149.8 0.8 layer.17
  150.6 1.3 collective-permute-start.7
  151.9 18.3 %conditional.2 = (bf16[256,256]{1,0:T(8,128)(2,1)S(1)}) conditional(s32[]{:T(128)} %convert_element_type.6, () %tuple.17, (bf16[512,256]{1,0:T(8,128)(2,1)S(1)}, s32[1]{0:T(128)}, bf16[256,256]{1,0:T(8,128)(2,1)S(1)}, bf16[256,256]{1,0:T(8,128)(2,1)S(1)}, bf16[256,512]{1,0:T(8,128)(2,1)S(1)}, /*index=5*/f32[256,128]{1,0:T(8,128)S(1)}, ...), branch_computations={%region_0.1_spmd, %region_1.2_spmd} | conditional | bytes 524296 | solution.py:385
  152.0 17.7 %all_to_all.43 = bf16[64,8,256]{2,1,0:T(8,128)(2,1)S(1)} all-to-all(bf16[64,8,256]{2,1,0:T(8,128)(2,1)S(1)} %bitcast.24), channel_id=1, replica_groups={{20,21,22,23,16,17,18,19,28,29,30,31,24,25,26,27,4,5,6,7,0,1,2,3,12,13,..., dimensions={0} | all-to-all | bytes 524288 | tf_op jit(solution)/shard_map/cond/branch_1_fun/all_to_all | solution.py:378
  169.7 0.5 layer.9
  170.2 0.0 collective-permute-done.7.above_ref
  170.3 1.3 collective-permute-start.8
  171.6 0.7 place_states.1.before_ref
  172.3 1.1 collective-permute-done.8.full_ref
  (4 shorter events, 0.1 us)
Async XLA Ops:
  0.0 28.4 %copy-start.3 = (s32[2,1,64,8]{2,3,1,0:T(8,128)S(1)}, s32[2,1,64,8]{2,3,1,0:T(8,128)}, u32[]{:S(2)}) copy-start(s32[2,1,64,8]{2,3,1,0:T(8,128)} %param.18) | copy-start | bytes 12292
  0.0 28.4 %copy-start.4 = (s32[2,1,64,8]{2,3,1,0:T(8,128)S(1)}, s32[2,1,64,8]{2,3,1,0:T(8,128)}, u32[]{:S(2)}) copy-start(s32[2,1,64,8]{2,3,1,0:T(8,128)} %param.19) | copy-start | bytes 12292
  2.4 26.0 %copy-start.1 = (bf16[2,256,256]{2,1,0:T(8,128)(2,1)S(1)}, bf16[2,256,256]{2,1,0:T(8,128)(2,1)}, u32[]{:S(2)}) copy-start(bf16[2,256,256]{2,1,0:T(8,128)(2,1)} %features_ref.3) | copy-start | bytes 786436
  2.4 26.0 %copy-start.2 = (bf16[512,256]{1,0:T(8,128)(2,1)S(1)}, bf16[512,256]{1,0:T(8,128)(2,1)}, u32[]{:S(2)}) copy-start(bf16[512,256]{1,0:T(8,128)(2,1)} %get-tuple-element.94.after_ref) | copy-start | bytes 786436
  2.4 31.2 %all-to-all-start.2 = ((bf16[64,8,256]{2,1,0:T(8,128)(2,1)}), bf16[64,8,256]{2,1,0:T(8,128)(2,1)S(1)}, u32[]{:S(2)}, u32[]{:S(2)}) async-start(bf16[64,8,256]{2,1,0:T(8,128)(2,1)} %bitcast.27), calls=%async_computation.2 | async-start | bytes 524288 | tf_op jit(solution)/shard_map/all_to_all | solution.py:356
  18.5 9.9 %copy-start.5 = (s32[2,2,4]{2,1,0:T(2,128)S(1)}, s32[2,2,4]{2,1,0:T(2,128)}, u32[]{:S(2)}) copy-start(s32[2,2,4]{2,1,0:T(2,128)} %col_ref.1) | copy-start | bytes 196
  18.5 12.6 %collective-permute-start = (bf16[144,256]{1,0:T(8,128)(2,1)}, bf16[144,256]{1,0:T(8,128)(2,1)S(1)}, u32[]{:S(2)}, u32[]{:S(2)}) collective-permute-start(bf16[144,256]{1,0:T(8,128)(2,1)} %get-tuple-element.101), channel_id=1, source_target_pairs={{0,448},{64,0},{128,64},{192,128},{256,192},{320,256},{384,320},{4... | collective-permute-start | bytes 221192 | tf_op jit(solution)/shard_map/ppermute | solution.py:360
  26.2 7.4 %collective-permute-start.1 = (bf16[144,256]{1,0:T(8,128)(2,1)}, bf16[144,256]{1,0:T(8,128)(2,1)S(1)}, u32[]{:S(2)}, u32[]{:S(2)}) collective-permute-start(bf16[144,256]{1,0:T(8,128)(2,1)} %get-tuple-element.101), channel_id=1, source_target_pairs={{0,384},{64,448},{128,0},{192,64},{256,128},{320,192},{384,256},{4... | collective-permute-start | bytes 221192 | tf_op jit(solution)/shard_map/ppermute | solution.py:365
  28.4 1.2 copy-start
  35.1 17.3 %all-to-all-start.3 = ((bf16[64,8,256]{2,1,0:T(8,128)(2,1)}), bf16[64,8,256]{2,1,0:T(8,128)(2,1)S(1)}, u32[]{:S(2)}, u32[]{:S(2)}) async-start(bf16[64,8,256]{2,1,0:T(8,128)(2,1)} %bitcast.11), calls=%async_computation.3 | async-start | bytes 524288 | tf_op jit(solution)/shard_map/all_to_all | solution.py:356
  41.0 7.0 %collective-permute-start.2 = (bf16[144,256]{1,0:T(8,128)(2,1)S(1)}, bf16[144,256]{1,0:T(8,128)(2,1)S(1)}, u32[]{:S(2)}, u32[]{:S(2)}) collective-permute-start(bf16[144,256]{1,0:T(8,128)(2,1)S(1)} %get-tuple-element.105), channel_id=1, source_target_pairs={{0,448},{64,0},{128,64},{192,128},{256,192},{320,256},{384,320},{4... | collective-permute-start | bytes 221192 | tf_op jit(solution)/shard_map/ppermute | solution.py:365
  54.0 18.0 %all-to-all-start.4 = ((bf16[64,8,256]{2,1,0:T(8,128)(2,1)}), bf16[64,8,256]{2,1,0:T(8,128)(2,1)S(1)}, u32[]{:S(2)}, u32[]{:S(2)}) async-start(bf16[64,8,256]{2,1,0:T(8,128)(2,1)} %bitcast.13), calls=%async_computation.4 | async-start | bytes 524288 | tf_op jit(solution)/shard_map/all_to_all | solution.py:356
  60.5 7.0 %collective-permute-start.3 = (bf16[144,256]{1,0:T(8,128)(2,1)S(1)}, bf16[144,256]{1,0:T(8,128)(2,1)S(1)}, u32[]{:S(2)}, u32[]{:S(2)}) collective-permute-start(bf16[144,256]{1,0:T(8,128)(2,1)S(1)} %get-tuple-element.108), channel_id=1, source_target_pairs={{0,448},{64,0},{128,64},{192,128},{256,192},{320,256},{384,320},{4... | collective-permute-start | bytes 221192 | tf_op jit(solution)/shard_map/ppermute | solution.py:365
  73.4 18.0 %all-to-all-start.5 = ((bf16[64,8,256]{2,1,0:T(8,128)(2,1)}), bf16[64,8,256]{2,1,0:T(8,128)(2,1)S(1)}, u32[]{:S(2)}, u32[]{:S(2)}) async-start(bf16[64,8,256]{2,1,0:T(8,128)(2,1)} %bitcast.15), calls=%async_computation.5 | async-start | bytes 524288 | tf_op jit(solution)/shard_map/all_to_all | solution.py:356
  80.0 7.0 %collective-permute-start.4 = (bf16[144,256]{1,0:T(8,128)(2,1)S(1)}, bf16[144,256]{1,0:T(8,128)(2,1)S(1)}, u32[]{:S(2)}, u32[]{:S(2)}) collective-permute-start(bf16[144,256]{1,0:T(8,128)(2,1)S(1)} %get-tuple-element.111), channel_id=1, source_target_pairs={{0,448},{64,0},{128,64},{192,128},{256,192},{320,256},{384,320},{4... | collective-permute-start | bytes 221192 | tf_op jit(solution)/shard_map/ppermute | solution.py:365
  92.9 18.0 %all-to-all-start.6 = ((bf16[64,8,256]{2,1,0:T(8,128)(2,1)}), bf16[64,8,256]{2,1,0:T(8,128)(2,1)S(1)}, u32[]{:S(2)}, u32[]{:S(2)}) async-start(bf16[64,8,256]{2,1,0:T(8,128)(2,1)} %bitcast.17), calls=%async_computation.6 | async-start | bytes 524288 | tf_op jit(solution)/shard_map/all_to_all | solution.py:356
  99.5 7.0 %collective-permute-start.5 = (bf16[144,256]{1,0:T(8,128)(2,1)S(1)}, bf16[144,256]{1,0:T(8,128)(2,1)S(1)}, u32[]{:S(2)}, u32[]{:S(2)}) collective-permute-start(bf16[144,256]{1,0:T(8,128)(2,1)S(1)} %get-tuple-element.114), channel_id=1, source_target_pairs={{0,448},{64,0},{128,64},{192,128},{256,192},{320,256},{384,320},{4... | collective-permute-start | bytes 221192 | tf_op jit(solution)/shard_map/ppermute | solution.py:365
  112.4 18.0 %all-to-all-start.7 = ((bf16[64,8,256]{2,1,0:T(8,128)(2,1)}), bf16[64,8,256]{2,1,0:T(8,128)(2,1)S(1)}, u32[]{:S(2)}, u32[]{:S(2)}) async-start(bf16[64,8,256]{2,1,0:T(8,128)(2,1)} %bitcast.19), calls=%async_computation.7 | async-start | bytes 524288 | tf_op jit(solution)/shard_map/all_to_all | solution.py:356
  118.9 7.0 %collective-permute-start.6 = (bf16[144,256]{1,0:T(8,128)(2,1)S(1)}, bf16[144,256]{1,0:T(8,128)(2,1)S(1)}, u32[]{:S(2)}, u32[]{:S(2)}) collective-permute-start(bf16[144,256]{1,0:T(8,128)(2,1)S(1)} %get-tuple-element.117), channel_id=1, source_target_pairs={{0,448},{64,0},{128,64},{192,128},{256,192},{320,256},{384,320},{4... | collective-permute-start | bytes 221192 | tf_op jit(solution)/shard_map/ppermute | solution.py:365
  131.9 18.0 %all-to-all-start.8 = ((bf16[64,8,256]{2,1,0:T(8,128)(2,1)}), bf16[64,8,256]{2,1,0:T(8,128)(2,1)S(1)}, u32[]{:S(2)}, u32[]{:S(2)}) async-start(bf16[64,8,256]{2,1,0:T(8,128)(2,1)} %bitcast.21), calls=%async_computation.8 | async-start | bytes 524288 | tf_op jit(solution)/shard_map/all_to_all | solution.py:356
  150.6 19.6 %collective-permute-start.7 = (bf16[256,256]{1,0:T(8,128)(2,1)S(1)}, bf16[256,256]{1,0:T(8,128)(2,1)S(1)}, u32[]{:S(2)}, u32[]{:S(2)}) collective-permute-start(bf16[256,256]{1,0:T(8,128)(2,1)S(1)} %get-tuple-element.122), channel_id=1, source_target_pairs={{64,0},{128,64},{192,128},{256,192},{320,256},{384,320},{448,384},... | collective-permute-start | bytes 393224 | tf_op jit(solution)/shard_map/ppermute | solution.py:375
  170.3 3.2 %collective-permute-start.8 = (bf16[256,256]{1,0:T(8,128)(2,1)S(1)}, bf16[256,256]{1,0:T(8,128)(2,1)S(1)}, u32[]{:S(2)}, u32[]{:S(2)}) collective-permute-start(bf16[256,256]{1,0:T(8,128)(2,1)S(1)} %broadcast_select_fusion), channel_id=1, source_target_pairs={{0,448},{1,449},{2,450},{3,451},{4,452},{5,453},{6,454},{7,455},{8... | collective-permute-start | bytes 393224 | tf_op jit(solution)/shard_map/ppermute | solution.py:386
